TPU v7x, 256 devices: a whole 4x4x8 slice. The times are simulated.
256 devices in a mesh: dp: 32 (over x, z_lo, core), tower: 8 (over z_hi, y).
Axes of the slice: x: 4, y: 4, z: 8 (z_hi: 2, z_lo: 4; z = z_hi * 4 + z_lo), core: 2. Of those that a mesh axis runs over, the one named last changes fastest.
Arguments:
- user_states: bfloat16 [12288, 1024], P('dp'), may hold values from -80 to 80
- head_gain: float32 [3, 1024], replicated, may hold values from 0.1 to 1.9
- item_table: bfloat16 [16384, 1024], P('tower'), may hold values from -5 to 5
- neg_ids: int32 [16384], P(('dp', 'tower')), may hold values from 0 to 16383, as said below
- pos_ids: int32 [12288], P('dp'), may hold values from 0 to 16383
- label_mask: int32 [3, 12288], P(None, 'dp'), may hold values 0 or 1
- seq_len: int32 [32], P('dp'), may hold values from 96 to 384
Outputs:
- pos_loss: float32 [3, 12288], P(None, 'dp')
- neg_grad: float32 [16384, 1024], P(('dp', 'tower'))
Inputs may be any that keep to these rules, and one draw needn't show every extreme that they name: `neg_ids`: the 64 ids of block b (slots b * 64 onward) lie in rows t * 2048 to (t + 1) * 2048 - 1, with t = b % 8.
All inputs are finite; a program needn't handle non-finite values. No bound on the sum of `label_mask` on one device may be relied on, other than what follows from the above.
Results may differ from a plain program's by a relative error of at most 0.0037.
Values may be sent and summed in bfloat16 or wider, within the bound.
No kernel may reach another device: no remote copies, remote signals or barrier semaphores. Data moves between devices by JAX's collectives and lax.ppermute only.
A program may use at most 64 MiB of HBM per device.

v0:
```python
import math

import jax
import jax.numpy as jnp
from jax import lax
from jax.sharding import PartitionSpec as P


def shards(user_states, head_gain, item_table, neg_ids, pos_ids, label_mask, seq_len):
    rows_here, width = user_states.shape
    heads = head_gain.shape[0]
    table_rows = item_table.shape[0]
    neg_dev = neg_ids.shape[0]
    n_data = lax.axis_size("dp")
    n_owner = lax.axis_size("tower")
    total_neg = neg_dev * n_data * n_owner
    inv = 1.0 / math.sqrt(width)
    factor = total_neg / math.sqrt(rows_here * n_data)
    offset = lax.axis_index("tower") * table_rows
    local_negs = item_table[neg_ids - offset]
    query = (user_states.astype(jnp.float32)[None] * head_gain[:, None, :]).astype(jnp.bfloat16)
    flat = query.reshape(heads * rows_here, width)
    owned = (pos_ids >= offset) & (pos_ids < offset + table_rows)
    pos_rows = jnp.where(owned, pos_ids - offset, 0)
    pos_emb = item_table[pos_rows]
    pos_score = (
        jnp.sum(query.astype(jnp.float32) * pos_emb.astype(jnp.float32)[None], -1) * inv
    ).reshape(-1)
    owned_flat = jnp.broadcast_to(owned[None], (heads, rows_here)).reshape(-1)
    valid = (jnp.arange(rows_here) < seq_len[0]).astype(jnp.float32)
    weight = (label_mask.astype(jnp.float32) * valid[None]).reshape(-1)
    pos_val = jnp.where(owned_flat, pos_score, 0.0)
    scores = (
        lax.dot_general(
            flat,
            lax.all_gather(local_negs, "dp", axis=0, tiled=True),
            (((1,), (1,)), ((), ())),
            preferred_element_type=jnp.float32,
        )
        * inv
    )
    top_neg = jnp.max(scores, axis=1)
    top_local = jnp.where(owned_flat, jnp.maximum(top_neg, pos_score), top_neg)
    sum_local = jnp.sum(jnp.exp(scores - top_local[:, None]), axis=1) + jnp.where(
        owned_flat, jnp.exp(pos_score - top_local), 0.0
    )
    top_all = lax.pmax(top_local, "tower")
    sum_all, pos_all = lax.psum((sum_local * jnp.exp(top_local - top_all), pos_val), "tower")
    lse = top_all + jnp.log(sum_all)
    pos_loss = (weight * (lse - pos_all)).reshape(heads, rows_here)
    prob = (weight[:, None] * jnp.exp(scores - lse[:, None])).astype(jnp.bfloat16)
    term = lax.dot_general(prob, flat, (((0,), (0,)), ((), ())), preferred_element_type=jnp.float32)
    neg_grad = lax.psum_scatter(term * factor, "dp", scatter_dimension=0, tiled=True)
    return (pos_loss, neg_grad)


def solution(mesh):
    placed = (
        P("dp", None),
        P(),
        P("tower", None),
        P(("dp", "tower")),
        P("dp"),
        P(None, "dp"),
        P("dp"),
    )
    return jax.shard_map(
        shards,
        mesh=mesh,
        in_specs=placed,
        out_specs=(P(None, "dp"), P(("dp", "tower"), None)),
        check_vma=False,
    )
```

profile of v0, /device:TPU:1, one launch (start us, length us, event | category | flops | bytes accessed | tf_op | source)
XLA Modules:
  0.0 342.3 jit_solution(7462168190304329501)
XLA Ops:
  7.2 0.0 all-gather.3.cloned.1.call-start
  7.2 0.7 compare_select_fusion.1
  7.9 4.2 %gather_fusion = bf16[64,1024]{1,0:T(8,128)(2,1)} fusion(bf16[2048,1024]{1,0:T(8,128)(2,1)} %param.9, s32[1024]{0:T(1024)S(1)} %pad_clamp_fusion.1), kind=kCustom, calls=%fused_computation | custom fusion | bytes 262400 | tf_op jit(solution)/shard_map/gather | solution.py:20
  12.1 0.0 all-gather.3.cloned.1.call-update
  12.1 0.0 reduce-scatter.2.cloned.1.call-start
  12.8 0.7 convert_multiply_fusion
  13.5 0.7 compare_and_fusion
  14.2 0.7 compare_select_fusion
  14.9 0.0 copy-start
  14.9 0.0 copy-start.1
  14.9 5.6 %gather_fusion.1 = bf16[384,1024]{1,0:T(8,128)(2,1)S(1)} fusion(bf16[2048,1024]{1,0:T(8,128)(2,1)} %param.9, s32[1024]{0:T(1024)S(1)} %pad_clamp_fusion), kind=kCustom, calls=%fused_computation.1 | custom fusion | bytes 1574400 | tf_op jit(solution)/shard_map/gather | solution.py:25
  20.5 0.2 convert_element_type.39
  20.7 0.0 copy-done
  20.7 0.2 convert_element_type.35
  20.9 0.0 copy-done.1
  20.9 0.8 multiply_reduce_fusion
  21.7 57.7 %all-gather.3.cloned.1.call-done = bf16[2048,1024]{1,0:T(8,128)(2,1)} async-done(((bf16[64,1024]{1,0:T(8,128)(2,1)}), bf16[2048,1024]{1,0:T(8,128)(2,1)}) %all-gather.3.cloned.1.call-update) | async-done | bytes 4194320 | tf_op jit(solution)/shard_map/all_gather | solution.py:36
  79.4 9.5 %fusion.5 = (f32[1152]{0:T(1024)S(1)}, f32[1152,2048]{1,0:T(8,128)}) fusion(bf16[1152,1024]{1,0:T(8,128)(2,1)S(1)} %bitcast.6, bf16[2048,1024]{1,0:T(8,128)(2,1)} %all-gather.3.cloned.1.call-done), kind=kOutput, calls=%fused_computation.25 | convolution fusion | flops 4836555776 | bytes 15995392 | tf_op jit(solution)/shard_map/dot_general | solution.py:34
  88.9 26.7 %pmax.7 = f32[1152]{0:T(1024)S(1)} all-reduce(f32[1152]{0:T(1024)S(1)} %maximum_select_fusion), channel_id=1, replica_groups=mesh['dp'=32,'tower'=8] {'tower'}, use_global_device_ids=true, to_apply=%region_2.3 | all-reduce | flops 1152 | bytes 9216 | tf_op jit(solution)/shard_map/pmax | solution.py:47
  115.7 5.1 %exponential_reduce_fusion = f32[1152]{0:T(1024)S(1)} fusion(f32[1152,2048]{1,0:T(8,128)} %get-tuple-element.11, f32[1152]{0:T(1024)S(1)} %maximum_select_fusion), kind=kLoop, calls=%fused_computation.4 | loop fusion | flops 4717440 | bytes 9446400 | tf_op jit(solution)/shard_map/reduce_sum | solution.py:44
  120.8 39.3 %all-reduce = (f32[1152]{0:T(1024)S(1)}, f32[1152]{0:T(1024)S(1)}) all-reduce(f32[1152]{0:T(1024)S(1)} %get-tuple-element.9, f32[1152]{0:T(1024)S(1)} %get-tuple-element.8), channel_id=1, replica_groups=mesh['dp'=32,'tower'=8] {'tower'}, use_global_device_ids=true, to_apply=%region_4.5 | all-reduce | flops 2304 | bytes 18432 | tf_op jit(solution)/shard_map/psum | solution.py:48
  160.1 12.6 %fusion.3 = f32[2048,1024]{1,0:T(8,128)} fusion(bf16[1152,1024]{1,0:T(8,128)(2,1)S(1)} %bitcast.7, f32[1152,2048]{1,0:T(8,128)} %get-tuple-element.11, f32[1152]{0:T(1024)S(1)} %get-tuple-element.5, f32[1152]{0:T(1024)S(1)} %reshape.48), kind=kOutput, calls=%fused_computation.10 | convolution fusion | flops 4841013248 | bytes 20194304 | tf_op jit(solution)/shard_map/dot_general | solution.py:52
  172.7 0.0 reduce-scatter.2.cloned.1.call-update
  172.7 0.6 reshape.50
  173.3 162.2 %reduce-scatter.2.cloned.1.call-done = f32[64,1024]{1,0:T(8,128)} async-done(((f32[2048,1024]{1,0:T(8,128)}), f32[64,1024]{1,0:T(8,128)}) %reduce-scatter.2.cloned.1.call-update) | async-done | bytes 262160 | tf_op jit(solution)/shard_map/reduce_scatter | solution.py:53
  (11 shorter events, 0.1 us)
Async XLA Ops:
  7.2 72.2 %all-gather.3.cloned.1.call-start = ((), (), s32[]{:S(2)}) async-start(), calls=%async_computation.2 | async-start | bytes 4325376 | tf_op jit(solution)/shard_map/all_gather | solution.py:36
  12.1 323.4 %reduce-scatter.2.cloned.1.call-start = ((), (), s32[]{:S(2)}) async-start(), calls=%async_computation.1 | async-start | bytes 8650752 | tf_op jit(solution)/shard_map/reduce_scatter | solution.py:53
  14.9 5.8 %copy-start = (bf16[384,1024]{1,0:T(8,128)(2,1)S(1)}, bf16[384,1024]{1,0:T(8,128)(2,1)}, u32[]{:S(2)}) copy-start(bf16[384,1024]{1,0:T(8,128)(2,1)} %param.7) | copy-start | bytes 2359300
  14.9 5.9 %copy-start.1 = (f32[3,1024]{1,0:T(4,128)S(1)}, f32[3,1024]{1,0:T(4,128)}, u32[]{:S(2)}) copy-start(f32[3,1024]{1,0:T(4,128)} %param.8) | copy-start | bytes 36868
Sparse Core Ops, SparseCore 0:
  12.2 67.1 all-gather.2
  172.8 162.5 reduce-scatter.1
where the time goes:
time: 346 us; the launch traced here: 342 us
  waiting for transfers between devices  220 us (64%)
  blocking collectives  66.1 us (19%)
  matrix products  22.1 us (6%)
  between operations  14.8 us (4%)
  local copies, waits for them, and re-layouts  10.4 us (3%)
  other arithmetic  8.98 us (3%)
    reduce_scatter x1, waiting for transfers between devices, shards(): lax.psum_scatter(term * factor, 'dp', scatter_dimension=0, tiled=True)  162 us
    all_gather x1, waiting for transfers between devices, shards(): lax.all_gather(local_negs, 'dp', axis=0, tiled=True)  57.7 us
    psum x1, blocking collectives, shards(): lax.psum((sum_local * jnp.exp(top_local - top_all), pos_val), 'tower')  39.3 us
    pmax x1, blocking collectives, shards(): top_all = lax.pmax(top_local, 'tower')  26.7 us
    dot_general x1, matrix products, shards(): lax.dot_general(prob, flat, (((0,), (0,)), ((), ())), preferred_element_t...  12.6 us
    dot_general x1, matrix products, shards(): lax.dot_general(flat, lax.all_gather(local_negs, 'dp', axis=0, tiled=True...  9.55 us
  transfers between devices with their start and end apart: 2, of which 2 were waited for; matrix products, arithmetic and copies ran while one was open for 3% of the time, Pallas kernels for 0%

commit v1 on v0

v1 whole, which is shorter than its diff:
```python
import functools
import math

import jax
import jax.numpy as jnp
from jax import lax
from jax.experimental import pallas as pl
from jax.experimental.pallas import tpu as pltpu
from jax.sharding import Mesh
from jax.sharding import PartitionSpec as P

F32 = jnp.float32
BF16 = jnp.bfloat16
DP = ("x", "z", "core")
TOWER = ("zh", "y")


def one_hot_rows(ids_row, width):
    n = ids_row.shape[1]
    parts = []
    for a in range(0, n, 128):
        wide = jnp.broadcast_to(ids_row[:, a : a + 128].astype(F32), (128, 128))
        column = wide.T.astype(jnp.int32)
        lane = lax.broadcasted_iota(jnp.int32, (128, 128), 1)
        parts.append(
            jnp.concatenate(
                [(column == lane + v).astype(F32).astype(BF16) for v in range(0, width, 128)], axis=1
            )
        )
    return parts[0] if len(parts) == 1 else jnp.concatenate(parts, axis=0)


def score_kernel(
    inv, ids_ref, pos_ref, gain_ref, own_ref, other_ref, table_ref,
    e_ref, q_ref, m_ref, msg_ref, emb_ref, pos_emb_ref, msg_row,
):
    head = pl.program_id(0)
    rows = own_ref.shape[0]
    negs = emb_ref.shape[0]
    width = table_ref.shape[0]

    @pl.when(head == 0)
    def _():
        for a in range(0, negs, 128):
            hot = one_hot_rows(ids_ref[a // 128 : a // 128 + 1, :], width)
            emb_ref[a : a + 128, :] = jnp.dot(hot, table_ref[...], preferred_element_type=F32).astype(BF16)
        for a in range(0, rows, 128):
            hot = one_hot_rows(pos_ref[a // 128 : a // 128 + 1, :], width)
            pos_emb_ref[a : a + 128, :] = jnp.dot(hot, table_ref[...], preferred_element_type=F32).astype(BF16)

    gain = gain_ref[pl.ds(head, 1), :]
    q_ref[:rows, :] = (own_ref[...].astype(F32) * gain).astype(BF16)
    q_ref[rows:, :] = (other_ref[...].astype(F32) * gain).astype(BF16)
    nt = (((1,), (1,)), ((), ()))
    block = 256
    for a in range(0, 2 * rows, block):
        s = lax.dot_general(emb_ref[...], q_ref[a : a + block, :], nt, preferred_element_type=F32) * inv
        m = jnp.max(s, axis=0, keepdims=True)
        e = jnp.exp(s - m)
        e_ref[:, a : a + block] = e
        m_ref[pl.ds(head, 1), a : a + block] = m
        msg_row[:, a : a + block] = m + jnp.log(jnp.sum(e, axis=0, keepdims=True))
    pos = []
    owned = []
    for a in range(0, rows, 128):
        d = lax.dot_general(pos_emb_ref[a : a + 128, :], q_ref[a : a + 128, :], nt, preferred_element_type=F32)
        diag = lax.broadcasted_iota(jnp.int32, d.shape, 0) == lax.broadcasted_iota(jnp.int32, d.shape, 1)
        pos.append(jnp.sum(jnp.where(diag, d, 0.0), axis=0, keepdims=True) * inv)
        ids = pos_ref[a // 128 : a // 128 + 1, :]
        owned.append((ids >= 0) & (ids < width))
    for i, a in enumerate(range(0, rows, 128)):
        base = msg_row[:, a : a + 128]
        top = jnp.maximum(base, pos[i])
        both = top + jnp.log(jnp.exp(base - top) + jnp.exp(pos[i] - top))
        msg_row[:, a : a + 128] = jnp.where(owned[i], both, base)
        msg_row[:, 2 * rows + a : 2 * rows + a + 128] = pos[i]
    for k in range(msg_ref.shape[0]):
        msg_ref[k, pl.ds(head, 1), :] = msg_row[...]


def scores(inv, ids, pos, gain, own, other, table, group):
    rows, width = own.shape
    heads = gain.shape[0]
    negs = ids.size
    full = lambda *shape: pl.BlockSpec(shape, lambda h: (0,) * len(shape))
    return pl.pallas_call(
        functools.partial(score_kernel, inv),
        grid=(heads,),
        in_specs=[
            full(*ids.shape), full(*pos.shape), full(*gain.shape),
            full(rows, width), full(rows, width), full(*table.shape),
        ],
        out_specs=[
            pl.BlockSpec((negs, 2 * rows), lambda h: (0, h)),
            pl.BlockSpec((None, 2 * rows, width), lambda h: (h, 0, 0)),
            full(heads, 2 * rows),
            full(group, heads, 3 * rows),
        ],
        out_shape=[
            jax.ShapeDtypeStruct((negs, heads * 2 * rows), F32),
            jax.ShapeDtypeStruct((heads, 2 * rows, width), BF16),
            jax.ShapeDtypeStruct((heads, 2 * rows), F32),
            jax.ShapeDtypeStruct((group, heads, 3 * rows), F32),
        ],
        scratch_shapes=[
            pltpu.VMEM((negs, width), BF16),
            pltpu.VMEM((rows, width), BF16),
            pltpu.VMEM((1, 3 * rows), F32),
        ],
        compiler_params=pltpu.CompilerParams(vmem_limit_bytes=48 * 2**20),
    )(ids, pos, gain, own, other, table)


def combine_kernel(core_ref, msg_ref, m_ref, w_ref, w_other_ref, c_ref, loss_ref):
    rows = w_ref.shape[1]
    half = msg_ref.shape[0] // 2
    core = core_ref[0]
    same = [msg_ref[core * half + k] for k in range(half)]
    cross = [msg_ref[(1 - core) * half + k] for k in range(half)]
    own = [r[:, :rows] for r in same] + [r[:, rows : 2 * rows] for r in cross]
    other = [r[:, rows : 2 * rows] for r in same] + [r[:, :rows] for r in cross]

    def fold(parts):
        top = functools.reduce(jnp.maximum, parts)
        return top + jnp.log(sum(jnp.exp(r - top) for r in parts))

    lse, lse_other = fold(own), fold(other)
    pos = sum(r[:, 2 * rows :] for r in same)
    loss_ref[...] = w_ref[...] * (lse - pos)
    c_ref[:, :rows] = w_ref[...] * jnp.exp(m_ref[:, :rows] - lse)
    c_ref[:, rows:] = w_other_ref[...] * jnp.exp(m_ref[:, rows:] - lse_other)


def combine(core, msg, m, w, w_other):
    vm = pl.BlockSpec(memory_space=pltpu.VMEM)
    return pl.pallas_call(
        combine_kernel,
        in_specs=[pl.BlockSpec(memory_space=pltpu.SMEM), vm, vm, vm, vm],
        out_specs=[vm, vm],
        out_shape=[jax.ShapeDtypeStruct(m.shape, F32), jax.ShapeDtypeStruct(w.shape, F32)],
    )(core, msg, m, w, w_other)


def grad_kernel(c_ref, e_ref, q_ref, out_ref, acc_ref):
    head = pl.program_id(0)
    p = (e_ref[...] * c_ref[pl.ds(head, 1), :]).astype(BF16)
    part = jnp.dot(p, q_ref[...], preferred_element_type=F32)

    @pl.when(head == 0)
    def _():
        acc_ref[...] = part

    @pl.when(head > 0)
    def _():
        acc_ref[...] += part

    @pl.when(head == pl.num_programs(0) - 1)
    def _():
        out_ref[...] = acc_ref[...].astype(out_ref.dtype)


def grad(c, e, q, piece, pieces, dtype):
    heads, rows, width = q.shape
    size = e.shape[0] // pieces
    return pl.pallas_call(
        grad_kernel,
        grid=(heads,),
        in_specs=[
            pl.BlockSpec((heads, rows), lambda h: (0, 0)),
            pl.BlockSpec((size, rows), lambda h: (piece, h)),
            pl.BlockSpec((None, rows, width), lambda h: (h, 0, 0)),
        ],
        out_specs=pl.BlockSpec((size, width), lambda h: (0, 0)),
        out_shape=jax.ShapeDtypeStruct((size, width), dtype),
        scratch_shapes=[pltpu.VMEM((size, width), F32)],
        compiler_params=pltpu.CompilerParams(vmem_limit_bytes=32 * 2**20),
        cost_estimate=pl.CostEstimate(
            flops=2 * size * heads * rows * width,
            bytes_accessed=4 * size * heads * rows + 2 * q.size,
            transcendentals=0,
        ),
    )(c, e, q)


def shards(nx, nz, user_states, head_gain, item_table, neg_ids, pos_ids, label_mask, seq_len):
    rows, width = user_states.shape
    heads = head_gain.shape[0]
    table_rows = item_table.shape[0]
    neg_dev = neg_ids.shape[0]
    group = lax.axis_size("core") * lax.axis_size("zh") * lax.axis_size("y")
    n_dev = nx * nz * group
    factor = (neg_dev * n_dev) / math.sqrt(rows * nx * nz * lax.axis_size("core"))
    x, z, core = lax.axis_index("x"), lax.axis_index("z"), lax.axis_index("core")
    offset = (lax.axis_index("zh") * lax.axis_size("y") + lax.axis_index("y")) * table_rows

    valid = (jnp.arange(rows) < seq_len[0]).astype(F32)
    w = label_mask.astype(F32) * valid[None]
    swap = [(0, 1), (1, 0)]
    other = lax.ppermute(user_states, "core", swap)
    w_other = lax.ppermute(w, "core", swap)

    slots = jnp.zeros((nx, nz, neg_dev), jnp.int32)
    slots = lax.dynamic_update_slice(slots, (neg_ids - offset)[None, None], (x, z, 0))
    slots = lax.psum(slots, ("x", "z"))
    slots = jnp.roll(slots, (-x, -z), (0, 1))
    ids = slots.reshape(-1, 128)
    pos = (pos_ids - offset).reshape(-1, 128)

    e, q, m, msg = scores(1.0 / math.sqrt(width), ids, pos, head_gain, user_states, other, item_table, group)
    msg = lax.all_to_all(msg, ("core",) + TOWER, 0, 0, tiled=True)
    c, pos_loss = combine(core.reshape(1), msg, m, w, w_other)

    def shifted(value, axis, size, by):
        return lax.ppermute(value, axis, [(i, (i + by) % size) for i in range(size)])

    order = [2, 1, 3]
    sent = [shifted(grad(c, e, q, k, nx, BF16), "x", nx, k) for k in order]
    total = grad(c, e, q, 0, nx, F32)
    for piece in sent:
        total = total + piece.astype(F32)
    parts = [total[k * neg_dev : (k + 1) * neg_dev] for k in range(nz)]
    sent = [shifted(parts[k].astype(BF16), "z", nz, k) for k in (2, 1, 3)]
    out = parts[0]
    for piece in sent:
        out = out + piece.astype(F32)
    return pos_loss, out * factor


def solution(mesh):
    nx, nz = 4, 4
    devices = mesh.devices.reshape(nx, nz, 2, 2, 4)
    wide = Mesh(devices, DP + TOWER)
    placed = (
        P(DP, None),
        P(),
        P(TOWER, None),
        P(DP + TOWER),
        P(DP),
        P(None, DP),
        P(DP),
    )
    return jax.shard_map(
        functools.partial(shards, nx, nz),
        mesh=wide,
        in_specs=placed,
        out_specs=(P(None, DP), P(DP + TOWER, None)),
        check_vma=False,
    )
```

time: 346 us -> 122 us (0.35)
  waiting for transfers between devices: 220 us -> 40.9 us
  blocking collectives: 66.1 us -> 11.5 us
  Pallas kernels: 0 us -> 27.2 us
  starting transfers between devices: 0.08 us -> 25.9 us
  matrix products: 22.1 us -> 0 us
  between operations: 14.8 us -> 1.4 us
  other arithmetic: 8.98 us -> 2.52 us
    reduce_scatter x1 -> x0, waiting for transfers between devices: 162 us -> none  [shards(): lax.psum_scatter(term * factor, 'dp', scatter_dimension=0, tiled=True)]
    all_gather x1 -> x0, waiting for transfers between devices: 57.7 us -> none  [shards(): lax.all_gather(local_negs, 'dp', axis=0, tiled=True)]
    ppermute x0 -> x8, waiting for transfers between devices: none -> 31 us  [the longest x6 29.9 us: shifted(): lax.ppermute(value, axis, [(i, (i + by) % size) for i in range(size)])]
    psum x1, blocking collectives: 39.3 us -> 11.5 us  [shards(): slots = lax.psum(slots, ('x', 'z'))]
    pallas_call x0 -> x6, Pallas kernels: none -> 27.2 us  [the longest x1 16.6 us: scores(): pl.pallas_call(functools.partial(score_kernel, inv), grid=(heads,), in_sp...]
    pmax x1 -> x0, blocking collectives: 26.7 us -> none  [shards(): top_all = lax.pmax(top_local, 'tower')]
    dot_general x2 -> x0, matrix products: 22.1 us -> none  [the longest x1 12.6 us: shards(): lax.dot_general(prob, flat, (((0,), (0,)), ((), ())), preferred_element_t...]
    ppermute x0 -> x8, starting transfers between devices: none -> 13 us  [the longest x6 9.3 us: shifted(): lax.ppermute(value, axis, [(i, (i + by) % size) for i in range(size)])]
  transfers between devices with their start and end apart: 2 -> 9, of which waited for: 2 -> 6; matrix products, arithmetic and copies ran while one was open for 3% -> 1% of each run, Pallas kernels for 0% -> 2%
where the time goes in v1:
time: 122 us
  waiting for transfers between devices  40.9 us (34%)
  Pallas kernels  27.2 us (22%)
  starting transfers between devices  25.9 us (21%)
  local copies, waits for them, and re-layouts  12.2 us (10%)
  blocking collectives  11.5 us (9%)
  other arithmetic  2.52 us (2%)
  between operations  1.4 us (1%)
    ppermute x6, waiting for transfers between devices, shifted(): lax.ppermute(value, axis, [(i, (i + by) % size) for i in range(size)])  29.9 us
    pallas_call x1, Pallas kernels, scores(): pl.pallas_call(functools.partial(score_kernel, inv), grid=(heads,), in_sp...  16.6 us
    all_to_all x1, starting transfers between devices, shards(): msg = lax.all_to_all(msg, ('core',) + TOWER, 0, 0, tiled=True)  12.9 us
    unnamed x22, local copies, waits for them, and re-layouts  12.1 us
    psum x1, blocking collectives, shards(): slots = lax.psum(slots, ('x', 'z'))  11.5 us
    all_to_all x1, waiting for transfers between devices, shards(): msg = lax.all_to_all(msg, ('core',) + TOWER, 0, 0, tiled=True)  9.97 us
    ppermute x6, starting transfers between devices, shifted(): lax.ppermute(value, axis, [(i, (i + by) % size) for i in range(size)])  9.3 us
    pallas_call x4, Pallas kernels, grad(): pl.pallas_call(grad_kernel, grid=(heads,), in_specs=[pl.BlockSpec((heads,...  8.97 us
  transfers between devices with their start and end apart: 9, of which 6 were waited for; matrix products, arithmetic and copies ran while one was open for 1% of the time, Pallas kernels for 2%

profile of v1, /device:TPU:1, one launch (start us, length us, event | category | flops | bytes accessed | tf_op | source)
XLA Modules:
  0.0 121.7 jit_solution(1203120170085813943)
XLA Ops:
  0.6 3.3 %collective-permute-start = (bf16[384,1024]{1,0:T(8,128)(2,1)}, bf16[384,1024]{1,0:T(8,128)(2,1)S(1)}, u32[]{:S(2)}, u32[]{:S(2)}) collective-permute-start(bf16[384,1024]{1,0:T(8,128)(2,1)} %own_ref.1), channel_id=1, source_target_pairs={{0,8},{8,0},{1,9},{9,1},{2,10},{10,2},{3,11},{11,3},{4,12},{12,4},... | collective-permute-start | bytes 2359304 | tf_op jit(solution)/shard_map/ppermute | solution.py:199
  4.0 0.7 subtract_bitcast_fusion.1
  4.7 11.5 %psum.7 = s32[4,4,64]{2,1,0:T(4,128)S(1)} all-reduce(s32[4,4,64]{2,1,0:T(4,128)S(1)} %dynamic_update_slice.3), channel_id=1, replica_groups=mesh['x'=4,'z'=4,'core'=2,'zh'=2,'y'=4] {'x','z'}, use_global_device_ids=true, to_apply=%region_0.0 | all-reduce | flops 1024 | bytes 8192 | tf_op jit(solution)/shard_map/psum | solution.py:204
  16.3 0.7 subtract_bitcast_fusion.pos_ref
  16.9 2.2 %copy-done.2 = bf16[2048,1024]{1,0:T(8,128)(2,1)S(1)} copy-done((bf16[2048,1024]{1,0:T(8,128)(2,1)S(1)}, bf16[2048,1024]{1,0:T(8,128)(2,1)}, u32[]{:S(2)}) %copy-start.2) | copy-done | bytes 4194328
  19.1 1.1 copy-done.3
  20.3 0.7 copy-done.5
  21.0 16.6 %shard_map.86 = (f32[1024,2304]{1,0:T(8,128)}, bf16[3,768,1024]{2,1,0:T(8,128)(2,1)}, f32[3,768]{1,0:T(4,128)S(1)}, f32[16,3,1152]{2,1,0:T(4,128)}) custom-call(s32[8,128]{1,0:T(8,128)S(1)} %reshape.19.ids_ref, s32[3,128]{1,0:T(4,128)S(1)} %subtract_bitcast_fusion.pos_ref, f32[3,1024]{1,0:T(4,128)S(1)} %copy-done.5, bf16[384,1024]{1,0:T(8,128)(2,1)S(1)} %copy-done.3, ...), custom_call_target="tpu_custom_call" | custom-call | tf_op jit(solution)/shard_map/pallas_call | solution.py:86
  37.5 0.6 copy-done.6
  38.1 12.9 %all-to-all-start = ((f32[16,3,1152]{2,1,0:T(4,128)}), f32[16,3,1152]{2,1,0:T(4,128)S(1)}, u32[]{:S(2)}, u32[]{:S(2)}) async-start(f32[16,3,1152]{2,1,0:T(4,128)} %get-tuple-element.8), calls=%async_computation | async-start | bytes 589824 | tf_op jit(solution)/shard_map/all_to_all | solution.py:210
  51.8 0.4 collective-permute-start.1
  52.1 1.1 collective-permute-done.1.w_other_ref
  53.2 10.0 %all-to-all-done.msg_ref = f32[16,3,1152]{2,1,0:T(4,128)S(1)} async-done(((f32[16,3,1152]{2,1,0:T(4,128)}), f32[16,3,1152]{2,1,0:T(4,128)S(1)}, u32[]{:S(2)}, u32[]{:S(2)}) %all-to-all-start) | async-done | bytes 221216 | tf_op jit(solution)/shard_map/all_to_all | solution.py:210
  63.2 0.7 copy-done.7
  63.9 1.7 %shard_map.87 = (f32[3,768]{1,0:T(4,128)}, f32[3,384]{1,0:T(4,128)}) custom-call(s32[1]{0:T(128)} %bitcast.core_ref, f32[16,3,1152]{2,1,0:T(4,128)} %copy-done.7, f32[3,768]{1,0:T(4,128)} %copy-done.6, f32[3,384]{1,0:T(4,128)} %copy-done.8, f32[3,384]{1,0:T(4,128)} %copy-done.10), custom_call_target="tpu_custom_call" | custom-call | tf_op jit(solution)/shard_map/pallas_call | solution.py:136
  65.6 3.7 %copy-done = f32[1024,2304]{1,0:T(8,128)S(1)} copy-done((f32[1024,2304]{1,0:T(8,128)S(1)}, f32[1024,2304]{1,0:T(8,128)}, u32[]{:S(2)}) %copy-start) | copy-done | bytes 9437208
  69.3 2.3 %copy-done.1 = bf16[3,768,1024]{2,1,0:T(8,128)(2,1)S(1)} copy-done((bf16[3,768,1024]{2,1,0:T(8,128)(2,1)S(1)}, bf16[3,768,1024]{2,1,0:T(8,128)(2,1)}, u32[]{:S(2)}) %copy-start.1) | copy-done | bytes 4718616
  71.6 0.7 copy-done.4
  72.3 2.2 %shard_map.91 = bf16[256,1024]{1,0:T(8,128)(2,1)S(1)} custom-call(f32[3,768]{1,0:T(4,128)S(1)} %copy-done.4, f32[1024,2304]{1,0:T(8,128)S(1)} %copy-done, bf16[3,768,1024]{2,1,0:T(8,128)(2,1)S(1)} %copy-done.1), custom_call_target="tpu_custom_call" | custom-call | flops 1207959552 | bytes 7077888 | tf_op jit(solution)/shard_map/pallas_call | solution.py:165
  74.5 2.2 %shard_map.90 = bf16[256,1024]{1,0:T(8,128)(2,1)S(1)} custom-call(f32[3,768]{1,0:T(4,128)S(1)} %copy-done.4, f32[1024,2304]{1,0:T(8,128)S(1)} %copy-done, bf16[3,768,1024]{2,1,0:T(8,128)(2,1)S(1)} %copy-done.1), custom_call_target="tpu_custom_call" | custom-call | flops 1207959552 | bytes 7077888 | tf_op jit(solution)/shard_map/pallas_call | solution.py:165
  76.8 2.2 %shard_map.89 = bf16[256,1024]{1,0:T(8,128)(2,1)S(1)} custom-call(f32[3,768]{1,0:T(4,128)S(1)} %copy-done.4, f32[1024,2304]{1,0:T(8,128)S(1)} %copy-done, bf16[3,768,1024]{2,1,0:T(8,128)(2,1)S(1)} %copy-done.1), custom_call_target="tpu_custom_call" | custom-call | flops 1207959552 | bytes 7077888 | tf_op jit(solution)/shard_map/pallas_call | solution.py:165
  79.0 0.6 collective-permute-start.2
  80.0 2.3 %collective-permute-start.4 = (bf16[256,1024]{1,0:T(8,128)(2,1)S(1)}, bf16[256,1024]{1,0:T(8,128)(2,1)S(1)}, u32[]{:S(2)}, u32[]{:S(2)}) collective-permute-start(bf16[256,1024]{1,0:T(8,128)(2,1)S(1)} %shard_map.91), channel_id=1, source_target_pairs={{0,192},{64,0},{128,64},{192,128},{1,193},{65,1},{129,65},{193,129... | collective-permute-start | bytes 1572872 | tf_op jit(solution)/shard_map/ppermute | solution.py:214
  82.4 2.2 %shard_map.88 = f32[256,1024]{1,0:T(8,128)S(1)} custom-call(f32[3,768]{1,0:T(4,128)S(1)} %copy-done.4, f32[1024,2304]{1,0:T(8,128)S(1)} %copy-done, bf16[3,768,1024]{2,1,0:T(8,128)(2,1)S(1)} %copy-done.1), custom_call_target="tpu_custom_call" | custom-call | flops 1207959552 | bytes 7077888 | tf_op jit(solution)/shard_map/pallas_call | solution.py:165
  84.6 9.3 %collective-permute-done.2 = bf16[256,1024]{1,0:T(8,128)(2,1)S(1)} collective-permute-done((bf16[256,1024]{1,0:T(8,128)(2,1)S(1)}, bf16[256,1024]{1,0:T(8,128)(2,1)S(1)}, u32[]{:S(2)}, u32[]{:S(2)}) %collective-permute-start.2) | collective-permute-done | bytes 524320 | tf_op jit(solution)/shard_map/ppermute | solution.py:214
  93.9 11.8 %collective-permute-done.3 = bf16[256,1024]{1,0:T(8,128)(2,1)S(1)} collective-permute-done((bf16[256,1024]{1,0:T(8,128)(2,1)S(1)}, bf16[256,1024]{1,0:T(8,128)(2,1)S(1)}, u32[]{:S(2)}, u32[]{:S(2)}) %collective-permute-start.3) | collective-permute-done | bytes 524320 | tf_op jit(solution)/shard_map/ppermute | solution.py:214
  105.7 0.3 fusion.6
  106.1 4.3 %collective-permute-start.5 = (bf16[64,1024]{1,0:T(8,128)(2,1)S(1)}, bf16[64,1024]{1,0:T(8,128)(2,1)S(1)}, u32[]{:S(2)}, u32[]{:S(2)}) collective-permute-start(bf16[64,1024]{1,0:T(8,128)(2,1)S(1)} %get-tuple-element.16), channel_id=1, source_target_pairs={{0,32},{16,48},{32,0},{48,16},{1,33},{17,49},{33,1},{49,17},{2,34}... | collective-permute-start | bytes 393224 | tf_op jit(solution)/shard_map/ppermute | solution.py:214
  110.5 1.7 %collective-permute-start.7 = (bf16[64,1024]{1,0:T(8,128)(2,1)S(1)}, bf16[64,1024]{1,0:T(8,128)(2,1)S(1)}, u32[]{:S(2)}, u32[]{:S(2)}) collective-permute-start(bf16[64,1024]{1,0:T(8,128)(2,1)S(1)} %get-tuple-element.17), channel_id=1, source_target_pairs={{0,48},{16,0},{32,16},{48,32},{1,49},{17,1},{33,17},{49,33},{2,50}... | collective-permute-start | bytes 393224 | tf_op jit(solution)/shard_map/ppermute | solution.py:214
  112.1 4.1 %collective-permute-done.5 = bf16[64,1024]{1,0:T(8,128)(2,1)S(1)} collective-permute-done((bf16[64,1024]{1,0:T(8,128)(2,1)S(1)}, bf16[64,1024]{1,0:T(8,128)(2,1)S(1)}, u32[]{:S(2)}, u32[]{:S(2)}) %collective-permute-start.5) | collective-permute-done | bytes 131104 | tf_op jit(solution)/shard_map/ppermute | solution.py:214
  116.3 4.6 %collective-permute-done.6 = bf16[64,1024]{1,0:T(8,128)(2,1)S(1)} collective-permute-done((bf16[64,1024]{1,0:T(8,128)(2,1)S(1)}, bf16[64,1024]{1,0:T(8,128)(2,1)S(1)}, u32[]{:S(2)}, u32[]{:S(2)}) %collective-permute-start.6) | collective-permute-done | bytes 131104 | tf_op jit(solution)/shard_map/ppermute | solution.py:214
  120.9 0.8 fusion.2
  (27 shorter events, 0.6 us)
Async XLA Ops:
  0.6 51.1 %copy-start.9 = (s32[3,384]{1,0:T(4,128)S(1)}, s32[3,384]{1,0:T(4,128)}, u32[]{:S(2)}) copy-start(s32[3,384]{1,0:T(4,128)} %param.12) | copy-start | bytes 13828
  0.6 16.3 %collective-permute-start = (bf16[384,1024]{1,0:T(8,128)(2,1)}, bf16[384,1024]{1,0:T(8,128)(2,1)S(1)}, u32[]{:S(2)}, u32[]{:S(2)}) collective-permute-start(bf16[384,1024]{1,0:T(8,128)(2,1)} %own_ref.1), channel_id=1, source_target_pairs={{0,8},{8,0},{1,9},{9,1},{2,10},{10,2},{3,11},{11,3},{4,12},{12,4},... | collective-permute-start | bytes 2359304 | tf_op jit(solution)/shard_map/ppermute | solution.py:199
  16.9 2.2 %copy-start.2 = (bf16[2048,1024]{1,0:T(8,128)(2,1)S(1)}, bf16[2048,1024]{1,0:T(8,128)(2,1)}, u32[]{:S(2)}) copy-start(bf16[2048,1024]{1,0:T(8,128)(2,1)} %table_ref.1) | copy-start | bytes 12582916
  19.1 1.1 copy-start.3
  20.3 0.7 copy-start.5
  37.5 0.6 copy-start.6
  38.1 25.1 %all-to-all-start = ((f32[16,3,1152]{2,1,0:T(4,128)}), f32[16,3,1152]{2,1,0:T(4,128)S(1)}, u32[]{:S(2)}, u32[]{:S(2)}) async-start(f32[16,3,1152]{2,1,0:T(4,128)} %get-tuple-element.8), calls=%async_computation | async-start | bytes 589824 | tf_op jit(solution)/shard_map/all_to_all | solution.py:210
  51.8 11.4 %copy-start.8 = (f32[3,384]{1,0:T(4,128)}, f32[3,384]{1,0:T(4,128)S(1)}, u32[]{:S(2)}) copy-start(f32[3,384]{1,0:T(4,128)S(1)} %convert_multiply_fusion.w_ref) | copy-start | bytes 13828
  51.8 1.4 %collective-permute-start.1 = (f32[3,384]{1,0:T(4,128)S(1)}, f32[3,384]{1,0:T(4,128)S(1)}, u32[]{:S(2)}, u32[]{:S(2)}) collective-permute-start(f32[3,384]{1,0:T(4,128)S(1)} %convert_multiply_fusion.w_ref), channel_id=1, source_target_pairs={{0,8},{8,0},{1,9},{9,1},{2,10},{10,2},{3,11},{11,3},{4,12},{12,4},... | collective-permute-start | bytes 13832 | tf_op jit(solution)/shard_map/ppermute | solution.py:200
  53.2 10.0 %copy-start.10 = (f32[3,384]{1,0:T(4,128)}, f32[3,384]{1,0:T(4,128)S(1)}, u32[]{:S(2)}) copy-start(f32[3,384]{1,0:T(4,128)S(1)} %collective-permute-done.1.w_other_ref) | copy-start | bytes 13828
  63.2 0.7 copy-start.7
  65.6 3.7 %copy-start = (f32[1024,2304]{1,0:T(8,128)S(1)}, f32[1024,2304]{1,0:T(8,128)}, u32[]{:S(2)}) copy-start(f32[1024,2304]{1,0:T(8,128)} %get-tuple-element.12.e_ref) | copy-start | bytes 28311556
  69.3 2.3 %copy-start.1 = (bf16[3,768,1024]{2,1,0:T(8,128)(2,1)S(1)}, bf16[3,768,1024]{2,1,0:T(8,128)(2,1)}, u32[]{:S(2)}) copy-start(bf16[3,768,1024]{2,1,0:T(8,128)(2,1)} %get-tuple-element.13.q_ref) | copy-start | bytes 14155780
  71.6 0.7 copy-start.4
  79.0 14.8 %collective-permute-start.2 = (bf16[256,1024]{1,0:T(8,128)(2,1)S(1)}, bf16[256,1024]{1,0:T(8,128)(2,1)S(1)}, u32[]{:S(2)}, u32[]{:S(2)}) collective-permute-start(bf16[256,1024]{1,0:T(8,128)(2,1)S(1)} %shard_map.89), channel_id=1, source_target_pairs={{0,128},{64,192},{128,0},{192,64},{1,129},{65,193},{129,1},{193,65... | collective-permute-start | bytes 1572872 | tf_op jit(solution)/shard_map/ppermute | solution.py:214
  79.7 26.0 %collective-permute-start.3 = (bf16[256,1024]{1,0:T(8,128)(2,1)S(1)}, bf16[256,1024]{1,0:T(8,128)(2,1)S(1)}, u32[]{:S(2)}, u32[]{:S(2)}) collective-permute-start(bf16[256,1024]{1,0:T(8,128)(2,1)S(1)} %shard_map.90), channel_id=1, source_target_pairs={{0,64},{64,128},{128,192},{192,0},{1,65},{65,129},{129,193},{193,1... | collective-permute-start | bytes 1572872 | tf_op jit(solution)/shard_map/ppermute | solution.py:214
  80.0 25.7 %collective-permute-start.4 = (bf16[256,1024]{1,0:T(8,128)(2,1)S(1)}, bf16[256,1024]{1,0:T(8,128)(2,1)S(1)}, u32[]{:S(2)}, u32[]{:S(2)}) collective-permute-start(bf16[256,1024]{1,0:T(8,128)(2,1)S(1)} %shard_map.91), channel_id=1, source_target_pairs={{0,192},{64,0},{128,64},{192,128},{1,193},{65,1},{129,65},{193,129... | collective-permute-start | bytes 1572872 | tf_op jit(solution)/shard_map/ppermute | solution.py:214
  106.1 10.1 %collective-permute-start.5 = (bf16[64,1024]{1,0:T(8,128)(2,1)S(1)}, bf16[64,1024]{1,0:T(8,128)(2,1)S(1)}, u32[]{:S(2)}, u32[]{:S(2)}) collective-permute-start(bf16[64,1024]{1,0:T(8,128)(2,1)S(1)} %get-tuple-element.16), channel_id=1, source_target_pairs={{0,32},{16,48},{32,0},{48,16},{1,33},{17,49},{33,1},{49,17},{2,34}... | collective-permute-start | bytes 393224 | tf_op jit(solution)/shard_map/ppermute | solution.py:214
  110.5 5.8 %collective-permute-start.7 = (bf16[64,1024]{1,0:T(8,128)(2,1)S(1)}, bf16[64,1024]{1,0:T(8,128)(2,1)S(1)}, u32[]{:S(2)}, u32[]{:S(2)}) collective-permute-start(bf16[64,1024]{1,0:T(8,128)(2,1)S(1)} %get-tuple-element.17), channel_id=1, source_target_pairs={{0,48},{16,0},{32,16},{48,32},{1,49},{17,1},{33,17},{49,33},{2,50}... | collective-permute-start | bytes 393224 | tf_op jit(solution)/shard_map/ppermute | solution.py:214
  112.1 8.8 %collective-permute-start.6 = (bf16[64,1024]{1,0:T(8,128)(2,1)S(1)}, bf16[64,1024]{1,0:T(8,128)(2,1)S(1)}, u32[]{:S(2)}, u32[]{:S(2)}) collective-permute-start(bf16[64,1024]{1,0:T(8,128)(2,1)S(1)} %get-tuple-element.18), channel_id=1, source_target_pairs={{0,16},{16,32},{32,48},{48,0},{1,17},{17,33},{33,49},{49,1},{2,18}... | collective-permute-start | bytes 393224 | tf_op jit(solution)/shard_map/ppermute | solution.py:214

commit v2 on v1

v2 whole, which is shorter than its diff:
```python
import functools
import math

import jax
import jax.numpy as jnp
from jax import lax
from jax.experimental import pallas as pl
from jax.experimental.pallas import tpu as pltpu
from jax.sharding import Mesh
from jax.sharding import PartitionSpec as P

F32 = jnp.float32
BF16 = jnp.bfloat16
DP = ("x", "z", "core")
TOWER = ("zh", "y")
LOG2E = math.log2(math.e)
NT = (((1,), (1,)), ((), ()))
ORDER = (2, 0, 1, 3)


def full(*shape):
    return pl.BlockSpec(shape, lambda *_: (0,) * len(shape))


def one_hot_rows(ids_row, width):
    column = jnp.broadcast_to(ids_row.astype(F32), (128, 128)).T
    lane = lax.broadcasted_iota(jnp.int32, (128, 128), 1).astype(F32)
    return jnp.concatenate(
        [jnp.where(column == lane + float(v), 1.0, 0.0).astype(BF16) for v in range(0, width, 128)], axis=1
    )


def score_kernel(inv, nx, nz, x_ref, z_ref, off_ref, ids_ref, pos_ref, gain_ref, own_ref, other_ref, table_hbm,
    e_ref, q_ref, m_ref, msg_ref, table_ref, emb_ref, pos_emb_ref, msg_row, sem):
    head = pl.program_id(0)
    rows = own_ref.shape[0]
    nd = ids_ref.shape[1]
    negs = emb_ref.shape[0]
    width = table_ref.shape[0]
    off = off_ref[0]
    @pl.when(head == 0)
    def _():
        copy = pltpu.make_async_copy(table_hbm, table_ref, sem)
        copy.start()
        copy.wait()
        x, z = x_ref[0], z_ref[0]
        for a in range(0, rows, 128):
            hot = one_hot_rows(pos_ref[:, a : a + 128] - off, width)
            pos_emb_ref[a : a + 128, :] = jnp.dot(hot, table_ref[...], preferred_element_type=F32).astype(BF16)
        for b in range(0, nx * nz, 2):
            pair = []
            for i in (b, b + 1):
                rx, rz = ORDER[i // nz], i % nz
                row = lax.rem(x + rx, nx) * nz + lax.rem(z + rz, nz)
                pair.append(ids_ref[pl.ds(row, 1), :] - off)
            hot = one_hot_rows(jnp.concatenate(pair, axis=1), width)
            emb_ref[b * nd : (b + 2) * nd, :] = jnp.dot(hot, table_ref[...], preferred_element_type=F32).astype(BF16)
    gain = gain_ref[pl.ds(head, 1), :]
    q_ref[:rows, :] = (own_ref[...].astype(F32) * gain).astype(BF16)
    q_ref[rows:, :] = (other_ref[...].astype(F32) * gain).astype(BF16)
    block = 256
    for a in range(0, 2 * rows, block):
        s = lax.dot_general(emb_ref[...], q_ref[a : a + block, :], NT, preferred_element_type=F32)
        m = jnp.max(s, axis=0, keepdims=True)
        e = jnp.exp2((s - m) * (inv * LOG2E))
        e_ref[:, a : a + block] = e
        m_ref[pl.ds(head, 1), a : a + block] = m * inv
        msg_row[:, a : a + block] = m * inv + jnp.log(jnp.sum(e, axis=0, keepdims=True))
    for a in range(0, rows, 128):
        d = lax.dot_general(pos_emb_ref[a : a + 128, :], q_ref[a : a + 128, :], NT, preferred_element_type=F32)
        diag = lax.broadcasted_iota(jnp.int32, d.shape, 0) == lax.broadcasted_iota(jnp.int32, d.shape, 1)
        pos = jnp.sum(jnp.where(diag, d, 0.0), axis=0, keepdims=True) * inv
        ids = pos_ref[:, a : a + 128] - off
        owned = (ids >= 0) & (ids < width)
        base = msg_row[:, a : a + 128]
        top = jnp.maximum(base, pos)
        both = top + jnp.log(jnp.exp(base - top) + jnp.exp(pos - top))
        msg_row[:, a : a + 128] = jnp.where(owned, both, base)
        msg_row[:, 2 * rows + a : 2 * rows + a + 128] = pos
    msg_ref[pl.ds(head, 1), :] = msg_row[...]

def scores(inv, nx, nz, x, z, off, ids, pos, gain, own, other, table):
    rows, width = own.shape
    heads = gain.shape[0]
    negs = ids.size
    sm = pl.BlockSpec(memory_space=pltpu.SMEM)
    return pl.pallas_call(
        functools.partial(score_kernel, inv, nx, nz),
        grid=(heads,),
        in_specs=[sm, sm, sm, full(*ids.shape), full(*pos.shape), full(*gain.shape),
            full(rows, width), full(rows, width), pl.BlockSpec(memory_space=pl.ANY)],
        out_specs=[
            pl.BlockSpec((negs, 2 * rows), lambda h: (0, h)),
            pl.BlockSpec((None, 2 * rows, width), lambda h: (h, 0, 0)),
            full(heads, 2 * rows),
            full(heads, 3 * rows),
        ],
        out_shape=[
            jax.ShapeDtypeStruct((negs, heads * 2 * rows), F32),
            jax.ShapeDtypeStruct((heads, 2 * rows, width), BF16),
            jax.ShapeDtypeStruct((heads, 2 * rows), F32),
            jax.ShapeDtypeStruct((heads, 3 * rows), F32),
        ],
        scratch_shapes=[
            pltpu.VMEM(table.shape, BF16),
            pltpu.VMEM((negs, width), BF16),
            pltpu.VMEM((rows, width), BF16),
            pltpu.VMEM((1, 3 * rows), F32),
            pltpu.SemaphoreType.DMA,
        ],
        compiler_params=pltpu.CompilerParams(vmem_limit_bytes=30 * 2**20),
    )(x, z, off, ids, pos, gain, own, other, table)


def pair_sum(a, b):
    top = jnp.maximum(a, b)
    return top + jnp.log(jnp.exp(a - top) + jnp.exp(b - top))


def fold_kernel(*refs):
    parts, out_ref = [r[...] for r in refs[:-1]], refs[-1]
    cut = out_ref.shape[1] // 3 * 2
    top = functools.reduce(jnp.maximum, [r[:, :cut] for r in parts])
    out_ref[:, :cut] = top + jnp.log(sum(jnp.exp(r[:, :cut] - top) for r in parts))
    out_ref[:, cut:] = sum(r[:, cut:] for r in parts)


def fold(*parts):
    shape = parts[0].shape
    return pl.pallas_call(
        fold_kernel,
        grid=(1,),
        in_specs=[full(*shape)] * len(parts),
        out_specs=full(*shape),
        out_shape=jax.ShapeDtypeStruct(shape, F32),
        compiler_params=pltpu.CompilerParams(vmem_limit_bytes=2**20),
    )(*parts)


def weights(part_ref, cross_ref, m_ref, w_ref, w_other_ref, c_ref, loss_ref):
    rows = w_ref.shape[1]
    lse = pair_sum(part_ref[:, :rows], cross_ref[:, rows : 2 * rows])
    lse_other = pair_sum(part_ref[:, rows : 2 * rows], cross_ref[:, :rows])
    loss_ref[...] = w_ref[...] * (lse - part_ref[:, 2 * rows :])
    c_ref[:, :rows] = w_ref[...] * jnp.exp(m_ref[:, :rows] - lse)
    c_ref[:, rows:] = w_other_ref[...] * jnp.exp(m_ref[:, rows:] - lse_other)


def products(c_ref, e_ref, q_ref, outs, p_ref):
    heads, rows = c_ref.shape
    for h in range(heads):
        part = slice(h * rows, (h + 1) * rows)
        p_ref[:, part] = (e_ref[:, part] * c_ref[h : h + 1, :]).astype(BF16)
    term = jnp.dot(p_ref[...], q_ref[...].reshape(heads * rows, -1), preferred_element_type=F32)
    at = 0
    for out in outs:
        n = out.shape[0]
        out[...] = term[at : at + n, :].astype(out.dtype)
        at += n


def first_kernel(part_ref, cross_ref, m_ref, w_ref, w_other_ref, e_ref, q_ref, c_ref, loss_ref, *rest):
    weights(part_ref, cross_ref, m_ref, w_ref, w_other_ref, c_ref, loss_ref)
    products(c_ref, e_ref, q_ref, rest[:-1], rest[-1])


def next_kernel(c_ref, e_ref, q_ref, *rest):
    products(c_ref, e_ref, q_ref, rest[:-1], rest[-1])


def grad(small, e, q, size, index, outs):
    heads, rows, width = q.shape
    first = len(small) > 1
    made = [(heads, rows), (heads, rows // 2)] if first else []
    shapes = [jax.ShapeDtypeStruct(s, F32) for s in made] + [jax.ShapeDtypeStruct((n, width), d) for n, d in outs]
    return pl.pallas_call(
        first_kernel if first else next_kernel,
        grid=(1,),
        in_specs=[full(*s.shape) for s in small]
        + [pl.BlockSpec((size, heads * rows), lambda _: (index, 0)), full(*q.shape)],
        out_specs=[full(*s.shape) for s in shapes],
        out_shape=shapes,
        scratch_shapes=[pltpu.VMEM((size, heads * rows), BF16)],
        compiler_params=pltpu.CompilerParams(vmem_limit_bytes=(10 + size // 32) * 2**20),
        cost_estimate=pl.CostEstimate(
            flops=2 * size * heads * rows * width,
            bytes_accessed=4 * size * heads * rows + 2 * q.size,
            transcendentals=0,
        ),
    )(*small, e, q)


def shards(nx, nz, user_states, head_gain, item_table, neg_ids, pos_ids, label_mask, seq_len):
    rows, width = user_states.shape
    heads = head_gain.shape[0]
    table_rows = item_table.shape[0]
    neg_dev = neg_ids.shape[0]
    n_dp = nx * nz * lax.axis_size("core")
    factor = neg_dev * n_dp * lax.axis_size("zh") * lax.axis_size("y") / math.sqrt(rows * n_dp)
    x, z = lax.axis_index("x"), lax.axis_index("z")
    offset = (lax.axis_index("zh") * lax.axis_size("y") + lax.axis_index("y")) * table_rows

    def shifted(value, axis, size, by):
        return lax.ppermute(value, axis, [(i, (i + by) % size) for i in range(size)])

    valid = (jnp.arange(rows) < seq_len[0]).astype(F32)
    w = label_mask.astype(F32) * valid[None]
    other = shifted(user_states, "core", 2, 1)
    w_other = shifted(w, "core", 2, 1)

    slot = lax.broadcasted_iota(jnp.int32, (nx * nz, neg_dev), 0)
    slots = lax.psum(jnp.where(slot == x * nz + z, neg_ids[None], 0), ("x", "z"))

    e, q, m, msg = scores(
        1.0 / math.sqrt(width), nx, nz, x.reshape(1), z.reshape(1), offset.reshape(1), slots, pos_ids[None],
        head_gain, user_states, other, item_table,
    )
    msg = fold(msg, *[lax.ppermute(msg, "y", [(i, i ^ k) for i in range(4)]) for k in (2, 1, 3)])
    part = fold(msg, shifted(msg, "zh", 2, 1))
    cross = shifted(part, "core", 2, 1)

    quarter = nz * neg_dev
    half = quarter // 2
    c, pos_loss, far_a, far_b = grad((part, cross, m, w, w_other), e, q, quarter, 0, [(half, BF16)] * 2)
    far_a, far_b = shifted(far_a, "x", nx, 1), shifted(far_b, "x", nx, -1)
    up_a, up_b, down_a, down_b = grad(
        (c,), e, q, 2 * quarter, 1, [(half, F32), (half, BF16), (half, BF16), (half, F32)]
    )
    up_b, down_a = shifted(up_b, "x", nx, 1), shifted(down_a, "x", nx, -1)
    own_a, own_b = grad((c,), e, q, quarter, 1, [(half, F32)] * 2)
    far_a, far_b = lax.optimization_barrier((far_a, far_b))
    up_a = shifted((up_a + far_a.astype(F32)).astype(BF16), "x", nx, 1)
    down_b = shifted((down_b + far_b.astype(F32)).astype(BF16), "x", nx, -1)
    own_a = own_a + down_a.astype(F32) + up_a.astype(F32)
    own_b = own_b + up_b.astype(F32) + down_b.astype(F32)
    total = jnp.concatenate([own_a, own_b], axis=0)

    parts = [total[k * neg_dev : (k + 1) * neg_dev] for k in range(nz)]
    sent = [shifted(parts[k].astype(BF16), "z", nz, k) for k in (2, 1, 3)]
    out = parts[0]
    for piece in sent:
        out = out + piece.astype(F32)
    return pos_loss, out * factor


def solution(mesh):
    nx, nz = 4, 4
    wide = Mesh(mesh.devices.reshape(nx, nz, 2, 2, 4), DP + TOWER)
    placed = (
        P(DP, None),
        P(),
        P(TOWER, None),
        P(DP + TOWER),
        P(DP),
        P(None, DP),
        P(DP),
    )
    return jax.shard_map(
        functools.partial(shards, nx, nz),
        mesh=wide,
        in_specs=placed,
        out_specs=(P(None, DP), P(DP + TOWER, None)),
        check_vma=False,
    )
```

time: 122 us -> 94.9 us (0.78)
  waiting for transfers between devices: 40.9 us -> 25.9 us
  local copies, waits for them, and re-layouts: 12.2 us -> 4.75 us
  Pallas kernels: 27.2 us -> 20.7 us
  starting transfers between devices: 25.9 us -> 28.6 us
    ppermute x6 -> x13, starting transfers between devices: 9.3 us -> 24.8 us  [shifted(): lax.ppermute(value, axis, [(i, (i + by) % size) for i in range(size)])]
    all_to_all x1 -> x0, starting transfers between devices: 12.9 us -> none  [shards(): msg = lax.all_to_all(msg, ('core',) + TOWER, 0, 0, tiled=True)]
    all_to_all x1 -> x0, waiting for transfers between devices: 9.97 us -> none  [shards(): msg = lax.all_to_all(msg, ('core',) + TOWER, 0, 0, tiled=True)]
    unnamed x22 -> x8, local copies, waits for them, and re-layouts: 12.1 us -> 4.04 us
    ppermute x6 -> x13, waiting for transfers between devices: 29.9 us -> 23.1 us  [shifted(): lax.ppermute(value, axis, [(i, (i + by) % size) for i in range(size)])]
    pallas_call x6, Pallas kernels: 27.2 us -> 20.7 us  [the longest x1 14.7 us: scores(): pl.pallas_call(functools.partial(score_kernel, inv, nx, nz), grid=(heads,...]
    ppermute x2 -> x3, waiting for transfers between devices: 1.08 us -> 2.77 us  [shards(): lax.ppermute(msg, 'y', [(i, i ^ k) for i in range(4)])]
    ppermute x2 -> x3, starting transfers between devices: 3.69 us -> 3.78 us  [shards(): lax.ppermute(msg, 'y', [(i, i ^ k) for i in range(4)])]
  transfers between devices with their start and end apart: 9 -> 16, of which waited for: 6 -> 9; matrix products, arithmetic and copies ran while one was open for 1% -> 2% of each run, Pallas kernels for 2% -> 4%
where the time goes in v2:
time: 94.9 us; the launch traced here: 94.6 us
  starting transfers between devices  28.6 us (30%)
  waiting for transfers between devices  25.9 us (27%)
  Pallas kernels  20.7 us (22%)
  blocking collectives  11.5 us (12%)
  local copies, waits for them, and re-layouts  4.75 us (5%)
  other arithmetic  1.8 us (2%)
  between operations  1.4 us (1%)
    ppermute x13, starting transfers between devices, shifted(): lax.ppermute(value, axis, [(i, (i + by) % size) for i in range(size)])  24.8 us
    ppermute x13, waiting for transfers between devices, shifted(): lax.ppermute(value, axis, [(i, (i + by) % size) for i in range(size)])  23.1 us
    pallas_call x1, Pallas kernels, scores(): pl.pallas_call(functools.partial(score_kernel, inv, nx, nz), grid=(heads,...  14.7 us
    psum x1, blocking collectives, shards(): lax.psum(jnp.where(slot == x * nz + z, neg_ids[None], 0), ('x', 'z'))  11.5 us
    pallas_call x3, Pallas kernels, grad(): pl.pallas_call(first_kernel if first else next_kernel, grid=(1,), in_spec...  5.93 us
    unnamed x8, local copies, waits for them, and re-layouts  4.04 us
    ppermute x3, starting transfers between devices, shards(): lax.ppermute(msg, 'y', [(i, i ^ k) for i in range(4)])  3.78 us
    ppermute x3, waiting for transfers between devices, shards(): lax.ppermute(msg, 'y', [(i, i ^ k) for i in range(4)])  2.77 us
  transfers between devices with their start and end apart: 16, of which 9 were waited for; matrix products, arithmetic and copies ran while one was open for 2% of the time, Pallas kernels for 4%

profile of v2, /device:TPU:1, one launch (start us, length us, event | category | flops | bytes accessed | tf_op | source)
XLA Modules:
  0.0 94.6 jit_solution(16912195295793482509)
XLA Ops:
  0.6 3.3 %collective-permute-start = (bf16[384,1024]{1,0:T(8,128)(2,1)}, bf16[384,1024]{1,0:T(8,128)(2,1)S(1)}, u32[]{:S(2)}, u32[]{:S(2)}) collective-permute-start(bf16[384,1024]{1,0:T(8,128)(2,1)} %own_ref.1), channel_id=1, source_target_pairs={{0,8},{8,0},{1,9},{9,1},{2,10},{10,2},{3,11},{11,3},{4,12},{12,4},... | collective-permute-start | bytes 2359304 | tf_op jit(solution)/shard_map/ppermute | solution.py:204
  4.0 0.7 broadcast_in_dim.19.pos_ref
  4.7 0.7 broadcast_select_fusion
  5.4 11.5 %psum.7.ids_ref = s32[16,64]{1,0:T(8,128)S(1)} all-reduce(s32[16,64]{1,0:T(8,128)S(1)} %broadcast_select_fusion), channel_id=1, replica_groups=mesh['x'=4,'z'=4,'core'=2,'zh'=2,'y'=4] {'x','z'}, use_global_device_ids=true, to_apply=%region_0.1 | all-reduce | flops 1024 | bytes 8192 | tf_op jit(solution)/shard_map/psum | solution.py:212
  16.9 2.2 %copy-done = bf16[2048,1024]{1,0:T(8,128)(2,1)S(1)} copy-done((bf16[2048,1024]{1,0:T(8,128)(2,1)S(1)}, bf16[2048,1024]{1,0:T(8,128)(2,1)}, u32[]{:S(2)}) %copy-start) | copy-done | bytes 4194328
  19.0 1.1 %copy-done.1 = bf16[384,1024]{1,0:T(8,128)(2,1)S(1)} copy-done((bf16[384,1024]{1,0:T(8,128)(2,1)S(1)}, bf16[384,1024]{1,0:T(8,128)(2,1)}, u32[]{:S(2)}) %copy-start.1) | copy-done | bytes 786456
  20.2 0.7 copy-done.2
  20.9 14.7 %shard_map.86 = (f32[1024,2304]{1,0:T(8,128)S(1)}, bf16[3,768,1024]{2,1,0:T(8,128)(2,1)S(1)}, f32[3,768]{1,0:T(4,128)S(1)}, f32[3,1152]{1,0:T(4,128)S(1)}) custom-call(s32[1]{0:T(128)} %bitcast.x_ref, s32[1]{0:T(128)} %bitcast.1.z_ref, s32[1]{0:T(128)} %bitcast.2.off_ref, s32[16,64]{1,0:T(8,128)S(1)} %psum.7.ids_ref, s32[1,384]{1,0:T(1,128)S(1)} %broadcast_in_dim.19.pos_ref, ...), custom_call_target="tpu_custom_call" | custom-call | tf_op jit(solution)/shard_map/pallas_call | solution.py:87
  35.6 3.0 %collective-permute-start.1 = (f32[3,1152]{1,0:T(4,128)S(1)}, f32[3,1152]{1,0:T(4,128)S(1)}, u32[]{:S(2)}, u32[]{:S(2)}) collective-permute-start(f32[3,1152]{1,0:T(4,128)S(1)} %get-tuple-element.18.refs_0_), channel_id=1, source_target_pairs={{0,2},{1,3},{2,0},{3,1},{4,6},{5,7},{6,4},{7,5},{8,10},{9,11},{10,... | collective-permute-start | bytes 41480 | tf_op jit(solution)/shard_map/ppermute | solution.py:218
  38.6 0.4 collective-permute-start.2
  39.0 0.4 collective-permute-start.3
  40.0 1.2 %collective-permute-done.2.refs_2_ = f32[3,1152]{1,0:T(4,128)S(1)} collective-permute-done((f32[3,1152]{1,0:T(4,128)S(1)}, f32[3,1152]{1,0:T(4,128)S(1)}, u32[]{:S(2)}, u32[]{:S(2)}) %collective-permute-start.2) | collective-permute-done | bytes 13856 | tf_op jit(solution)/shard_map/ppermute | solution.py:218
  41.2 1.6 %collective-permute-done.3.refs_3_ = f32[3,1152]{1,0:T(4,128)S(1)} collective-permute-done((f32[3,1152]{1,0:T(4,128)S(1)}, f32[3,1152]{1,0:T(4,128)S(1)}, u32[]{:S(2)}, u32[]{:S(2)}) %collective-permute-start.3) | collective-permute-done | bytes 13856 | tf_op jit(solution)/shard_map/ppermute | solution.py:218
  42.8 5.0 %collective-permute-start.4 = (f32[3,1152]{1,0:T(4,128)S(1)}, f32[3,1152]{1,0:T(4,128)S(1)}, u32[]{:S(2)}, u32[]{:S(2)}) collective-permute-start(f32[3,1152]{1,0:T(4,128)S(1)} %shard_map.87.refs_0_), channel_id=1, source_target_pairs={{0,4},{4,0},{1,5},{5,1},{2,6},{6,2},{3,7},{7,3},{8,12},{12,8},{9,1... | collective-permute-start | bytes 41480 | tf_op jit(solution)/shard_map/ppermute | solution.py:204
  47.8 1.6 %collective-permute-done.4.refs_1_ = f32[3,1152]{1,0:T(4,128)S(1)} collective-permute-done((f32[3,1152]{1,0:T(4,128)S(1)}, f32[3,1152]{1,0:T(4,128)S(1)}, u32[]{:S(2)}, u32[]{:S(2)}) %collective-permute-start.4) | collective-permute-done | bytes 13856 | tf_op jit(solution)/shard_map/ppermute | solution.py:204
  49.5 6.8 %collective-permute-start.5 = (f32[3,1152]{1,0:T(4,128)S(1)}, f32[3,1152]{1,0:T(4,128)S(1)}, u32[]{:S(2)}, u32[]{:S(2)}) collective-permute-start(f32[3,1152]{1,0:T(4,128)S(1)} %shard_map.88.part_ref), channel_id=1, source_target_pairs={{0,8},{8,0},{1,9},{9,1},{2,10},{10,2},{3,11},{11,3},{4,12},{12,4},... | collective-permute-start | bytes 41480 | tf_op jit(solution)/shard_map/ppermute | solution.py:204
  56.3 0.1 collective-permute-start.6
  56.4 1.1 %collective-permute-done.6.w_other_ref = f32[3,384]{1,0:T(4,128)S(1)} collective-permute-done((f32[3,384]{1,0:T(4,128)S(1)}, f32[3,384]{1,0:T(4,128)S(1)}, u32[]{:S(2)}, u32[]{:S(2)}) %collective-permute-start.6) | collective-permute-done | bytes 4640 | tf_op jit(solution)/shard_map/ppermute | solution.py:204
  57.4 1.9 %shard_map.89 = (f32[3,768]{1,0:T(4,128)S(1)}, f32[3,384]{1,0:T(4,128)}, bf16[128,1024]{1,0:T(8,128)(2,1)S(1)}, bf16[128,1024]{1,0:T(8,128)(2,1)S(1)}) custom-call(f32[3,1152]{1,0:T(4,128)S(1)} %shard_map.88.part_ref, f32[3,1152]{1,0:T(4,128)S(1)} %collective-permute-done.5.cross_ref, f32[3,768]{1,0:T(4,128)S(1)} %get-tuple-element.19.m_ref, ...), custom_call_target="tpu_custom_call" | custom-call | flops 1207959552 | bytes 7077888 | tf_op jit(solution)/shard_map/pallas_call | solution.py:176
  59.3 2.7 %collective-permute-start.9 = (bf16[128,1024]{1,0:T(8,128)(2,1)S(1)}, bf16[128,1024]{1,0:T(8,128)(2,1)S(1)}, u32[]{:S(2)}, u32[]{:S(2)}) collective-permute-start(bf16[128,1024]{1,0:T(8,128)(2,1)S(1)} %get-tuple-element.28), channel_id=1, source_target_pairs={{0,192},{64,0},{128,64},{192,128},{1,193},{65,1},{129,65},{193,129... | collective-permute-start | bytes 786440 | tf_op jit(solution)/shard_map/ppermute | solution.py:204
  62.0 2.6 %shard_map.91 = (f32[128,1024]{1,0:T(8,128)S(1)}, bf16[128,1024]{1,0:T(8,128)(2,1)S(1)}, bf16[128,1024]{1,0:T(8,128)(2,1)S(1)}, f32[128,1024]{1,0:T(8,128)S(1)}) custom-call(f32[3,768]{1,0:T(4,128)S(1)} %get-tuple-element.23.c_ref, f32[1024,2304]{1,0:T(8,128)S(1)} %get-tuple-element.20.e_ref, bf16[3,768,1024]{2,1,0:T(8,128)(2,1)S(1)} %get-tuple-element.21.q_ref), custom_call_target="tpu_custom_call" | custom-call | flops 2415919104 | bytes 9437184 | tf_op jit(solution)/shard_map/pallas_call | solution.py:176
  64.7 3.6 %collective-permute-done.8 = bf16[128,1024]{1,0:T(8,128)(2,1)S(1)} collective-permute-done((bf16[128,1024]{1,0:T(8,128)(2,1)S(1)}, bf16[128,1024]{1,0:T(8,128)(2,1)S(1)}, u32[]{:S(2)}, u32[]{:S(2)}) %collective-permute-start.8) | collective-permute-done | bytes 262176 | tf_op jit(solution)/shard_map/ppermute | solution.py:204
  68.4 2.4 %collective-permute-start.12 = (bf16[128,1024]{1,0:T(8,128)(2,1)S(1)}, bf16[128,1024]{1,0:T(8,128)(2,1)S(1)}, u32[]{:S(2)}, u32[]{:S(2)}) collective-permute-start(bf16[128,1024]{1,0:T(8,128)(2,1)S(1)} %add_convert_fusion.1), channel_id=1, source_target_pairs={{0,192},{64,0},{128,64},{192,128},{1,193},{65,1},{129,65},{193,129... | collective-permute-start | bytes 786440 | tf_op jit(solution)/shard_map/ppermute | solution.py:204
  70.8 1.4 %shard_map.90 = (f32[128,1024]{1,0:T(8,128)S(1)}, f32[128,1024]{1,0:T(8,128)S(1)}) custom-call(f32[3,768]{1,0:T(4,128)S(1)} %get-tuple-element.23.c_ref, f32[1024,2304]{1,0:T(8,128)S(1)} %get-tuple-element.20.e_ref, bf16[3,768,1024]{2,1,0:T(8,128)(2,1)S(1)} %get-tuple-element.21.q_ref), custom_call_target="tpu_custom_call" | custom-call | flops 1207959552 | bytes 7077888 | tf_op jit(solution)/shard_map/pallas_call | solution.py:176
  72.4 1.5 %collective-permute-start.10 = (bf16[128,1024]{1,0:T(8,128)(2,1)S(1)}, bf16[128,1024]{1,0:T(8,128)(2,1)S(1)}, u32[]{:S(2)}, u32[]{:S(2)}) collective-permute-start(bf16[128,1024]{1,0:T(8,128)(2,1)S(1)} %add_convert_fusion.2), channel_id=1, source_target_pairs={{0,64},{64,128},{128,192},{192,0},{1,65},{65,129},{129,193},{193,1... | collective-permute-start | bytes 786440 | tf_op jit(solution)/shard_map/ppermute | solution.py:204
  73.9 1.2 %collective-permute-done.12 = bf16[128,1024]{1,0:T(8,128)(2,1)S(1)} collective-permute-done((bf16[128,1024]{1,0:T(8,128)(2,1)S(1)}, bf16[128,1024]{1,0:T(8,128)(2,1)S(1)}, u32[]{:S(2)}, u32[]{:S(2)}) %collective-permute-start.12) | collective-permute-done | bytes 262176 | tf_op jit(solution)/shard_map/ppermute | solution.py:204
  75.3 1.1 %collective-permute-start.15 = (bf16[64,1024]{1,0:T(8,128)(2,1)S(1)}, bf16[64,1024]{1,0:T(8,128)(2,1)S(1)}, u32[]{:S(2)}, u32[]{:S(2)}) collective-permute-start(bf16[64,1024]{1,0:T(8,128)(2,1)S(1)} %get-tuple-element.35), channel_id=1, source_target_pairs={{0,48},{16,0},{32,16},{48,32},{1,49},{17,1},{33,17},{49,33},{2,50}... | collective-permute-start | bytes 393224 | tf_op jit(solution)/shard_map/ppermute | solution.py:204
  76.4 4.4 %collective-permute-done.7 = bf16[128,1024]{1,0:T(8,128)(2,1)S(1)} collective-permute-done((bf16[128,1024]{1,0:T(8,128)(2,1)S(1)}, bf16[128,1024]{1,0:T(8,128)(2,1)S(1)}, u32[]{:S(2)}, u32[]{:S(2)}) %collective-permute-start.7) | collective-permute-done | bytes 262176 | tf_op jit(solution)/shard_map/ppermute | solution.py:204
  80.9 1.7 %collective-permute-start.14 = (bf16[64,1024]{1,0:T(8,128)(2,1)S(1)}, bf16[64,1024]{1,0:T(8,128)(2,1)S(1)}, u32[]{:S(2)}, u32[]{:S(2)}) collective-permute-start(bf16[64,1024]{1,0:T(8,128)(2,1)S(1)} %slice.31), channel_id=1, source_target_pairs={{0,16},{16,32},{32,48},{48,0},{1,17},{17,33},{33,49},{49,1},{2,18}... | collective-permute-start | bytes 393224 | tf_op jit(solution)/shard_map/ppermute | solution.py:204
  82.5 4.1 %collective-permute-done.14 = bf16[64,1024]{1,0:T(8,128)(2,1)S(1)} collective-permute-done((bf16[64,1024]{1,0:T(8,128)(2,1)S(1)}, bf16[64,1024]{1,0:T(8,128)(2,1)S(1)}, u32[]{:S(2)}, u32[]{:S(2)}) %collective-permute-start.14) | collective-permute-done | bytes 131104 | tf_op jit(solution)/shard_map/ppermute | solution.py:204
  86.6 7.1 %collective-permute-done.13 = bf16[64,1024]{1,0:T(8,128)(2,1)S(1)} collective-permute-done((bf16[64,1024]{1,0:T(8,128)(2,1)S(1)}, bf16[64,1024]{1,0:T(8,128)(2,1)S(1)}, u32[]{:S(2)}, u32[]{:S(2)}) %collective-permute-start.13) | collective-permute-done | bytes 131104 | tf_op jit(solution)/shard_map/ppermute | solution.py:204
  93.8 0.8 fusion.2
  (27 shorter events, 0.6 us)
Async XLA Ops:
  0.6 55.6 %copy-start.3 = (s32[3,384]{1,0:T(4,128)S(1)}, s32[3,384]{1,0:T(4,128)}, u32[]{:S(2)}) copy-start(s32[3,384]{1,0:T(4,128)} %param.12) | copy-start | bytes 13828
  0.6 16.2 %collective-permute-start = (bf16[384,1024]{1,0:T(8,128)(2,1)}, bf16[384,1024]{1,0:T(8,128)(2,1)S(1)}, u32[]{:S(2)}, u32[]{:S(2)}) collective-permute-start(bf16[384,1024]{1,0:T(8,128)(2,1)} %own_ref.1), channel_id=1, source_target_pairs={{0,8},{8,0},{1,9},{9,1},{2,10},{10,2},{3,11},{11,3},{4,12},{12,4},... | collective-permute-start | bytes 2359304 | tf_op jit(solution)/shard_map/ppermute | solution.py:204
  16.8 2.2 %copy-start = (bf16[2048,1024]{1,0:T(8,128)(2,1)S(1)}, bf16[2048,1024]{1,0:T(8,128)(2,1)}, u32[]{:S(2)}) copy-start(bf16[2048,1024]{1,0:T(8,128)(2,1)} %table_hbm.1) | copy-start | bytes 12582916
  19.0 1.1 %copy-start.1 = (bf16[384,1024]{1,0:T(8,128)(2,1)S(1)}, bf16[384,1024]{1,0:T(8,128)(2,1)}, u32[]{:S(2)}) copy-start(bf16[384,1024]{1,0:T(8,128)(2,1)} %own_ref.1) | copy-start | bytes 2359300
  20.2 0.7 copy-start.2
  35.6 4.4 %collective-permute-start.1 = (f32[3,1152]{1,0:T(4,128)S(1)}, f32[3,1152]{1,0:T(4,128)S(1)}, u32[]{:S(2)}, u32[]{:S(2)}) collective-permute-start(f32[3,1152]{1,0:T(4,128)S(1)} %get-tuple-element.18.refs_0_), channel_id=1, source_target_pairs={{0,2},{1,3},{2,0},{3,1},{4,6},{5,7},{6,4},{7,5},{8,10},{9,11},{10,... | collective-permute-start | bytes 41480 | tf_op jit(solution)/shard_map/ppermute | solution.py:218
  38.6 2.6 %collective-permute-start.2 = (f32[3,1152]{1,0:T(4,128)S(1)}, f32[3,1152]{1,0:T(4,128)S(1)}, u32[]{:S(2)}, u32[]{:S(2)}) collective-permute-start(f32[3,1152]{1,0:T(4,128)S(1)} %get-tuple-element.18.refs_0_), channel_id=1, source_target_pairs={{0,1},{1,0},{2,3},{3,2},{4,5},{5,4},{6,7},{7,6},{8,9},{9,8},{10,11... | collective-permute-start | bytes 41480 | tf_op jit(solution)/shard_map/ppermute | solution.py:218
  39.0 3.8 %collective-permute-start.3 = (f32[3,1152]{1,0:T(4,128)S(1)}, f32[3,1152]{1,0:T(4,128)S(1)}, u32[]{:S(2)}, u32[]{:S(2)}) collective-permute-start(f32[3,1152]{1,0:T(4,128)S(1)} %get-tuple-element.18.refs_0_), channel_id=1, source_target_pairs={{0,3},{1,2},{2,1},{3,0},{4,7},{5,6},{6,5},{7,4},{8,11},{9,10},{10,... | collective-permute-start | bytes 41480 | tf_op jit(solution)/shard_map/ppermute | solution.py:218
  42.8 6.6 %collective-permute-start.4 = (f32[3,1152]{1,0:T(4,128)S(1)}, f32[3,1152]{1,0:T(4,128)S(1)}, u32[]{:S(2)}, u32[]{:S(2)}) collective-permute-start(f32[3,1152]{1,0:T(4,128)S(1)} %shard_map.87.refs_0_), channel_id=1, source_target_pairs={{0,4},{4,0},{1,5},{5,1},{2,6},{6,2},{3,7},{7,3},{8,12},{12,8},{9,1... | collective-permute-start | bytes 41480 | tf_op jit(solution)/shard_map/ppermute | solution.py:204
  49.5 8.0 %collective-permute-start.5 = (f32[3,1152]{1,0:T(4,128)S(1)}, f32[3,1152]{1,0:T(4,128)S(1)}, u32[]{:S(2)}, u32[]{:S(2)}) collective-permute-start(f32[3,1152]{1,0:T(4,128)S(1)} %shard_map.88.part_ref), channel_id=1, source_target_pairs={{0,8},{8,0},{1,9},{9,1},{2,10},{10,2},{3,11},{11,3},{4,12},{12,4},... | collective-permute-start | bytes 41480 | tf_op jit(solution)/shard_map/ppermute | solution.py:204
  56.3 1.2 %collective-permute-start.6 = (f32[3,384]{1,0:T(4,128)S(1)}, f32[3,384]{1,0:T(4,128)S(1)}, u32[]{:S(2)}, u32[]{:S(2)}) collective-permute-start(f32[3,384]{1,0:T(4,128)S(1)} %convert_multiply_fusion.w_ref), channel_id=1, source_target_pairs={{0,8},{8,0},{1,9},{9,1},{2,10},{10,2},{3,11},{11,3},{4,12},{12,4},... | collective-permute-start | bytes 13832 | tf_op jit(solution)/shard_map/ppermute | solution.py:204
  59.3 9.0 %collective-permute-start.8 = (bf16[128,1024]{1,0:T(8,128)(2,1)S(1)}, bf16[128,1024]{1,0:T(8,128)(2,1)S(1)}, u32[]{:S(2)}, u32[]{:S(2)}) collective-permute-start(bf16[128,1024]{1,0:T(8,128)(2,1)S(1)} %get-tuple-element.27), channel_id=1, source_target_pairs={{0,64},{64,128},{128,192},{192,0},{1,65},{65,129},{129,193},{193,1... | collective-permute-start | bytes 786440 | tf_op jit(solution)/shard_map/ppermute | solution.py:204
  59.3 9.0 %collective-permute-start.9 = (bf16[128,1024]{1,0:T(8,128)(2,1)S(1)}, bf16[128,1024]{1,0:T(8,128)(2,1)S(1)}, u32[]{:S(2)}, u32[]{:S(2)}) collective-permute-start(bf16[128,1024]{1,0:T(8,128)(2,1)S(1)} %get-tuple-element.28), channel_id=1, source_target_pairs={{0,192},{64,0},{128,64},{192,128},{1,193},{65,1},{129,65},{193,129... | collective-permute-start | bytes 786440 | tf_op jit(solution)/shard_map/ppermute | solution.py:204
  64.6 9.3 %collective-permute-start.11 = (bf16[128,1024]{1,0:T(8,128)(2,1)S(1)}, bf16[128,1024]{1,0:T(8,128)(2,1)S(1)}, u32[]{:S(2)}, u32[]{:S(2)}) collective-permute-start(bf16[128,1024]{1,0:T(8,128)(2,1)S(1)} %get-tuple-element.31), channel_id=1, source_target_pairs={{0,64},{64,128},{128,192},{192,0},{1,65},{65,129},{129,193},{193,1... | collective-permute-start | bytes 786440 | tf_op jit(solution)/shard_map/ppermute | solution.py:204
  68.4 6.7 %collective-permute-start.12 = (bf16[128,1024]{1,0:T(8,128)(2,1)S(1)}, bf16[128,1024]{1,0:T(8,128)(2,1)S(1)}, u32[]{:S(2)}, u32[]{:S(2)}) collective-permute-start(bf16[128,1024]{1,0:T(8,128)(2,1)S(1)} %add_convert_fusion.1), channel_id=1, source_target_pairs={{0,192},{64,0},{128,64},{192,128},{1,193},{65,1},{129,65},{193,129... | collective-permute-start | bytes 786440 | tf_op jit(solution)/shard_map/ppermute | solution.py:204
  72.2 8.5 %collective-permute-start.7 = (bf16[128,1024]{1,0:T(8,128)(2,1)S(1)}, bf16[128,1024]{1,0:T(8,128)(2,1)S(1)}, u32[]{:S(2)}, u32[]{:S(2)}) collective-permute-start(bf16[128,1024]{1,0:T(8,128)(2,1)S(1)} %get-tuple-element.25), channel_id=1, source_target_pairs={{0,192},{64,0},{128,64},{192,128},{1,193},{65,1},{129,65},{193,129... | collective-permute-start | bytes 786440 | tf_op jit(solution)/shard_map/ppermute | solution.py:204
  72.4 8.4 %collective-permute-start.10 = (bf16[128,1024]{1,0:T(8,128)(2,1)S(1)}, bf16[128,1024]{1,0:T(8,128)(2,1)S(1)}, u32[]{:S(2)}, u32[]{:S(2)}) collective-permute-start(bf16[128,1024]{1,0:T(8,128)(2,1)S(1)} %add_convert_fusion.2), channel_id=1, source_target_pairs={{0,64},{64,128},{128,192},{192,0},{1,65},{65,129},{129,193},{193,1... | collective-permute-start | bytes 786440 | tf_op jit(solution)/shard_map/ppermute | solution.py:204
  75.3 7.3 %collective-permute-start.15 = (bf16[64,1024]{1,0:T(8,128)(2,1)S(1)}, bf16[64,1024]{1,0:T(8,128)(2,1)S(1)}, u32[]{:S(2)}, u32[]{:S(2)}) collective-permute-start(bf16[64,1024]{1,0:T(8,128)(2,1)S(1)} %get-tuple-element.35), channel_id=1, source_target_pairs={{0,48},{16,0},{32,16},{48,32},{1,49},{17,1},{33,17},{49,33},{2,50}... | collective-permute-start | bytes 393224 | tf_op jit(solution)/shard_map/ppermute | solution.py:204
  80.9 5.8 %collective-permute-start.14 = (bf16[64,1024]{1,0:T(8,128)(2,1)S(1)}, bf16[64,1024]{1,0:T(8,128)(2,1)S(1)}, u32[]{:S(2)}, u32[]{:S(2)}) collective-permute-start(bf16[64,1024]{1,0:T(8,128)(2,1)S(1)} %slice.31), channel_id=1, source_target_pairs={{0,16},{16,32},{32,48},{48,0},{1,17},{17,33},{33,49},{49,1},{2,18}... | collective-permute-start | bytes 393224 | tf_op jit(solution)/shard_map/ppermute | solution.py:204
  82.5 11.2 %collective-permute-start.13 = (bf16[64,1024]{1,0:T(8,128)(2,1)S(1)}, bf16[64,1024]{1,0:T(8,128)(2,1)S(1)}, u32[]{:S(2)}, u32[]{:S(2)}) collective-permute-start(bf16[64,1024]{1,0:T(8,128)(2,1)S(1)} %get-tuple-element.34), channel_id=1, source_target_pairs={{0,32},{16,48},{32,0},{48,16},{1,33},{17,49},{33,1},{49,17},{2,34}... | collective-permute-start | bytes 393224 | tf_op jit(solution)/shard_map/ppermute | solution.py:204

commit v3 on v2

v3 whole, which is shorter than its diff:
```python
import functools
import math

import jax
import jax.numpy as jnp
from jax import lax
from jax.experimental import pallas as pl
from jax.experimental.pallas import tpu as pltpu
from jax.sharding import Mesh
from jax.sharding import PartitionSpec as P

F32 = jnp.float32
BF16 = jnp.bfloat16
DP = ("x", "z", "core")
TOWER = ("zh", "y")
LOG2E = math.log2(math.e)
NT = (((1,), (1,)), ((), ()))
ORDER = (2, 0, 1, 3)
Z_ORDER = (2, 3, 1, 0)


def full(*shape):
    return pl.BlockSpec(shape, lambda *_: (0,) * len(shape))


def one_hot_rows(ids_row, width):
    column = jnp.broadcast_to(ids_row.astype(F32), (128, 128)).T
    lane = lax.broadcasted_iota(jnp.int32, (128, 128), 1).astype(F32)
    return jnp.concatenate(
        [jnp.where(column == lane + float(v), 1.0, 0.0).astype(BF16) for v in range(0, width, 128)], axis=1
    )


def score_kernel(
    inv, nx, nz, x_ref, z_ref, off_ref, ids_ref, pos_ref, gain_ref, own_ref, other_ref, table_hbm,
    e_ref, q_ref, m_ref, msg_ref, table_ref, emb_ref, pos_emb_ref, sem,
):
    heads = gain_ref.shape[0]
    rows = own_ref.shape[0]
    nd = ids_ref.shape[1]
    width = table_ref.shape[0]
    off = off_ref[0]
    x, z = x_ref[0], z_ref[0]
    copy = pltpu.make_async_copy(table_hbm, table_ref, sem)
    copy.start()
    for head in range(heads):
        gain = gain_ref[head : head + 1, :]
        q_ref[head, :rows, :] = (own_ref[...].astype(F32) * gain).astype(BF16)
        q_ref[head, rows:, :] = (other_ref[...].astype(F32) * gain).astype(BF16)
    copy.wait()
    for b in range(0, nx * nz, 2):
        pair = []
        for i in (b, b + 1):
            rx, rz = ORDER[i // nz], Z_ORDER[i % nz]
            row = lax.rem(x + rx, nx) * nz + lax.rem(z + rz, nz)
            pair.append(ids_ref[pl.ds(row, 1), :] - off)
        hot = one_hot_rows(jnp.concatenate(pair, axis=1), width)
        emb_ref[b * nd : (b + 2) * nd, :] = jnp.dot(hot, table_ref[...], preferred_element_type=F32).astype(BF16)
    pos_ids = [pos_ref[a : a + 128].reshape(1, 128) - off for a in range(0, rows, 128)]
    for i, ids in enumerate(pos_ids):
        hot = one_hot_rows(ids, width)
        pos_emb_ref[i * 128 : i * 128 + 128, :] = jnp.dot(hot, table_ref[...], preferred_element_type=F32).astype(BF16)
    block = 256
    for head in range(heads):
        for a in range(0, 2 * rows, block):
            s = lax.dot_general(emb_ref[...], q_ref[head, a : a + block, :], NT, preferred_element_type=F32)
            m = jnp.max(s, axis=0, keepdims=True)
            e = jnp.exp2((s - m) * (inv * LOG2E))
            at = head * 2 * rows + a
            e_ref[:, at : at + block] = e
            m_ref[head : head + 1, a : a + block] = m * inv
            msg_ref[head : head + 1, a : a + block] = m * inv + jnp.log(jnp.sum(e, axis=0, keepdims=True))
        for i, ids in enumerate(pos_ids):
            a = i * 128
            d = lax.dot_general(
                pos_emb_ref[a : a + 128, :], q_ref[head, a : a + 128, :], NT, preferred_element_type=F32
            )
            diag = lax.broadcasted_iota(jnp.int32, d.shape, 0) == lax.broadcasted_iota(jnp.int32, d.shape, 1)
            pos = jnp.sum(jnp.where(diag, d, 0.0), axis=0, keepdims=True) * inv
            owned = (ids >= 0) & (ids < width)
            base = msg_ref[head : head + 1, a : a + 128]
            msg_ref[head : head + 1, a : a + 128] = jnp.where(owned, pair_sum(base, pos), base)
            msg_ref[head : head + 1, 2 * rows + a : 2 * rows + a + 128] = pos


def scores(inv, nx, nz, x, z, off, ids, pos, gain, own, other, table):
    rows, width = own.shape
    heads = gain.shape[0]
    negs = ids.size
    sm = pl.BlockSpec(memory_space=pltpu.SMEM)
    return pl.pallas_call(
        functools.partial(score_kernel, inv, nx, nz),
        grid=(1,),
        in_specs=[sm, sm, sm, full(*ids.shape), full(*pos.shape), full(*gain.shape),
            full(rows, width), full(rows, width), pl.BlockSpec(memory_space=pl.ANY)],
        out_specs=[
            full(negs, heads * 2 * rows),
            full(heads, 2 * rows, width),
            full(heads, 2 * rows),
            full(heads, 3 * rows),
        ],
        out_shape=[
            jax.ShapeDtypeStruct((negs, heads * 2 * rows), F32),
            jax.ShapeDtypeStruct((heads, 2 * rows, width), BF16),
            jax.ShapeDtypeStruct((heads, 2 * rows), F32),
            jax.ShapeDtypeStruct((heads, 3 * rows), F32),
        ],
        scratch_shapes=[
            pltpu.VMEM(table.shape, BF16),
            pltpu.VMEM((negs, width), BF16),
            pltpu.VMEM((rows, width), BF16),
            pltpu.SemaphoreType.DMA,
        ],
        compiler_params=pltpu.CompilerParams(vmem_limit_bytes=30 * 2**20),
    )(x, z, off, ids, pos, gain, own, other, table)


def pair_sum(a, b):
    top = jnp.maximum(a, b)
    return top + jnp.log(jnp.exp(a - top) + jnp.exp(b - top))


def fold_kernel(*refs):
    parts, out_ref = [r[...] for r in refs[:-1]], refs[-1]
    cut = out_ref.shape[1] // 3 * 2
    top = functools.reduce(jnp.maximum, [r[:, :cut] for r in parts])
    out_ref[:, :cut] = top + jnp.log(sum(jnp.exp(r[:, :cut] - top) for r in parts))
    out_ref[:, cut:] = sum(r[:, cut:] for r in parts)


def fold(*parts):
    shape = parts[0].shape
    return pl.pallas_call(
        fold_kernel,
        grid=(1,),
        in_specs=[full(*shape)] * len(parts),
        out_specs=full(*shape),
        out_shape=jax.ShapeDtypeStruct(shape, F32),
        compiler_params=pltpu.CompilerParams(vmem_limit_bytes=2**20),
    )(*parts)


def mask_kernel(len_ref, mask_ref, msg_ref, near_ref, out_ref):
    rows = mask_ref.shape[1]
    a, b = msg_ref[...], near_ref[...]
    out_ref[:, : 2 * rows] = pair_sum(a[:, : 2 * rows], b[:, : 2 * rows])
    out_ref[:, 2 * rows : 3 * rows] = a[:, 2 * rows :] + b[:, 2 * rows :]
    valid = lax.broadcasted_iota(jnp.int32, mask_ref.shape, 1) < len_ref[0]
    out_ref[:, 3 * rows :] = jnp.where(valid, mask_ref[...].astype(F32), 0.0)


def fold_with_mask(seq_len, mask, msg, near):
    heads, rows = mask.shape
    return pl.pallas_call(
        mask_kernel,
        grid=(1,),
        in_specs=[pl.BlockSpec(memory_space=pltpu.SMEM), full(*mask.shape), full(*msg.shape), full(*msg.shape)],
        out_specs=full(heads, 4 * rows),
        out_shape=jax.ShapeDtypeStruct((heads, 4 * rows), F32),
        compiler_params=pltpu.CompilerParams(vmem_limit_bytes=2**20),
    )(seq_len, mask, msg, near)


def weights(part_ref, cross_ref, m_ref, c_ref, loss_ref):
    rows = loss_ref.shape[1]
    w = part_ref[:, 3 * rows :]
    lse = pair_sum(part_ref[:, :rows], cross_ref[:, rows : 2 * rows])
    lse_other = pair_sum(part_ref[:, rows : 2 * rows], cross_ref[:, :rows])
    loss_ref[...] = w * (lse - part_ref[:, 2 * rows : 3 * rows])
    c_ref[:, :rows] = w * jnp.exp(m_ref[:, :rows] - lse)
    c_ref[:, rows:] = cross_ref[:, 3 * rows :] * jnp.exp(m_ref[:, rows:] - lse_other)


def products(c_ref, e_ref, q_ref, outs, p_ref):
    heads, rows = c_ref.shape
    for h in range(heads):
        part = slice(h * rows, (h + 1) * rows)
        p_ref[:, part] = (e_ref[:, part] * c_ref[h : h + 1, :]).astype(BF16)
    term = jnp.dot(p_ref[...], q_ref[...].reshape(heads * rows, -1), preferred_element_type=F32)
    at = 0
    for out in outs:
        n = out.shape[0]
        out[...] = term[at : at + n, :].astype(out.dtype)
        at += n


def first_kernel(part_ref, cross_ref, m_ref, e_ref, q_ref, c_ref, loss_ref, *rest):
    weights(part_ref, cross_ref, m_ref, c_ref, loss_ref)
    products(c_ref, e_ref, q_ref, rest[:-1], rest[-1])


def next_kernel(c_ref, e_ref, q_ref, *rest):
    products(c_ref, e_ref, q_ref, rest[:-1], rest[-1])


def last_kernel(c_ref, in_a_ref, in_b_ref, e_ref, q_ref, out_a_ref, out_b_ref, p_ref):
    products(c_ref, e_ref, q_ref, (out_a_ref, out_b_ref), p_ref)
    out_a_ref[...] += in_a_ref[...].astype(F32)
    out_b_ref[...] += in_b_ref[...].astype(F32)


def grad(small, e, q, size, index, outs):
    heads, rows, width = q.shape
    body = next_kernel if len(small) == 1 else first_kernel if small[-1].dtype == F32 else last_kernel
    made = [(heads, rows), (heads, rows // 2)] if body is first_kernel else []
    shapes = [jax.ShapeDtypeStruct(s, F32) for s in made] + [jax.ShapeDtypeStruct((n, width), d) for n, d in outs]
    return pl.pallas_call(
        body,
        grid=(1,),
        in_specs=[full(*s.shape) for s in small]
        + [pl.BlockSpec((size, heads * rows), lambda _: (index, 0)), full(*q.shape)],
        out_specs=[full(*s.shape) for s in shapes],
        out_shape=shapes,
        scratch_shapes=[pltpu.VMEM((size, heads * rows), BF16)],
        compiler_params=pltpu.CompilerParams(vmem_limit_bytes=(10 + size // 32) * 2**20),
        cost_estimate=pl.CostEstimate(
            flops=2 * size * heads * rows * width,
            bytes_accessed=4 * size * heads * rows + 2 * q.size,
            transcendentals=0,
        ),
    )(*small, e, q)


def shards(nx, nz, user_states, head_gain, item_table, neg_ids, pos_ids, label_mask, seq_len):
    rows, width = user_states.shape
    heads = head_gain.shape[0]
    table_rows = item_table.shape[0]
    neg_dev = neg_ids.shape[0]
    n_dp = nx * nz * lax.axis_size("core")
    factor = neg_dev * n_dp * lax.axis_size("zh") * lax.axis_size("y") / math.sqrt(rows * n_dp)
    x, z = lax.axis_index("x"), lax.axis_index("z")
    offset = (lax.axis_index("zh") * lax.axis_size("y") + lax.axis_index("y")) * table_rows

    def shifted(value, axis, size, by):
        return lax.ppermute(value, axis, [(i, (i + by) % size) for i in range(size)])

    other = shifted(user_states, "core", 2, 1)
    table = shifted(item_table, "core", 2, 1)
    gain = shifted(head_gain, "core", 2, 1)

    slot = lax.broadcasted_iota(jnp.int32, (nx * nz, neg_dev), 0)
    slots = lax.psum(jnp.where(slot == x * nz + z, neg_ids[None], 0), ("x", "z"))

    e, q, m, msg = scores(
        1.0 / math.sqrt(width), nx, nz, x.reshape(1), z.reshape(1), offset.reshape(1), slots, pos_ids,
        gain, user_states, other, table,
    )
    msg = fold(msg, *[lax.ppermute(msg, "y", [(i, i ^ k) for i in range(4)]) for k in (2, 1, 3)])
    part = fold_with_mask(seq_len, label_mask, msg, shifted(msg, "zh", 2, 1))
    cross = shifted(part, "core", 2, 1)

    quarter = nz * neg_dev
    half = quarter // 2
    c, pos_loss, far_a, far_b = grad((part, cross, m), e, q, quarter, 0, [(half, BF16)] * 2)
    far_a, far_b = shifted(far_a, "x", nx, 1), shifted(far_b, "x", nx, -1)
    up_a, up_b, down_a, down_b = grad(
        (c,), e, q, 2 * quarter, 1, [(half, F32), (half, BF16), (half, BF16), (half, F32)]
    )
    up_b, down_a = shifted(up_b, "x", nx, 1), shifted(down_a, "x", nx, -1)
    far_a, far_b = lax.optimization_barrier((far_a, far_b))
    up_a = shifted((up_a + far_a.astype(F32)).astype(BF16), "x", nx, 1)
    down_b = shifted((down_b + far_b.astype(F32)).astype(BF16), "x", nx, -1)
    own_a, own_b = grad((c, down_a, up_b), e, q, quarter, 1, [(half, F32)] * 2)
    total = jnp.concatenate([own_a + up_a.astype(F32), own_b + down_b.astype(F32)], axis=0)

    parts = {k: total[i * neg_dev : (i + 1) * neg_dev] for i, k in enumerate(Z_ORDER)}
    sent = [shifted(parts[k].astype(BF16), "z", nz, k) for k in Z_ORDER if k]
    out = parts[0]
    for piece in sent:
        out = out + piece.astype(F32)
    return pos_loss, out * factor


def solution(mesh):
    nx, nz = 4, 4
    wide = Mesh(mesh.devices.reshape(nx, nz, 2, 2, 4), DP + TOWER)
    placed = (
        P(DP, None),
        P(),
        P(TOWER, None),
        P(DP + TOWER),
        P(DP),
        P(None, DP),
        P(DP),
    )
    return jax.shard_map(
        functools.partial(shards, nx, nz),
        mesh=wide,
        in_specs=placed,
        out_specs=(P(None, DP), P(DP + TOWER, None)),
        check_vma=False,
    )
```

time: 94.9 us -> 90.3 us (0.952); the launches traced: 94.6 us -> 88.7 us
  waiting for transfers between devices: 25.9 us -> 20.6 us
  local copies, waits for them, and re-layouts: 4.75 us -> 1.85 us
  starting transfers between devices: 28.6 us -> 30.2 us
    ppermute x13 -> x14, waiting for transfers between devices: 23.1 us -> 17.2 us  [shifted(): lax.ppermute(value, axis, [(i, (i + by) % size) for i in range(size)])]
    unnamed x8 -> x6, local copies, waits for them, and re-layouts: 4.04 us -> 1.81 us
    ppermute x13 -> x14, starting transfers between devices: 24.8 us -> 26.4 us  [shifted(): lax.ppermute(value, axis, [(i, (i + by) % size) for i in range(size)])]
    pallas_call x4 -> x5, Pallas kernels: 20.6 us -> 21.4 us  [the longest x1 15.4 us: scores(): pl.pallas_call(functools.partial(score_kernel, inv, nx, nz), grid=(1,), i...]
  transfers between devices with their start and end apart: 16 -> 17, of which waited for: 9 -> 12; matrix products, arithmetic and copies ran while one was open for 2% -> 1% of each run, Pallas kernels for 4% -> 5%
where the time goes in v3:
time: 90.3 us; the launch traced here: 88.7 us
  starting transfers between devices  30.2 us (33%)
  Pallas kernels  21.4 us (24%)
  waiting for transfers between devices  20.6 us (23%)
  blocking collectives  11.5 us (13%)
  local copies, waits for them, and re-layouts  1.85 us (2%)
  other arithmetic  1.74 us (2%)
  between operations  1.42 us (2%)
    ppermute x14, starting transfers between devices, shifted(): lax.ppermute(value, axis, [(i, (i + by) % size) for i in range(size)])  26.4 us
    ppermute x14, waiting for transfers between devices, shifted(): lax.ppermute(value, axis, [(i, (i + by) % size) for i in range(size)])  17.2 us
    pallas_call x1, Pallas kernels, scores(): pl.pallas_call(functools.partial(score_kernel, inv, nx, nz), grid=(1,), i...  15.4 us
    psum x1, blocking collectives, shards(): lax.psum(jnp.where(slot == x * nz + z, neg_ids[None], 0), ('x', 'z'))  11.5 us
    pallas_call x3, Pallas kernels, grad(): pl.pallas_call(body, grid=(1,), in_specs=[full(*s.shape) for s in small]...  5.95 us
    ppermute x3, starting transfers between devices, shards(): lax.ppermute(msg, 'y', [(i, i ^ k) for i in range(4)])  3.79 us
    ppermute x3, waiting for transfers between devices, shards(): lax.ppermute(msg, 'y', [(i, i ^ k) for i in range(4)])  3.44 us
    unnamed x6, local copies, waits for them, and re-layouts  1.81 us
  transfers between devices with their start and end apart: 17, of which 12 were waited for; matrix products, arithmetic and copies ran while one was open for 1% of the time, Pallas kernels for 5%

profile of v3, /device:TPU:1, one launch (start us, length us, event | category | flops | bytes accessed | tf_op | source)
XLA Modules:
  0.0 88.7 jit_solution(15895676431687628889)
XLA Ops:
  0.6 3.3 %collective-permute-start.2 = (bf16[2048,1024]{1,0:T(8,128)(2,1)}, bf16[2048,1024]{1,0:T(8,128)(2,1)}, u32[]{:S(2)}, u32[]{:S(2)}) collective-permute-start(bf16[2048,1024]{1,0:T(8,128)(2,1)} %param.9), channel_id=1, source_target_pairs={{0,8},{8,0},{1,9},{9,1},{2,10},{10,2},{3,11},{11,3},{4,12},{12,4},... | collective-permute-start | bytes 12582920 | tf_op jit(solution)/shard_map/ppermute | solution.py:235
  4.1 0.4 collective-permute-start
  4.5 0.7 broadcast_select_fusion
  5.2 11.5 %psum.7.ids_ref = s32[16,64]{1,0:T(8,128)S(1)} all-reduce(s32[16,64]{1,0:T(8,128)S(1)} %broadcast_select_fusion), channel_id=1, replica_groups=mesh['x'=4,'z'=4,'core'=2,'zh'=2,'y'=4] {'x','z'}, use_global_device_ids=true, to_apply=%region_0.1 | all-reduce | flops 1024 | bytes 8192 | tf_op jit(solution)/shard_map/psum | solution.py:242
  16.7 1.1 %copy-done = bf16[384,1024]{1,0:T(8,128)(2,1)S(1)} copy-done((bf16[384,1024]{1,0:T(8,128)(2,1)S(1)}, bf16[384,1024]{1,0:T(8,128)(2,1)}, u32[]{:S(2)}) %copy-start) | copy-done | bytes 786456
  17.8 0.7 copy-done.2
  18.5 15.4 %shard_map.86 = (f32[1024,2304]{1,0:T(8,128)S(1)}, bf16[3,768,1024]{2,1,0:T(8,128)(2,1)S(1)}, f32[3,768]{1,0:T(4,128)S(1)}, f32[3,1152]{1,0:T(4,128)S(1)}) custom-call(s32[1]{0:T(128)} %bitcast.x_ref, s32[1]{0:T(128)} %bitcast.1.z_ref, s32[1]{0:T(128)} %bitcast.2.off_ref, s32[16,64]{1,0:T(8,128)S(1)} %psum.7.ids_ref, s32[384]{0:T(512)S(1)} %copy-done.2, ...), custom_call_target="tpu_custom_call" | custom-call | tf_op jit(solution)/shard_map/pallas_call | solution.py:91
  34.0 3.0 %collective-permute-start.3 = (f32[3,1152]{1,0:T(4,128)S(1)}, f32[3,1152]{1,0:T(4,128)S(1)}, u32[]{:S(2)}, u32[]{:S(2)}) collective-permute-start(f32[3,1152]{1,0:T(4,128)S(1)} %get-tuple-element.18.refs_0_), channel_id=1, source_target_pairs={{0,2},{1,3},{2,0},{3,1},{4,6},{5,7},{6,4},{7,5},{8,10},{9,11},{10,... | collective-permute-start | bytes 41480 | tf_op jit(solution)/shard_map/ppermute | solution.py:248
  37.0 0.4 collective-permute-start.4
  37.4 0.4 collective-permute-start.5
  37.7 0.4 collective-permute-done.3.refs_1_
  38.2 1.4 %collective-permute-done.4.refs_2_ = f32[3,1152]{1,0:T(4,128)S(1)} collective-permute-done((f32[3,1152]{1,0:T(4,128)S(1)}, f32[3,1152]{1,0:T(4,128)S(1)}, u32[]{:S(2)}, u32[]{:S(2)}) %collective-permute-start.4) | collective-permute-done | bytes 13856 | tf_op jit(solution)/shard_map/ppermute | solution.py:248
  39.6 1.6 %collective-permute-done.5.refs_3_ = f32[3,1152]{1,0:T(4,128)S(1)} collective-permute-done((f32[3,1152]{1,0:T(4,128)S(1)}, f32[3,1152]{1,0:T(4,128)S(1)}, u32[]{:S(2)}, u32[]{:S(2)}) %collective-permute-start.5) | collective-permute-done | bytes 13856 | tf_op jit(solution)/shard_map/ppermute | solution.py:248
  41.2 5.0 %collective-permute-start.6 = (f32[3,1152]{1,0:T(4,128)S(1)}, f32[3,1152]{1,0:T(4,128)S(1)}, u32[]{:S(2)}, u32[]{:S(2)}) collective-permute-start(f32[3,1152]{1,0:T(4,128)S(1)} %shard_map.87.msg_ref), channel_id=1, source_target_pairs={{0,4},{4,0},{1,5},{5,1},{2,6},{6,2},{3,7},{7,3},{8,12},{12,8},{9,1... | collective-permute-start | bytes 41480 | tf_op jit(solution)/shard_map/ppermute | solution.py:235
  46.9 0.9 %collective-permute-done.6.near_ref = f32[3,1152]{1,0:T(4,128)S(1)} collective-permute-done((f32[3,1152]{1,0:T(4,128)S(1)}, f32[3,1152]{1,0:T(4,128)S(1)}, u32[]{:S(2)}, u32[]{:S(2)}) %collective-permute-start.6) | collective-permute-done | bytes 13856 | tf_op jit(solution)/shard_map/ppermute | solution.py:235
  47.8 6.6 %collective-permute-start.7 = (f32[3,1536]{1,0:T(4,128)S(1)}, f32[3,1536]{1,0:T(4,128)S(1)}, u32[]{:S(2)}, u32[]{:S(2)}) collective-permute-start(f32[3,1536]{1,0:T(4,128)S(1)} %shard_map.88.part_ref), channel_id=1, source_target_pairs={{0,8},{8,0},{1,9},{9,1},{2,10},{10,2},{3,11},{11,3},{4,12},{12,4},... | collective-permute-start | bytes 55304 | tf_op jit(solution)/shard_map/ppermute | solution.py:235
  54.5 0.8 collective-permute-done.7.cross_ref
  55.3 1.9 %shard_map.89 = (f32[3,768]{1,0:T(4,128)S(1)}, f32[3,384]{1,0:T(4,128)}, bf16[128,1024]{1,0:T(8,128)(2,1)S(1)}, bf16[128,1024]{1,0:T(8,128)(2,1)S(1)}) custom-call(f32[3,1536]{1,0:T(4,128)S(1)} %shard_map.88.part_ref, f32[3,1536]{1,0:T(4,128)S(1)} %collective-permute-done.7.cross_ref, f32[3,768]{1,0:T(4,128)S(1)} %get-tuple-element.19.m_ref, ...), custom_call_target="tpu_custom_call" | custom-call | flops 1207959552 | bytes 7077888 | tf_op jit(solution)/shard_map/pallas_call | solution.py:207
  57.2 2.7 %collective-permute-start.11 = (bf16[128,1024]{1,0:T(8,128)(2,1)S(1)}, bf16[128,1024]{1,0:T(8,128)(2,1)S(1)}, u32[]{:S(2)}, u32[]{:S(2)}) collective-permute-start(bf16[128,1024]{1,0:T(8,128)(2,1)S(1)} %get-tuple-element.29), channel_id=1, source_target_pairs={{0,192},{64,0},{128,64},{192,128},{1,193},{65,1},{129,65},{193,129... | collective-permute-start | bytes 786440 | tf_op jit(solution)/shard_map/ppermute | solution.py:235
  59.9 2.6 %shard_map.90 = (f32[128,1024]{1,0:T(8,128)S(1)}, bf16[128,1024]{1,0:T(8,128)(2,1)S(1)}, bf16[128,1024]{1,0:T(8,128)(2,1)S(1)}, f32[128,1024]{1,0:T(8,128)S(1)}) custom-call(f32[3,768]{1,0:T(4,128)S(1)} %get-tuple-element.23.c_ref, f32[1024,2304]{1,0:T(8,128)S(1)} %get-tuple-element.20.e_ref, bf16[3,768,1024]{2,1,0:T(8,128)(2,1)S(1)} %get-tuple-element.21.q_ref), custom_call_target="tpu_custom_call" | custom-call | flops 2415919104 | bytes 9437184 | tf_op jit(solution)/shard_map/pallas_call | solution.py:207
  62.6 1.5 %collective-permute-start.9 = (bf16[128,1024]{1,0:T(8,128)(2,1)S(1)}, bf16[128,1024]{1,0:T(8,128)(2,1)S(1)}, u32[]{:S(2)}, u32[]{:S(2)}) collective-permute-start(bf16[128,1024]{1,0:T(8,128)(2,1)S(1)} %get-tuple-element.25), channel_id=1, source_target_pairs={{0,64},{64,128},{128,192},{192,0},{1,65},{65,129},{129,193},{193,1... | collective-permute-start | bytes 786440 | tf_op jit(solution)/shard_map/ppermute | solution.py:235
  64.1 1.9 %collective-permute-done.10 = bf16[128,1024]{1,0:T(8,128)(2,1)S(1)} collective-permute-done((bf16[128,1024]{1,0:T(8,128)(2,1)S(1)}, bf16[128,1024]{1,0:T(8,128)(2,1)S(1)}, u32[]{:S(2)}, u32[]{:S(2)}) %collective-permute-start.10) | collective-permute-done | bytes 262176 | tf_op jit(solution)/shard_map/ppermute | solution.py:235
  66.2 2.7 %collective-permute-start.12 = (bf16[128,1024]{1,0:T(8,128)(2,1)S(1)}, bf16[128,1024]{1,0:T(8,128)(2,1)S(1)}, u32[]{:S(2)}, u32[]{:S(2)}) collective-permute-start(bf16[128,1024]{1,0:T(8,128)(2,1)S(1)} %add_convert_fusion.2), channel_id=1, source_target_pairs={{0,192},{64,0},{128,64},{192,128},{1,193},{65,1},{129,65},{193,129... | collective-permute-start | bytes 786440 | tf_op jit(solution)/shard_map/ppermute | solution.py:235
  69.0 1.6 %collective-permute-done.8.in_a_ref = bf16[128,1024]{1,0:T(8,128)(2,1)S(1)} collective-permute-done((bf16[128,1024]{1,0:T(8,128)(2,1)S(1)}, bf16[128,1024]{1,0:T(8,128)(2,1)S(1)}, u32[]{:S(2)}, u32[]{:S(2)}) %collective-permute-start.8) | collective-permute-done | bytes 262176 | tf_op jit(solution)/shard_map/ppermute | solution.py:235
  70.6 0.6 collective-permute-done.9.in_b_ref
  71.1 1.4 %shard_map.91 = (f32[128,1024]{1,0:T(8,128)S(1)}, f32[128,1024]{1,0:T(8,128)S(1)}) custom-call(f32[3,768]{1,0:T(4,128)S(1)} %get-tuple-element.23.c_ref, bf16[128,1024]{1,0:T(8,128)(2,1)S(1)} %collective-permute-done.8.in_a_ref, bf16[128,1024]{1,0:T(8,128)(2,1)S(1)} %collective-permute-done.9.in_b_ref, f32[1024,2304]{1,0:T(8,128)S(1)} %get-tuple-element.20.e_ref, ...), custom_call_target="tpu_custom_call" | custom-call | flops 1207959552 | bytes 7077888 | tf_op jit(solution)/shard_map/pallas_call | solution.py:207
  72.6 4.2 %collective-permute-done.13 = bf16[128,1024]{1,0:T(8,128)(2,1)S(1)} collective-permute-done((bf16[128,1024]{1,0:T(8,128)(2,1)S(1)}, bf16[128,1024]{1,0:T(8,128)(2,1)S(1)}, u32[]{:S(2)}, u32[]{:S(2)}) %collective-permute-start.13) | collective-permute-done | bytes 262176 | tf_op jit(solution)/shard_map/ppermute | solution.py:235
  76.8 0.7 collective-permute-start.14
  77.5 3.1 %collective-permute-start.15 = (bf16[64,1024]{1,0:T(8,128)(2,1)S(1)}, bf16[64,1024]{1,0:T(8,128)(2,1)S(1)}, u32[]{:S(2)}, u32[]{:S(2)}) collective-permute-start(bf16[64,1024]{1,0:T(8,128)(2,1)S(1)} %get-tuple-element.35), channel_id=1, source_target_pairs={{0,48},{16,0},{32,16},{48,32},{1,49},{17,1},{33,17},{49,33},{2,50}... | collective-permute-start | bytes 393224 | tf_op jit(solution)/shard_map/ppermute | solution.py:235
  80.8 2.3 %collective-permute-done.14 = bf16[64,1024]{1,0:T(8,128)(2,1)S(1)} collective-permute-done((bf16[64,1024]{1,0:T(8,128)(2,1)S(1)}, bf16[64,1024]{1,0:T(8,128)(2,1)S(1)}, u32[]{:S(2)}, u32[]{:S(2)}) %collective-permute-start.14) | collective-permute-done | bytes 131104 | tf_op jit(solution)/shard_map/ppermute | solution.py:235
  83.4 4.6 %collective-permute-done.16 = bf16[64,1024]{1,0:T(8,128)(2,1)S(1)} collective-permute-done((bf16[64,1024]{1,0:T(8,128)(2,1)S(1)}, bf16[64,1024]{1,0:T(8,128)(2,1)S(1)}, u32[]{:S(2)}, u32[]{:S(2)}) %collective-permute-start.16) | collective-permute-done | bytes 131104 | tf_op jit(solution)/shard_map/ppermute | solution.py:235
  88.0 0.8 fusion.2
  (24 shorter events, 1.0 us)
Async XLA Ops:
  0.6 47.2 %copy-start.1 = (s32[3,384]{1,0:T(4,128)S(1)}, s32[3,384]{1,0:T(4,128)}, u32[]{:S(2)}) copy-start(s32[3,384]{1,0:T(4,128)} %mask_ref.1) | copy-start | bytes 13828
  0.6 16.0 %collective-permute-start.2 = (bf16[2048,1024]{1,0:T(8,128)(2,1)}, bf16[2048,1024]{1,0:T(8,128)(2,1)}, u32[]{:S(2)}, u32[]{:S(2)}) collective-permute-start(bf16[2048,1024]{1,0:T(8,128)(2,1)} %param.9), channel_id=1, source_target_pairs={{0,8},{8,0},{1,9},{9,1},{2,10},{10,2},{3,11},{11,3},{4,12},{12,4},... | collective-permute-start | bytes 12582920 | tf_op jit(solution)/shard_map/ppermute | solution.py:235
  4.0 12.7 %collective-permute-start.1 = (bf16[384,1024]{1,0:T(8,128)(2,1)}, bf16[384,1024]{1,0:T(8,128)(2,1)S(1)}, u32[]{:S(2)}, u32[]{:S(2)}) collective-permute-start(bf16[384,1024]{1,0:T(8,128)(2,1)} %own_ref.1), channel_id=1, source_target_pairs={{0,8},{8,0},{1,9},{9,1},{2,10},{10,2},{3,11},{11,3},{4,12},{12,4},... | collective-permute-start | bytes 2359304 | tf_op jit(solution)/shard_map/ppermute | solution.py:235
  4.1 12.6 %collective-permute-start = (f32[3,1024]{1,0:T(4,128)}, f32[3,1024]{1,0:T(4,128)S(1)}, u32[]{:S(2)}, u32[]{:S(2)}) collective-permute-start(f32[3,1024]{1,0:T(4,128)} %param.8), channel_id=1, source_target_pairs={{0,8},{8,0},{1,9},{9,1},{2,10},{10,2},{3,11},{11,3},{4,12},{12,4},... | collective-permute-start | bytes 36872 | tf_op jit(solution)/shard_map/ppermute | solution.py:235
  16.7 1.1 %copy-start = (bf16[384,1024]{1,0:T(8,128)(2,1)S(1)}, bf16[384,1024]{1,0:T(8,128)(2,1)}, u32[]{:S(2)}) copy-start(bf16[384,1024]{1,0:T(8,128)(2,1)} %own_ref.1) | copy-start | bytes 2359300
  17.8 0.7 copy-start.2
  34.0 4.2 %collective-permute-start.3 = (f32[3,1152]{1,0:T(4,128)S(1)}, f32[3,1152]{1,0:T(4,128)S(1)}, u32[]{:S(2)}, u32[]{:S(2)}) collective-permute-start(f32[3,1152]{1,0:T(4,128)S(1)} %get-tuple-element.18.refs_0_), channel_id=1, source_target_pairs={{0,2},{1,3},{2,0},{3,1},{4,6},{5,7},{6,4},{7,5},{8,10},{9,11},{10,... | collective-permute-start | bytes 41480 | tf_op jit(solution)/shard_map/ppermute | solution.py:248
  37.0 2.6 %collective-permute-start.4 = (f32[3,1152]{1,0:T(4,128)S(1)}, f32[3,1152]{1,0:T(4,128)S(1)}, u32[]{:S(2)}, u32[]{:S(2)}) collective-permute-start(f32[3,1152]{1,0:T(4,128)S(1)} %get-tuple-element.18.refs_0_), channel_id=1, source_target_pairs={{0,1},{1,0},{2,3},{3,2},{4,5},{5,4},{6,7},{7,6},{8,9},{9,8},{10,11... | collective-permute-start | bytes 41480 | tf_op jit(solution)/shard_map/ppermute | solution.py:248
  37.4 3.8 %collective-permute-start.5 = (f32[3,1152]{1,0:T(4,128)S(1)}, f32[3,1152]{1,0:T(4,128)S(1)}, u32[]{:S(2)}, u32[]{:S(2)}) collective-permute-start(f32[3,1152]{1,0:T(4,128)S(1)} %get-tuple-element.18.refs_0_), channel_id=1, source_target_pairs={{0,3},{1,2},{2,1},{3,0},{4,7},{5,6},{6,5},{7,4},{8,11},{9,10},{10,... | collective-permute-start | bytes 41480 | tf_op jit(solution)/shard_map/ppermute | solution.py:248
  41.2 6.6 %collective-permute-start.6 = (f32[3,1152]{1,0:T(4,128)S(1)}, f32[3,1152]{1,0:T(4,128)S(1)}, u32[]{:S(2)}, u32[]{:S(2)}) collective-permute-start(f32[3,1152]{1,0:T(4,128)S(1)} %shard_map.87.msg_ref), channel_id=1, source_target_pairs={{0,4},{4,0},{1,5},{5,1},{2,6},{6,2},{3,7},{7,3},{8,12},{12,8},{9,1... | collective-permute-start | bytes 41480 | tf_op jit(solution)/shard_map/ppermute | solution.py:235
  47.8 7.5 %collective-permute-start.7 = (f32[3,1536]{1,0:T(4,128)S(1)}, f32[3,1536]{1,0:T(4,128)S(1)}, u32[]{:S(2)}, u32[]{:S(2)}) collective-permute-start(f32[3,1536]{1,0:T(4,128)S(1)} %shard_map.88.part_ref), channel_id=1, source_target_pairs={{0,8},{8,0},{1,9},{9,1},{2,10},{10,2},{3,11},{11,3},{4,12},{12,4},... | collective-permute-start | bytes 55304 | tf_op jit(solution)/shard_map/ppermute | solution.py:235
  57.2 8.8 %collective-permute-start.10 = (bf16[128,1024]{1,0:T(8,128)(2,1)S(1)}, bf16[128,1024]{1,0:T(8,128)(2,1)S(1)}, u32[]{:S(2)}, u32[]{:S(2)}) collective-permute-start(bf16[128,1024]{1,0:T(8,128)(2,1)S(1)} %get-tuple-element.28), channel_id=1, source_target_pairs={{0,64},{64,128},{128,192},{192,0},{1,65},{65,129},{129,193},{193,1... | collective-permute-start | bytes 786440 | tf_op jit(solution)/shard_map/ppermute | solution.py:235
  57.2 8.8 %collective-permute-start.11 = (bf16[128,1024]{1,0:T(8,128)(2,1)S(1)}, bf16[128,1024]{1,0:T(8,128)(2,1)S(1)}, u32[]{:S(2)}, u32[]{:S(2)}) collective-permute-start(bf16[128,1024]{1,0:T(8,128)(2,1)S(1)} %get-tuple-element.29), channel_id=1, source_target_pairs={{0,192},{64,0},{128,64},{192,128},{1,193},{65,1},{129,65},{193,129... | collective-permute-start | bytes 786440 | tf_op jit(solution)/shard_map/ppermute | solution.py:235
  62.5 8.0 %collective-permute-start.8 = (bf16[128,1024]{1,0:T(8,128)(2,1)S(1)}, bf16[128,1024]{1,0:T(8,128)(2,1)S(1)}, u32[]{:S(2)}, u32[]{:S(2)}) collective-permute-start(bf16[128,1024]{1,0:T(8,128)(2,1)S(1)} %get-tuple-element.24), channel_id=1, source_target_pairs={{0,192},{64,0},{128,64},{192,128},{1,193},{65,1},{129,65},{193,129... | collective-permute-start | bytes 786440 | tf_op jit(solution)/shard_map/ppermute | solution.py:235
  62.6 8.5 %collective-permute-start.9 = (bf16[128,1024]{1,0:T(8,128)(2,1)S(1)}, bf16[128,1024]{1,0:T(8,128)(2,1)S(1)}, u32[]{:S(2)}, u32[]{:S(2)}) collective-permute-start(bf16[128,1024]{1,0:T(8,128)(2,1)S(1)} %get-tuple-element.25), channel_id=1, source_target_pairs={{0,64},{64,128},{128,192},{192,0},{1,65},{65,129},{129,193},{193,1... | collective-permute-start | bytes 786440 | tf_op jit(solution)/shard_map/ppermute | solution.py:235
  66.1 10.7 %collective-permute-start.13 = (bf16[128,1024]{1,0:T(8,128)(2,1)S(1)}, bf16[128,1024]{1,0:T(8,128)(2,1)S(1)}, u32[]{:S(2)}, u32[]{:S(2)}) collective-permute-start(bf16[128,1024]{1,0:T(8,128)(2,1)S(1)} %add_convert_fusion.1), channel_id=1, source_target_pairs={{0,64},{64,128},{128,192},{192,0},{1,65},{65,129},{129,193},{193,1... | collective-permute-start | bytes 786440 | tf_op jit(solution)/shard_map/ppermute | solution.py:235
  66.2 14.4 %collective-permute-start.12 = (bf16[128,1024]{1,0:T(8,128)(2,1)S(1)}, bf16[128,1024]{1,0:T(8,128)(2,1)S(1)}, u32[]{:S(2)}, u32[]{:S(2)}) collective-permute-start(bf16[128,1024]{1,0:T(8,128)(2,1)S(1)} %add_convert_fusion.2), channel_id=1, source_target_pairs={{0,192},{64,0},{128,64},{192,128},{1,193},{65,1},{129,65},{193,129... | collective-permute-start | bytes 786440 | tf_op jit(solution)/shard_map/ppermute | solution.py:235
  76.8 6.3 %collective-permute-start.14 = (bf16[64,1024]{1,0:T(8,128)(2,1)S(1)}, bf16[64,1024]{1,0:T(8,128)(2,1)S(1)}, u32[]{:S(2)}, u32[]{:S(2)}) collective-permute-start(bf16[64,1024]{1,0:T(8,128)(2,1)S(1)} %get-tuple-element.34), channel_id=1, source_target_pairs={{0,32},{16,48},{32,0},{48,16},{1,33},{17,49},{33,1},{49,17},{2,34}... | collective-permute-start | bytes 393224 | tf_op jit(solution)/shard_map/ppermute | solution.py:235
  77.5 5.8 %collective-permute-start.15 = (bf16[64,1024]{1,0:T(8,128)(2,1)S(1)}, bf16[64,1024]{1,0:T(8,128)(2,1)S(1)}, u32[]{:S(2)}, u32[]{:S(2)}) collective-permute-start(bf16[64,1024]{1,0:T(8,128)(2,1)S(1)} %get-tuple-element.35), channel_id=1, source_target_pairs={{0,48},{16,0},{32,16},{48,32},{1,49},{17,1},{33,17},{49,33},{2,50}... | collective-permute-start | bytes 393224 | tf_op jit(solution)/shard_map/ppermute | solution.py:235
  80.7 7.2 %collective-permute-start.16 = (bf16[64,1024]{1,0:T(8,128)(2,1)S(1)}, bf16[64,1024]{1,0:T(8,128)(2,1)S(1)}, u32[]{:S(2)}, u32[]{:S(2)}) collective-permute-start(bf16[64,1024]{1,0:T(8,128)(2,1)S(1)} %slice.31), channel_id=1, source_target_pairs={{0,16},{16,32},{32,48},{48,0},{1,17},{17,33},{33,49},{49,1},{2,18}... | collective-permute-start | bytes 393224 | tf_op jit(solution)/shard_map/ppermute | solution.py:235

commit v4 on v3

--- a/solution.py
+++ b/solution.py
@@ -32,8 +32,8 @@
 
 
 def score_kernel(
-    inv, nx, nz, x_ref, z_ref, off_ref, ids_ref, pos_ref, gain_ref, own_ref, other_ref, table_hbm,
-    e_ref, q_ref, m_ref, msg_ref, table_ref, emb_ref, pos_emb_ref, sem,
+    inv, nx, nz, x_ref, z_ref, core_ref, off_ref, ids_ref, pos_ref, pos_other_ref, gain_ref, own_ref, other_ref, table_hbm,
+    e_ref, q_ref, m_ref, msg_ref, emb_ref, pos_emb_ref, near_ref, table_ref, sem,
 ):
     heads = gain_ref.shape[0]
     rows = own_ref.shape[0]
@@ -56,10 +56,25 @@
             pair.append(ids_ref[pl.ds(row, 1), :] - off)
         hot = one_hot_rows(jnp.concatenate(pair, axis=1), width)
         emb_ref[b * nd : (b + 2) * nd, :] = jnp.dot(hot, table_ref[...], preferred_element_type=F32).astype(BF16)
-    pos_ids = [pos_ref[a : a + 128].reshape(1, 128) - off for a in range(0, rows, 128)]
-    for i, ids in enumerate(pos_ids):
-        hot = one_hot_rows(ids, width)
-        pos_emb_ref[i * 128 : i * 128 + 128, :] = jnp.dot(hot, table_ref[...], preferred_element_type=F32).astype(BF16)
+    one = core_ref[0] == 1
+    near_ref[...] = jnp.zeros_like(near_ref)
+    pos_ids = [r[a : a + 128].reshape(1, 128) - off for r in (pos_ref, pos_other_ref) for a in range(0, rows, 128)]
+
+    @pl.when(one)
+    def _():
+        for i, ids in enumerate(pos_ids):
+            part = slice(i * 128, i * 128 + 128)
+            hot = one_hot_rows(ids, width)
+            pos_emb_ref[part, :] = jnp.dot(hot, table_ref[...], preferred_element_type=F32).astype(BF16)
+        diag = lax.broadcasted_iota(jnp.int32, (128, 128), 0) == lax.broadcasted_iota(jnp.int32, (128, 128), 1)
+        for i in range(len(pos_ids)):
+            part = slice(i * 128, i * 128 + 128)
+            q = q_ref[:, part, :].reshape(heads * 128, -1)
+            d = lax.dot_general(pos_emb_ref[part, :], q, NT, preferred_element_type=F32)
+            for head in range(heads):
+                mine = jnp.where(diag, d[:, head * 128 : head * 128 + 128], 0.0)
+                near_ref[head : head + 1, part] = jnp.sum(mine, axis=0, keepdims=True) * inv
+
     block = 256
     for head in range(heads):
         for a in range(0, 2 * rows, block):
@@ -70,20 +85,15 @@
             e_ref[:, at : at + block] = e
             m_ref[head : head + 1, a : a + block] = m * inv
             msg_ref[head : head + 1, a : a + block] = m * inv + jnp.log(jnp.sum(e, axis=0, keepdims=True))
-        for i, ids in enumerate(pos_ids):
-            a = i * 128
-            d = lax.dot_general(
-                pos_emb_ref[a : a + 128, :], q_ref[head, a : a + 128, :], NT, preferred_element_type=F32
-            )
-            diag = lax.broadcasted_iota(jnp.int32, d.shape, 0) == lax.broadcasted_iota(jnp.int32, d.shape, 1)
-            pos = jnp.sum(jnp.where(diag, d, 0.0), axis=0, keepdims=True) * inv
-            owned = (ids >= 0) & (ids < width)
-            base = msg_ref[head : head + 1, a : a + 128]
-            msg_ref[head : head + 1, a : a + 128] = jnp.where(owned, pair_sum(base, pos), base)
-            msg_ref[head : head + 1, 2 * rows + a : 2 * rows + a + 128] = pos
-
-
-def scores(inv, nx, nz, x, z, off, ids, pos, gain, own, other, table):
+    for i, ids in enumerate(pos_ids):
+        part = slice(i * 128, i * 128 + 128)
+        base, pos = msg_ref[:, part], near_ref[:, part]
+        owned = (ids >= 0) & (ids < width) & one
+        msg_ref[:, part] = jnp.where(owned, pair_sum(base, pos), base)
+    msg_ref[:, 2 * rows :] = near_ref[...]
+
+
+def scores(inv, nx, nz, x, z, core, off, ids, pos, pos_other, gain, own, other, table):
     rows, width = own.shape
     heads = gain.shape[0]
     negs = ids.size
@@ -91,28 +101,29 @@
     return pl.pallas_call(
         functools.partial(score_kernel, inv, nx, nz),
         grid=(1,),
-        in_specs=[sm, sm, sm, full(*ids.shape), full(*pos.shape), full(*gain.shape),
+        in_specs=[sm, sm, sm, sm, full(*ids.shape), full(*pos.shape), full(*pos.shape), full(*gain.shape),
             full(rows, width), full(rows, width), pl.BlockSpec(memory_space=pl.ANY)],
         out_specs=[
             full(negs, heads * 2 * rows),
             full(heads, 2 * rows, width),
             full(heads, 2 * rows),
-            full(heads, 3 * rows),
+            full(heads, 4 * rows),
         ],
         out_shape=[
             jax.ShapeDtypeStruct((negs, heads * 2 * rows), F32),
             jax.ShapeDtypeStruct((heads, 2 * rows, width), BF16),
             jax.ShapeDtypeStruct((heads, 2 * rows), F32),
-            jax.ShapeDtypeStruct((heads, 3 * rows), F32),
+            jax.ShapeDtypeStruct((heads, 4 * rows), F32),
         ],
         scratch_shapes=[
+            pltpu.VMEM((negs, width), BF16),
+            pltpu.VMEM((2 * rows, width), BF16),
+            pltpu.VMEM((heads, 2 * rows), F32),
             pltpu.VMEM(table.shape, BF16),
-            pltpu.VMEM((negs, width), BF16),
-            pltpu.VMEM((rows, width), BF16),
             pltpu.SemaphoreType.DMA,
         ],
         compiler_params=pltpu.CompilerParams(vmem_limit_bytes=30 * 2**20),
-    )(x, z, off, ids, pos, gain, own, other, table)
+    )(x, z, core, off, ids, pos, pos_other, gain, own, other, table)
 
 
 def pair_sum(a, b):
@@ -122,7 +133,7 @@
 
 def fold_kernel(*refs):
     parts, out_ref = [r[...] for r in refs[:-1]], refs[-1]
-    cut = out_ref.shape[1] // 3 * 2
+    cut = out_ref.shape[1] // 2
     top = functools.reduce(jnp.maximum, [r[:, :cut] for r in parts])
     out_ref[:, :cut] = top + jnp.log(sum(jnp.exp(r[:, :cut] - top) for r in parts))
     out_ref[:, cut:] = sum(r[:, cut:] for r in parts)
@@ -144,9 +155,9 @@
     rows = mask_ref.shape[1]
     a, b = msg_ref[...], near_ref[...]
     out_ref[:, : 2 * rows] = pair_sum(a[:, : 2 * rows], b[:, : 2 * rows])
-    out_ref[:, 2 * rows : 3 * rows] = a[:, 2 * rows :] + b[:, 2 * rows :]
+    out_ref[:, 2 * rows : 4 * rows] = a[:, 2 * rows :] + b[:, 2 * rows :]
     valid = lax.broadcasted_iota(jnp.int32, mask_ref.shape, 1) < len_ref[0]
-    out_ref[:, 3 * rows :] = jnp.where(valid, mask_ref[...].astype(F32), 0.0)
+    out_ref[:, 4 * rows :] = jnp.where(valid, mask_ref[...].astype(F32), 0.0)
 
 
 def fold_with_mask(seq_len, mask, msg, near):
@@ -155,20 +166,20 @@
         mask_kernel,
         grid=(1,),
         in_specs=[pl.BlockSpec(memory_space=pltpu.SMEM), full(*mask.shape), full(*msg.shape), full(*msg.shape)],
-        out_specs=full(heads, 4 * rows),
-        out_shape=jax.ShapeDtypeStruct((heads, 4 * rows), F32),
+        out_specs=full(heads, 5 * rows),
+        out_shape=jax.ShapeDtypeStruct((heads, 5 * rows), F32),
         compiler_params=pltpu.CompilerParams(vmem_limit_bytes=2**20),
     )(seq_len, mask, msg, near)
 
 
 def weights(part_ref, cross_ref, m_ref, c_ref, loss_ref):
     rows = loss_ref.shape[1]
-    w = part_ref[:, 3 * rows :]
+    w = part_ref[:, 4 * rows :]
     lse = pair_sum(part_ref[:, :rows], cross_ref[:, rows : 2 * rows])
     lse_other = pair_sum(part_ref[:, rows : 2 * rows], cross_ref[:, :rows])
-    loss_ref[...] = w * (lse - part_ref[:, 2 * rows : 3 * rows])
+    loss_ref[...] = w * (lse - part_ref[:, 2 * rows : 3 * rows] - cross_ref[:, 3 * rows : 4 * rows])
     c_ref[:, :rows] = w * jnp.exp(m_ref[:, :rows] - lse)
-    c_ref[:, rows:] = cross_ref[:, 3 * rows :] * jnp.exp(m_ref[:, rows:] - lse_other)
+    c_ref[:, rows:] = cross_ref[:, 4 * rows :] * jnp.exp(m_ref[:, rows:] - lse_other)
 
 
 def products(c_ref, e_ref, q_ref, outs, p_ref):
@@ -228,7 +239,7 @@
     neg_dev = neg_ids.shape[0]
     n_dp = nx * nz * lax.axis_size("core")
     factor = neg_dev * n_dp * lax.axis_size("zh") * lax.axis_size("y") / math.sqrt(rows * n_dp)
-    x, z = lax.axis_index("x"), lax.axis_index("z")
+    x, z, core = lax.axis_index("x"), lax.axis_index("z"), lax.axis_index("core")
     offset = (lax.axis_index("zh") * lax.axis_size("y") + lax.axis_index("y")) * table_rows
 
     def shifted(value, axis, size, by):
@@ -237,12 +248,13 @@
     other = shifted(user_states, "core", 2, 1)
     table = shifted(item_table, "core", 2, 1)
     gain = shifted(head_gain, "core", 2, 1)
+    pos_other = shifted(pos_ids, "core", 2, 1)
 
     slot = lax.broadcasted_iota(jnp.int32, (nx * nz, neg_dev), 0)
     slots = lax.psum(jnp.where(slot == x * nz + z, neg_ids[None], 0), ("x", "z"))
 
     e, q, m, msg = scores(
-        1.0 / math.sqrt(width), nx, nz, x.reshape(1), z.reshape(1), offset.reshape(1), slots, pos_ids,
+        1.0 / math.sqrt(width), nx, nz, x.reshape(1), z.reshape(1), core.reshape(1), offset.reshape(1), slots, pos_ids, pos_other,
         gain, user_states, other, table,
     )
     msg = fold(msg, *[lax.ppermute(msg, "y", [(i, i ^ k) for i in range(4)]) for k in (2, 1, 3)])

time: 90.3 us -> 89.4 us (0.990)
  starting transfers between devices: 30.2 us -> 26.4 us
  Pallas kernels: 21.4 us -> 24.4 us
    ppermute x14 -> x15, starting transfers between devices: 26.4 us -> 22.6 us  [shifted(): lax.ppermute(value, axis, [(i, (i + by) % size) for i in range(size)])]
    pallas_call x1, Pallas kernels: 15.4 us -> 18.4 us  [scores(): pl.pallas_call(functools.partial(score_kernel, inv, nx, nz), grid=(1,), i...]
    ppermute x14 -> x15, waiting for transfers between devices: 17.2 us -> 16.6 us  [shifted(): lax.ppermute(value, axis, [(i, (i + by) % size) for i in range(size)])]
  transfers between devices with their start and end apart: 17 -> 18, of which waited for: 12 -> 11; matrix products, arithmetic and copies ran while one was open for 1% -> 1% of each run, Pallas kernels for 5% -> 5%
where the time goes in v4:
time: 89.4 us; the launch traced here: 87.8 us
  starting transfers between devices  26.4 us (30%)
  Pallas kernels  24.4 us (27%)
  waiting for transfers between devices  20.5 us (23%)
  blocking collectives  11.5 us (13%)
  local copies, waits for them, and re-layouts  1.85 us (2%)
  other arithmetic  1.72 us (2%)
  between operations  1.43 us (2%)
    ppermute x15, starting transfers between devices, shifted(): lax.ppermute(value, axis, [(i, (i + by) % size) for i in range(size)])  22.6 us
    pallas_call x1, Pallas kernels, scores(): pl.pallas_call(functools.partial(score_kernel, inv, nx, nz), grid=(1,), i...  18.4 us
    ppermute x15, waiting for transfers between devices, shifted(): lax.ppermute(value, axis, [(i, (i + by) % size) for i in range(size)])  16.6 us
    psum x1, blocking collectives, shards(): lax.psum(jnp.where(slot == x * nz + z, neg_ids[None], 0), ('x', 'z'))  11.5 us
    pallas_call x3, Pallas kernels, grad(): pl.pallas_call(body, grid=(1,), in_specs=[full(*s.shape) for s in small]...  5.95 us
    ppermute x3, waiting for transfers between devices, shards(): lax.ppermute(msg, 'y', [(i, i ^ k) for i in range(4)])  3.93 us
    ppermute x3, starting transfers between devices, shards(): lax.ppermute(msg, 'y', [(i, i ^ k) for i in range(4)])  3.78 us
    unnamed x6, local copies, waits for them, and re-layouts  1.81 us
  transfers between devices with their start and end apart: 18, of which 11 were waited for; matrix products, arithmetic and copies ran while one was open for 1% of the time, Pallas kernels for 5%

profile of v4, /device:TPU:1, one launch (start us, length us, event | category | flops | bytes accessed | tf_op | source)
XLA Modules:
  0.0 87.8 jit_solution(13691325882659487728)
XLA Ops:
  0.6 3.3 %collective-permute-start.3 = (bf16[2048,1024]{1,0:T(8,128)(2,1)}, bf16[2048,1024]{1,0:T(8,128)(2,1)}, u32[]{:S(2)}, u32[]{:S(2)}) collective-permute-start(bf16[2048,1024]{1,0:T(8,128)(2,1)} %param.9), channel_id=1, source_target_pairs={{0,8},{8,0},{1,9},{9,1},{2,10},{10,2},{3,11},{11,3},{4,12},{12,4},... | collective-permute-start | bytes 12582920 | tf_op jit(solution)/shard_map/ppermute | solution.py:246
  4.0 0.1 collective-permute-start.2
  4.1 0.4 collective-permute-start.1
  4.6 0.7 broadcast_select_fusion
  5.3 11.5 %psum.7.ids_ref = s32[16,64]{1,0:T(8,128)S(1)} all-reduce(s32[16,64]{1,0:T(8,128)S(1)} %broadcast_select_fusion), channel_id=1, replica_groups=mesh['x'=4,'z'=4,'core'=2,'zh'=2,'y'=4] {'x','z'}, use_global_device_ids=true, to_apply=%region_0.1 | all-reduce | flops 1024 | bytes 8192 | tf_op jit(solution)/shard_map/psum | solution.py:254
  16.8 1.1 %copy-done = bf16[384,1024]{1,0:T(8,128)(2,1)S(1)} copy-done((bf16[384,1024]{1,0:T(8,128)(2,1)S(1)}, bf16[384,1024]{1,0:T(8,128)(2,1)}, u32[]{:S(2)}) %copy-start) | copy-done | bytes 786456
  17.9 0.7 copy-done.2
  18.6 18.4 %shard_map.86 = (f32[1024,2304]{1,0:T(8,128)S(1)}, bf16[3,768,1024]{2,1,0:T(8,128)(2,1)S(1)}, f32[3,768]{1,0:T(4,128)S(1)}, f32[3,1536]{1,0:T(4,128)S(1)}) custom-call(s32[1]{0:T(128)} %bitcast.x_ref, s32[1]{0:T(128)} %bitcast.1.z_ref, s32[1]{0:T(128)} %bitcast.2.core_ref, s32[1]{0:T(128)} %bitcast.3.off_ref, s32[16,64]{1,0:T(8,128)S(1)} %psum.7.ids_ref, ...), custom_call_target="tpu_custom_call" | custom-call | tf_op jit(solution)/shard_map/pallas_call | solution.py:101
  37.1 3.0 %collective-permute-start.4 = (f32[3,1536]{1,0:T(4,128)S(1)}, f32[3,1536]{1,0:T(4,128)S(1)}, u32[]{:S(2)}, u32[]{:S(2)}) collective-permute-start(f32[3,1536]{1,0:T(4,128)S(1)} %get-tuple-element.18.refs_0_), channel_id=1, source_target_pairs={{0,2},{1,3},{2,0},{3,1},{4,6},{5,7},{6,4},{7,5},{8,10},{9,11},{10,... | collective-permute-start | bytes 55304 | tf_op jit(solution)/shard_map/ppermute | solution.py:260
  40.1 0.4 collective-permute-start.5
  40.5 0.4 collective-permute-start.6
  40.9 0.5 collective-permute-done.4.refs_1_
  41.3 1.7 %collective-permute-done.5.refs_2_ = f32[3,1536]{1,0:T(4,128)S(1)} collective-permute-done((f32[3,1536]{1,0:T(4,128)S(1)}, f32[3,1536]{1,0:T(4,128)S(1)}, u32[]{:S(2)}, u32[]{:S(2)}) %collective-permute-start.5) | collective-permute-done | bytes 18464 | tf_op jit(solution)/shard_map/ppermute | solution.py:260
  43.0 1.8 %collective-permute-done.6.refs_3_ = f32[3,1536]{1,0:T(4,128)S(1)} collective-permute-done((f32[3,1536]{1,0:T(4,128)S(1)}, f32[3,1536]{1,0:T(4,128)S(1)}, u32[]{:S(2)}, u32[]{:S(2)}) %collective-permute-start.6) | collective-permute-done | bytes 18464 | tf_op jit(solution)/shard_map/ppermute | solution.py:260
  44.8 4.6 %collective-permute-start.7 = (f32[3,1536]{1,0:T(4,128)S(1)}, f32[3,1536]{1,0:T(4,128)S(1)}, u32[]{:S(2)}, u32[]{:S(2)}) collective-permute-start(f32[3,1536]{1,0:T(4,128)S(1)} %shard_map.87.msg_ref), channel_id=1, source_target_pairs={{0,4},{4,0},{1,5},{5,1},{2,6},{6,2},{3,7},{7,3},{8,12},{12,8},{9,1... | collective-permute-start | bytes 55304 | tf_op jit(solution)/shard_map/ppermute | solution.py:246
  50.1 1.4 %collective-permute-done.7.near_ref = f32[3,1536]{1,0:T(4,128)S(1)} collective-permute-done((f32[3,1536]{1,0:T(4,128)S(1)}, f32[3,1536]{1,0:T(4,128)S(1)}, u32[]{:S(2)}, u32[]{:S(2)}) %collective-permute-start.7) | collective-permute-done | bytes 18464 | tf_op jit(solution)/shard_map/ppermute | solution.py:246
  51.5 2.0 %collective-permute-start.8 = (f32[3,1920]{1,0:T(4,128)S(1)}, f32[3,1920]{1,0:T(4,128)S(1)}, u32[]{:S(2)}, u32[]{:S(2)}) collective-permute-start(f32[3,1920]{1,0:T(4,128)S(1)} %shard_map.88.part_ref), channel_id=1, source_target_pairs={{0,8},{8,0},{1,9},{9,1},{2,10},{10,2},{3,11},{11,3},{4,12},{12,4},... | collective-permute-start | bytes 69128 | tf_op jit(solution)/shard_map/ppermute | solution.py:246
  53.5 0.9 collective-permute-done.8.cross_ref
  54.4 1.9 %shard_map.89 = (f32[3,768]{1,0:T(4,128)S(1)}, f32[3,384]{1,0:T(4,128)}, bf16[128,1024]{1,0:T(8,128)(2,1)S(1)}, bf16[128,1024]{1,0:T(8,128)(2,1)S(1)}) custom-call(f32[3,1920]{1,0:T(4,128)S(1)} %shard_map.88.part_ref, f32[3,1920]{1,0:T(4,128)S(1)} %collective-permute-done.8.cross_ref, f32[3,768]{1,0:T(4,128)S(1)} %get-tuple-element.19.m_ref, ...), custom_call_target="tpu_custom_call" | custom-call | flops 1207959552 | bytes 7077888 | tf_op jit(solution)/shard_map/pallas_call | solution.py:218
  56.3 2.7 %collective-permute-start.12 = (bf16[128,1024]{1,0:T(8,128)(2,1)S(1)}, bf16[128,1024]{1,0:T(8,128)(2,1)S(1)}, u32[]{:S(2)}, u32[]{:S(2)}) collective-permute-start(bf16[128,1024]{1,0:T(8,128)(2,1)S(1)} %get-tuple-element.29), channel_id=1, source_target_pairs={{0,192},{64,0},{128,64},{192,128},{1,193},{65,1},{129,65},{193,129... | collective-permute-start | bytes 786440 | tf_op jit(solution)/shard_map/ppermute | solution.py:246
  58.9 2.6 %shard_map.90 = (f32[128,1024]{1,0:T(8,128)S(1)}, bf16[128,1024]{1,0:T(8,128)(2,1)S(1)}, bf16[128,1024]{1,0:T(8,128)(2,1)S(1)}, f32[128,1024]{1,0:T(8,128)S(1)}) custom-call(f32[3,768]{1,0:T(4,128)S(1)} %get-tuple-element.23.c_ref, f32[1024,2304]{1,0:T(8,128)S(1)} %get-tuple-element.20.e_ref, bf16[3,768,1024]{2,1,0:T(8,128)(2,1)S(1)} %get-tuple-element.21.q_ref), custom_call_target="tpu_custom_call" | custom-call | flops 2415919104 | bytes 9437184 | tf_op jit(solution)/shard_map/pallas_call | solution.py:218
  61.7 2.7 %collective-permute-start.9 = (bf16[128,1024]{1,0:T(8,128)(2,1)S(1)}, bf16[128,1024]{1,0:T(8,128)(2,1)S(1)}, u32[]{:S(2)}, u32[]{:S(2)}) collective-permute-start(bf16[128,1024]{1,0:T(8,128)(2,1)S(1)} %get-tuple-element.24), channel_id=1, source_target_pairs={{0,192},{64,0},{128,64},{192,128},{1,193},{65,1},{129,65},{193,129... | collective-permute-start | bytes 786440 | tf_op jit(solution)/shard_map/ppermute | solution.py:246
  64.3 0.7 collective-permute-done.11
  65.2 2.7 %collective-permute-start.13 = (bf16[128,1024]{1,0:T(8,128)(2,1)S(1)}, bf16[128,1024]{1,0:T(8,128)(2,1)S(1)}, u32[]{:S(2)}, u32[]{:S(2)}) collective-permute-start(bf16[128,1024]{1,0:T(8,128)(2,1)S(1)} %add_convert_fusion.2), channel_id=1, source_target_pairs={{0,192},{64,0},{128,64},{192,128},{1,193},{65,1},{129,65},{193,129... | collective-permute-start | bytes 786440 | tf_op jit(solution)/shard_map/ppermute | solution.py:246
  68.0 2.2 %collective-permute-done.10.in_b_ref = bf16[128,1024]{1,0:T(8,128)(2,1)S(1)} collective-permute-done((bf16[128,1024]{1,0:T(8,128)(2,1)S(1)}, bf16[128,1024]{1,0:T(8,128)(2,1)S(1)}, u32[]{:S(2)}, u32[]{:S(2)}) %collective-permute-start.10) | collective-permute-done | bytes 262176 | tf_op jit(solution)/shard_map/ppermute | solution.py:246
  70.2 1.4 %shard_map.91 = (f32[128,1024]{1,0:T(8,128)S(1)}, f32[128,1024]{1,0:T(8,128)S(1)}) custom-call(f32[3,768]{1,0:T(4,128)S(1)} %get-tuple-element.23.c_ref, bf16[128,1024]{1,0:T(8,128)(2,1)S(1)} %collective-permute-done.9.in_a_ref, bf16[128,1024]{1,0:T(8,128)(2,1)S(1)} %collective-permute-done.10.in_b_ref, f32[1024,2304]{1,0:T(8,128)S(1)} %get-tuple-element.20.e_ref, ...), custom_call_target="tpu_custom_call" | custom-call | flops 1207959552 | bytes 7077888 | tf_op jit(solution)/shard_map/pallas_call | solution.py:218
  71.6 4.2 %collective-permute-done.14 = bf16[128,1024]{1,0:T(8,128)(2,1)S(1)} collective-permute-done((bf16[128,1024]{1,0:T(8,128)(2,1)S(1)}, bf16[128,1024]{1,0:T(8,128)(2,1)S(1)}, u32[]{:S(2)}, u32[]{:S(2)}) %collective-permute-start.14) | collective-permute-done | bytes 262176 | tf_op jit(solution)/shard_map/ppermute | solution.py:246
  75.9 0.6 collective-permute-start.15
  76.6 3.1 %collective-permute-start.16 = (bf16[64,1024]{1,0:T(8,128)(2,1)S(1)}, bf16[64,1024]{1,0:T(8,128)(2,1)S(1)}, u32[]{:S(2)}, u32[]{:S(2)}) collective-permute-start(bf16[64,1024]{1,0:T(8,128)(2,1)S(1)} %get-tuple-element.35), channel_id=1, source_target_pairs={{0,48},{16,0},{32,16},{48,32},{1,49},{17,1},{33,17},{49,33},{2,50}... | collective-permute-start | bytes 393224 | tf_op jit(solution)/shard_map/ppermute | solution.py:246
  79.8 2.4 %collective-permute-done.15 = bf16[64,1024]{1,0:T(8,128)(2,1)S(1)} collective-permute-done((bf16[64,1024]{1,0:T(8,128)(2,1)S(1)}, bf16[64,1024]{1,0:T(8,128)(2,1)S(1)}, u32[]{:S(2)}, u32[]{:S(2)}) %collective-permute-start.15) | collective-permute-done | bytes 131104 | tf_op jit(solution)/shard_map/ppermute | solution.py:246
  82.4 4.7 %collective-permute-done.17 = bf16[64,1024]{1,0:T(8,128)(2,1)S(1)} collective-permute-done((bf16[64,1024]{1,0:T(8,128)(2,1)S(1)}, bf16[64,1024]{1,0:T(8,128)(2,1)S(1)}, u32[]{:S(2)}, u32[]{:S(2)}) %collective-permute-start.17) | collective-permute-done | bytes 131104 | tf_op jit(solution)/shard_map/ppermute | solution.py:246
  87.0 0.8 fusion.2
  (26 shorter events, 0.8 us)
Async XLA Ops:
  0.6 50.9 %copy-start.1 = (s32[3,384]{1,0:T(4,128)S(1)}, s32[3,384]{1,0:T(4,128)}, u32[]{:S(2)}) copy-start(s32[3,384]{1,0:T(4,128)} %mask_ref.1) | copy-start | bytes 13828
  0.6 16.2 %collective-permute-start.3 = (bf16[2048,1024]{1,0:T(8,128)(2,1)}, bf16[2048,1024]{1,0:T(8,128)(2,1)}, u32[]{:S(2)}, u32[]{:S(2)}) collective-permute-start(bf16[2048,1024]{1,0:T(8,128)(2,1)} %param.9), channel_id=1, source_target_pairs={{0,8},{8,0},{1,9},{9,1},{2,10},{10,2},{3,11},{11,3},{4,12},{12,4},... | collective-permute-start | bytes 12582920 | tf_op jit(solution)/shard_map/ppermute | solution.py:246
  4.0 12.8 %collective-permute-start.2 = (bf16[384,1024]{1,0:T(8,128)(2,1)}, bf16[384,1024]{1,0:T(8,128)(2,1)S(1)}, u32[]{:S(2)}, u32[]{:S(2)}) collective-permute-start(bf16[384,1024]{1,0:T(8,128)(2,1)} %own_ref.1), channel_id=1, source_target_pairs={{0,8},{8,0},{1,9},{9,1},{2,10},{10,2},{3,11},{11,3},{4,12},{12,4},... | collective-permute-start | bytes 2359304 | tf_op jit(solution)/shard_map/ppermute | solution.py:246
  4.1 12.7 %collective-permute-start.1 = (f32[3,1024]{1,0:T(4,128)}, f32[3,1024]{1,0:T(4,128)S(1)}, u32[]{:S(2)}, u32[]{:S(2)}) collective-permute-start(f32[3,1024]{1,0:T(4,128)} %param.8), channel_id=1, source_target_pairs={{0,8},{8,0},{1,9},{9,1},{2,10},{10,2},{3,11},{11,3},{4,12},{12,4},... | collective-permute-start | bytes 36872 | tf_op jit(solution)/shard_map/ppermute | solution.py:246
  4.5 12.3 %collective-permute-start = (s32[384]{0:T(512)}, s32[384]{0:T(512)S(1)}, u32[]{:S(2)}, u32[]{:S(2)}) collective-permute-start(s32[384]{0:T(512)} %pos_ref.1), channel_id=1, source_target_pairs={{0,8},{8,0},{1,9},{9,1},{2,10},{10,2},{3,11},{11,3},{4,12},{12,4},... | collective-permute-start | bytes 4616 | tf_op jit(solution)/shard_map/ppermute | solution.py:246
  16.8 1.1 %copy-start = (bf16[384,1024]{1,0:T(8,128)(2,1)S(1)}, bf16[384,1024]{1,0:T(8,128)(2,1)}, u32[]{:S(2)}) copy-start(bf16[384,1024]{1,0:T(8,128)(2,1)} %own_ref.1) | copy-start | bytes 2359300
  17.9 0.7 copy-start.2
  37.1 4.3 %collective-permute-start.4 = (f32[3,1536]{1,0:T(4,128)S(1)}, f32[3,1536]{1,0:T(4,128)S(1)}, u32[]{:S(2)}, u32[]{:S(2)}) collective-permute-start(f32[3,1536]{1,0:T(4,128)S(1)} %get-tuple-element.18.refs_0_), channel_id=1, source_target_pairs={{0,2},{1,3},{2,0},{3,1},{4,6},{5,7},{6,4},{7,5},{8,10},{9,11},{10,... | collective-permute-start | bytes 55304 | tf_op jit(solution)/shard_map/ppermute | solution.py:260
  40.1 2.9 %collective-permute-start.5 = (f32[3,1536]{1,0:T(4,128)S(1)}, f32[3,1536]{1,0:T(4,128)S(1)}, u32[]{:S(2)}, u32[]{:S(2)}) collective-permute-start(f32[3,1536]{1,0:T(4,128)S(1)} %get-tuple-element.18.refs_0_), channel_id=1, source_target_pairs={{0,1},{1,0},{2,3},{3,2},{4,5},{5,4},{6,7},{7,6},{8,9},{9,8},{10,11... | collective-permute-start | bytes 55304 | tf_op jit(solution)/shard_map/ppermute | solution.py:260
  40.5 4.3 %collective-permute-start.6 = (f32[3,1536]{1,0:T(4,128)S(1)}, f32[3,1536]{1,0:T(4,128)S(1)}, u32[]{:S(2)}, u32[]{:S(2)}) collective-permute-start(f32[3,1536]{1,0:T(4,128)S(1)} %get-tuple-element.18.refs_0_), channel_id=1, source_target_pairs={{0,3},{1,2},{2,1},{3,0},{4,7},{5,6},{6,5},{7,4},{8,11},{9,10},{10,... | collective-permute-start | bytes 55304 | tf_op jit(solution)/shard_map/ppermute | solution.py:260
  44.8 6.7 %collective-permute-start.7 = (f32[3,1536]{1,0:T(4,128)S(1)}, f32[3,1536]{1,0:T(4,128)S(1)}, u32[]{:S(2)}, u32[]{:S(2)}) collective-permute-start(f32[3,1536]{1,0:T(4,128)S(1)} %shard_map.87.msg_ref), channel_id=1, source_target_pairs={{0,4},{4,0},{1,5},{5,1},{2,6},{6,2},{3,7},{7,3},{8,12},{12,8},{9,1... | collective-permute-start | bytes 55304 | tf_op jit(solution)/shard_map/ppermute | solution.py:246
  51.5 2.8 %collective-permute-start.8 = (f32[3,1920]{1,0:T(4,128)S(1)}, f32[3,1920]{1,0:T(4,128)S(1)}, u32[]{:S(2)}, u32[]{:S(2)}) collective-permute-start(f32[3,1920]{1,0:T(4,128)S(1)} %shard_map.88.part_ref), channel_id=1, source_target_pairs={{0,8},{8,0},{1,9},{9,1},{2,10},{10,2},{3,11},{11,3},{4,12},{12,4},... | collective-permute-start | bytes 69128 | tf_op jit(solution)/shard_map/ppermute | solution.py:246
  56.3 8.8 %collective-permute-start.11 = (bf16[128,1024]{1,0:T(8,128)(2,1)S(1)}, bf16[128,1024]{1,0:T(8,128)(2,1)S(1)}, u32[]{:S(2)}, u32[]{:S(2)}) collective-permute-start(bf16[128,1024]{1,0:T(8,128)(2,1)S(1)} %get-tuple-element.28), channel_id=1, source_target_pairs={{0,64},{64,128},{128,192},{192,0},{1,65},{65,129},{129,193},{193,1... | collective-permute-start | bytes 786440 | tf_op jit(solution)/shard_map/ppermute | solution.py:246
  56.3 8.8 %collective-permute-start.12 = (bf16[128,1024]{1,0:T(8,128)(2,1)S(1)}, bf16[128,1024]{1,0:T(8,128)(2,1)S(1)}, u32[]{:S(2)}, u32[]{:S(2)}) collective-permute-start(bf16[128,1024]{1,0:T(8,128)(2,1)S(1)} %get-tuple-element.29), channel_id=1, source_target_pairs={{0,192},{64,0},{128,64},{192,128},{1,193},{65,1},{129,65},{193,129... | collective-permute-start | bytes 786440 | tf_op jit(solution)/shard_map/ppermute | solution.py:246
  61.6 8.6 %collective-permute-start.10 = (bf16[128,1024]{1,0:T(8,128)(2,1)S(1)}, bf16[128,1024]{1,0:T(8,128)(2,1)S(1)}, u32[]{:S(2)}, u32[]{:S(2)}) collective-permute-start(bf16[128,1024]{1,0:T(8,128)(2,1)S(1)} %get-tuple-element.25), channel_id=1, source_target_pairs={{0,64},{64,128},{128,192},{192,0},{1,65},{65,129},{129,193},{193,1... | collective-permute-start | bytes 786440 | tf_op jit(solution)/shard_map/ppermute | solution.py:246
  61.7 8.6 %collective-permute-start.9 = (bf16[128,1024]{1,0:T(8,128)(2,1)S(1)}, bf16[128,1024]{1,0:T(8,128)(2,1)S(1)}, u32[]{:S(2)}, u32[]{:S(2)}) collective-permute-start(bf16[128,1024]{1,0:T(8,128)(2,1)S(1)} %get-tuple-element.24), channel_id=1, source_target_pairs={{0,192},{64,0},{128,64},{192,128},{1,193},{65,1},{129,65},{193,129... | collective-permute-start | bytes 786440 | tf_op jit(solution)/shard_map/ppermute | solution.py:246
  65.1 10.8 %collective-permute-start.14 = (bf16[128,1024]{1,0:T(8,128)(2,1)S(1)}, bf16[128,1024]{1,0:T(8,128)(2,1)S(1)}, u32[]{:S(2)}, u32[]{:S(2)}) collective-permute-start(bf16[128,1024]{1,0:T(8,128)(2,1)S(1)} %add_convert_fusion.1), channel_id=1, source_target_pairs={{0,64},{64,128},{128,192},{192,0},{1,65},{65,129},{129,193},{193,1... | collective-permute-start | bytes 786440 | tf_op jit(solution)/shard_map/ppermute | solution.py:246
  65.2 14.4 %collective-permute-start.13 = (bf16[128,1024]{1,0:T(8,128)(2,1)S(1)}, bf16[128,1024]{1,0:T(8,128)(2,1)S(1)}, u32[]{:S(2)}, u32[]{:S(2)}) collective-permute-start(bf16[128,1024]{1,0:T(8,128)(2,1)S(1)} %add_convert_fusion.2), channel_id=1, source_target_pairs={{0,192},{64,0},{128,64},{192,128},{1,193},{65,1},{129,65},{193,129... | collective-permute-start | bytes 786440 | tf_op jit(solution)/shard_map/ppermute | solution.py:246
  75.9 6.4 %collective-permute-start.15 = (bf16[64,1024]{1,0:T(8,128)(2,1)S(1)}, bf16[64,1024]{1,0:T(8,128)(2,1)S(1)}, u32[]{:S(2)}, u32[]{:S(2)}) collective-permute-start(bf16[64,1024]{1,0:T(8,128)(2,1)S(1)} %get-tuple-element.34), channel_id=1, source_target_pairs={{0,32},{16,48},{32,0},{48,16},{1,33},{17,49},{33,1},{49,17},{2,34}... | collective-permute-start | bytes 393224 | tf_op jit(solution)/shard_map/ppermute | solution.py:246
  76.6 5.8 %collective-permute-start.16 = (bf16[64,1024]{1,0:T(8,128)(2,1)S(1)}, bf16[64,1024]{1,0:T(8,128)(2,1)S(1)}, u32[]{:S(2)}, u32[]{:S(2)}) collective-permute-start(bf16[64,1024]{1,0:T(8,128)(2,1)S(1)} %get-tuple-element.35), channel_id=1, source_target_pairs={{0,48},{16,0},{32,16},{48,32},{1,49},{17,1},{33,17},{49,33},{2,50}... | collective-permute-start | bytes 393224 | tf_op jit(solution)/shard_map/ppermute | solution.py:246
  79.7 7.3 %collective-permute-start.17 = (bf16[64,1024]{1,0:T(8,128)(2,1)S(1)}, bf16[64,1024]{1,0:T(8,128)(2,1)S(1)}, u32[]{:S(2)}, u32[]{:S(2)}) collective-permute-start(bf16[64,1024]{1,0:T(8,128)(2,1)S(1)} %slice.31), channel_id=1, source_target_pairs={{0,16},{16,32},{32,48},{48,0},{1,17},{17,33},{33,49},{49,1},{2,18}... | collective-permute-start | bytes 393224 | tf_op jit(solution)/shard_map/ppermute | solution.py:246

commit v5 on v4

--- a/solution.py
+++ b/solution.py
@@ -249,12 +249,13 @@
     table = shifted(item_table, "core", 2, 1)
     gain = shifted(head_gain, "core", 2, 1)
     pos_other = shifted(pos_ids, "core", 2, 1)
+    pos_near = shifted(pos_ids, "y", 4, 1)
 
     slot = lax.broadcasted_iota(jnp.int32, (nx * nz, neg_dev), 0)
     slots = lax.psum(jnp.where(slot == x * nz + z, neg_ids[None], 0), ("x", "z"))
 
     e, q, m, msg = scores(
-        1.0 / math.sqrt(width), nx, nz, x.reshape(1), z.reshape(1), core.reshape(1), offset.reshape(1), slots, pos_ids, pos_other,
+        1.0 / math.sqrt(width), nx, nz, x.reshape(1), z.reshape(1), core.reshape(1), offset.reshape(1), slots, pos_near, pos_other,
         gain, user_states, other, table,
     )
     msg = fold(msg, *[lax.ppermute(msg, "y", [(i, i ^ k) for i in range(4)]) for k in (2, 1, 3)])

time: 89.4 us -> 89.3 us (level)
  blocking collectives: 11.5 us -> 12.9 us
    psum x1, blocking collectives: 11.5 us -> 12.9 us  [shards(): lax.psum(jnp.where(slot == x * nz + z, neg_ids[None], 0), ('x', 'z'))]
    unnamed x6 -> x4, local copies, waits for them, and re-layouts: 1.81 us -> 1.13 us
    ppermute x15 -> x16, starting transfers between devices: 22.6 us -> 22.1 us  [shifted(): lax.ppermute(value, axis, [(i, (i + by) % size) for i in range(size)])]
    ppermute x15 -> x16, waiting for transfers between devices: 16.6 us -> 17 us  [shifted(): lax.ppermute(value, axis, [(i, (i + by) % size) for i in range(size)])]
  transfers between devices with their start and end apart: 18 -> 19, of which waited for: 11 -> 12; matrix products, arithmetic and copies ran while one was open for 1% -> 1% of each run, Pallas kernels for 5% -> 5%
where the time goes in v5:
time: 89.3 us; the launch traced here: 87.9 us
  starting transfers between devices  25.9 us (29%)
  Pallas kernels  24.4 us (27%)
  waiting for transfers between devices  20.3 us (23%)
  blocking collectives  12.9 us (14%)
  other arithmetic  1.74 us (2%)
  between operations  1.44 us (2%)
  local copies, waits for them, and re-layouts  1.17 us (1%)
    ppermute x16, starting transfers between devices, shifted(): lax.ppermute(value, axis, [(i, (i + by) % size) for i in range(size)])  22.1 us
    pallas_call x1, Pallas kernels, scores(): pl.pallas_call(functools.partial(score_kernel, inv, nx, nz), grid=(1,), i...  18.4 us
    ppermute x16, waiting for transfers between devices, shifted(): lax.ppermute(value, axis, [(i, (i + by) % size) for i in range(size)])  17 us
    psum x1, blocking collectives, shards(): lax.psum(jnp.where(slot == x * nz + z, neg_ids[None], 0), ('x', 'z'))  12.9 us
    pallas_call x3, Pallas kernels, grad(): pl.pallas_call(body, grid=(1,), in_specs=[full(*s.shape) for s in small]...  5.96 us
    ppermute x3, starting transfers between devices, shards(): lax.ppermute(msg, 'y', [(i, i ^ k) for i in range(4)])  3.78 us
    ppermute x3, waiting for transfers between devices, shards(): lax.ppermute(msg, 'y', [(i, i ^ k) for i in range(4)])  3.27 us
  transfers between devices with their start and end apart: 19, of which 12 were waited for; matrix products, arithmetic and copies ran while one was open for 1% of the time, Pallas kernels for 5%

profile of v5, /device:TPU:1, one launch (start us, length us, event | category | flops | bytes accessed | tf_op | source)
XLA Modules:
  0.0 87.9 jit_solution(17986634425888919580)
XLA Ops:
  0.6 3.3 %collective-permute-start.4 = (bf16[2048,1024]{1,0:T(8,128)(2,1)}, bf16[2048,1024]{1,0:T(8,128)(2,1)}, u32[]{:S(2)}, u32[]{:S(2)}) collective-permute-start(bf16[2048,1024]{1,0:T(8,128)(2,1)} %param.9), channel_id=1, source_target_pairs={{0,8},{8,0},{1,9},{9,1},{2,10},{10,2},{3,11},{11,3},{4,12},{12,4},... | collective-permute-start | bytes 12582920 | tf_op jit(solution)/shard_map/ppermute | solution.py:246
  4.0 0.1 collective-permute-start.3
  4.1 0.4 collective-permute-start.1
  4.6 0.7 broadcast_select_fusion
  5.3 12.9 %psum.7.ids_ref = s32[16,64]{1,0:T(8,128)S(1)} all-reduce(s32[16,64]{1,0:T(8,128)S(1)} %broadcast_select_fusion), channel_id=1, replica_groups=mesh['x'=4,'z'=4,'core'=2,'zh'=2,'y'=4] {'x','z'}, use_global_device_ids=true, to_apply=%region_0.1 | all-reduce | flops 1024 | bytes 8192 | tf_op jit(solution)/shard_map/psum | solution.py:255
  18.3 1.1 %copy-done = bf16[384,1024]{1,0:T(8,128)(2,1)S(1)} copy-done((bf16[384,1024]{1,0:T(8,128)(2,1)S(1)}, bf16[384,1024]{1,0:T(8,128)(2,1)}, u32[]{:S(2)}) %copy-start) | copy-done | bytes 786456
  19.4 18.4 %shard_map.86 = (f32[1024,2304]{1,0:T(8,128)S(1)}, bf16[3,768,1024]{2,1,0:T(8,128)(2,1)S(1)}, f32[3,768]{1,0:T(4,128)S(1)}, f32[3,1536]{1,0:T(4,128)S(1)}) custom-call(s32[1]{0:T(128)} %bitcast.x_ref, s32[1]{0:T(128)} %bitcast.1.z_ref, s32[1]{0:T(128)} %bitcast.2.core_ref, s32[1]{0:T(128)} %bitcast.3.off_ref, s32[16,64]{1,0:T(8,128)S(1)} %psum.7.ids_ref, ...), custom_call_target="tpu_custom_call" | custom-call | tf_op jit(solution)/shard_map/pallas_call | solution.py:101
  37.9 2.7 %collective-permute-start.5 = (f32[3,1536]{1,0:T(4,128)S(1)}, f32[3,1536]{1,0:T(4,128)S(1)}, u32[]{:S(2)}, u32[]{:S(2)}) collective-permute-start(f32[3,1536]{1,0:T(4,128)S(1)} %get-tuple-element.18.refs_0_), channel_id=1, source_target_pairs={{0,2},{1,3},{2,0},{3,1},{4,6},{5,7},{6,4},{7,5},{8,10},{9,11},{10,... | collective-permute-start | bytes 55304 | tf_op jit(solution)/shard_map/ppermute | solution.py:261
  40.6 1.1 %collective-permute-start.7 = (f32[3,1536]{1,0:T(4,128)S(1)}, f32[3,1536]{1,0:T(4,128)S(1)}, u32[]{:S(2)}, u32[]{:S(2)}) collective-permute-start(f32[3,1536]{1,0:T(4,128)S(1)} %get-tuple-element.18.refs_0_), channel_id=1, source_target_pairs={{0,3},{1,2},{2,1},{3,0},{4,7},{5,6},{6,5},{7,4},{8,11},{9,10},{10,... | collective-permute-start | bytes 55304 | tf_op jit(solution)/shard_map/ppermute | solution.py:261
  41.7 0.5 collective-permute-done.5.refs_1_
  42.1 1.6 %collective-permute-done.6.refs_2_ = f32[3,1536]{1,0:T(4,128)S(1)} collective-permute-done((f32[3,1536]{1,0:T(4,128)S(1)}, f32[3,1536]{1,0:T(4,128)S(1)}, u32[]{:S(2)}, u32[]{:S(2)}) %collective-permute-start.6) | collective-permute-done | bytes 18464 | tf_op jit(solution)/shard_map/ppermute | solution.py:261
  43.7 1.2 %collective-permute-done.7.refs_3_ = f32[3,1536]{1,0:T(4,128)S(1)} collective-permute-done((f32[3,1536]{1,0:T(4,128)S(1)}, f32[3,1536]{1,0:T(4,128)S(1)}, u32[]{:S(2)}, u32[]{:S(2)}) %collective-permute-start.7) | collective-permute-done | bytes 18464 | tf_op jit(solution)/shard_map/ppermute | solution.py:261
  45.0 5.2 %collective-permute-start.8 = (f32[3,1536]{1,0:T(4,128)S(1)}, f32[3,1536]{1,0:T(4,128)S(1)}, u32[]{:S(2)}, u32[]{:S(2)}) collective-permute-start(f32[3,1536]{1,0:T(4,128)S(1)} %shard_map.87.msg_ref), channel_id=1, source_target_pairs={{0,4},{4,0},{1,5},{5,1},{2,6},{6,2},{3,7},{7,3},{8,12},{12,8},{9,1... | collective-permute-start | bytes 55304 | tf_op jit(solution)/shard_map/ppermute | solution.py:246
  50.8 0.8 collective-permute-done.8.near_ref
  51.7 1.9 %collective-permute-start.9 = (f32[3,1920]{1,0:T(4,128)S(1)}, f32[3,1920]{1,0:T(4,128)S(1)}, u32[]{:S(2)}, u32[]{:S(2)}) collective-permute-start(f32[3,1920]{1,0:T(4,128)S(1)} %shard_map.88.part_ref), channel_id=1, source_target_pairs={{0,8},{8,0},{1,9},{9,1},{2,10},{10,2},{3,11},{11,3},{4,12},{12,4},... | collective-permute-start | bytes 69128 | tf_op jit(solution)/shard_map/ppermute | solution.py:246
  53.5 0.9 collective-permute-done.9.cross_ref
  54.4 1.9 %shard_map.89 = (f32[3,768]{1,0:T(4,128)S(1)}, f32[3,384]{1,0:T(4,128)}, bf16[128,1024]{1,0:T(8,128)(2,1)S(1)}, bf16[128,1024]{1,0:T(8,128)(2,1)S(1)}) custom-call(f32[3,1920]{1,0:T(4,128)S(1)} %shard_map.88.part_ref, f32[3,1920]{1,0:T(4,128)S(1)} %collective-permute-done.9.cross_ref, f32[3,768]{1,0:T(4,128)S(1)} %get-tuple-element.19.m_ref, ...), custom_call_target="tpu_custom_call" | custom-call | flops 1207959552 | bytes 7077888 | tf_op jit(solution)/shard_map/pallas_call | solution.py:218
  56.3 2.7 %collective-permute-start.13 = (bf16[128,1024]{1,0:T(8,128)(2,1)S(1)}, bf16[128,1024]{1,0:T(8,128)(2,1)S(1)}, u32[]{:S(2)}, u32[]{:S(2)}) collective-permute-start(bf16[128,1024]{1,0:T(8,128)(2,1)S(1)} %get-tuple-element.29), channel_id=1, source_target_pairs={{0,192},{64,0},{128,64},{192,128},{1,193},{65,1},{129,65},{193,129... | collective-permute-start | bytes 786440 | tf_op jit(solution)/shard_map/ppermute | solution.py:246
  59.0 2.6 %shard_map.90 = (f32[128,1024]{1,0:T(8,128)S(1)}, bf16[128,1024]{1,0:T(8,128)(2,1)S(1)}, bf16[128,1024]{1,0:T(8,128)(2,1)S(1)}, f32[128,1024]{1,0:T(8,128)S(1)}) custom-call(f32[3,768]{1,0:T(4,128)S(1)} %get-tuple-element.23.c_ref, f32[1024,2304]{1,0:T(8,128)S(1)} %get-tuple-element.20.e_ref, bf16[3,768,1024]{2,1,0:T(8,128)(2,1)S(1)} %get-tuple-element.21.q_ref), custom_call_target="tpu_custom_call" | custom-call | flops 2415919104 | bytes 9437184 | tf_op jit(solution)/shard_map/pallas_call | solution.py:218
  61.7 1.5 %collective-permute-start.11 = (bf16[128,1024]{1,0:T(8,128)(2,1)S(1)}, bf16[128,1024]{1,0:T(8,128)(2,1)S(1)}, u32[]{:S(2)}, u32[]{:S(2)}) collective-permute-start(bf16[128,1024]{1,0:T(8,128)(2,1)S(1)} %get-tuple-element.25), channel_id=1, source_target_pairs={{0,64},{64,128},{128,192},{192,0},{1,65},{65,129},{129,193},{193,1... | collective-permute-start | bytes 786440 | tf_op jit(solution)/shard_map/ppermute | solution.py:246
  63.1 1.9 %collective-permute-done.12 = bf16[128,1024]{1,0:T(8,128)(2,1)S(1)} collective-permute-done((bf16[128,1024]{1,0:T(8,128)(2,1)S(1)}, bf16[128,1024]{1,0:T(8,128)(2,1)S(1)}, u32[]{:S(2)}, u32[]{:S(2)}) %collective-permute-start.12) | collective-permute-done | bytes 262176 | tf_op jit(solution)/shard_map/ppermute | solution.py:246
  65.3 2.7 %collective-permute-start.14 = (bf16[128,1024]{1,0:T(8,128)(2,1)S(1)}, bf16[128,1024]{1,0:T(8,128)(2,1)S(1)}, u32[]{:S(2)}, u32[]{:S(2)}) collective-permute-start(bf16[128,1024]{1,0:T(8,128)(2,1)S(1)} %add_convert_fusion.2), channel_id=1, source_target_pairs={{0,192},{64,0},{128,64},{192,128},{1,193},{65,1},{129,65},{193,129... | collective-permute-start | bytes 786440 | tf_op jit(solution)/shard_map/ppermute | solution.py:246
  68.0 1.6 %collective-permute-done.10.in_a_ref = bf16[128,1024]{1,0:T(8,128)(2,1)S(1)} collective-permute-done((bf16[128,1024]{1,0:T(8,128)(2,1)S(1)}, bf16[128,1024]{1,0:T(8,128)(2,1)S(1)}, u32[]{:S(2)}, u32[]{:S(2)}) %collective-permute-start.10) | collective-permute-done | bytes 262176 | tf_op jit(solution)/shard_map/ppermute | solution.py:246
  69.6 0.6 collective-permute-done.11.in_b_ref
  70.1 1.4 %shard_map.91 = (f32[128,1024]{1,0:T(8,128)S(1)}, f32[128,1024]{1,0:T(8,128)S(1)}) custom-call(f32[3,768]{1,0:T(4,128)S(1)} %get-tuple-element.23.c_ref, bf16[128,1024]{1,0:T(8,128)(2,1)S(1)} %collective-permute-done.10.in_a_ref, bf16[128,1024]{1,0:T(8,128)(2,1)S(1)} %collective-permute-done.11.in_b_ref, f32[1024,2304]{1,0:T(8,128)S(1)} %get-tuple-element.20.e_ref, ...), custom_call_target="tpu_custom_call" | custom-call | flops 1207959552 | bytes 7077888 | tf_op jit(solution)/shard_map/pallas_call | solution.py:218
  71.6 4.2 %collective-permute-done.15 = bf16[128,1024]{1,0:T(8,128)(2,1)S(1)} collective-permute-done((bf16[128,1024]{1,0:T(8,128)(2,1)S(1)}, bf16[128,1024]{1,0:T(8,128)(2,1)S(1)}, u32[]{:S(2)}, u32[]{:S(2)}) %collective-permute-start.15) | collective-permute-done | bytes 262176 | tf_op jit(solution)/shard_map/ppermute | solution.py:246
  75.9 0.8 collective-permute-start.16
  76.6 3.2 %collective-permute-start.17 = (bf16[64,1024]{1,0:T(8,128)(2,1)S(1)}, bf16[64,1024]{1,0:T(8,128)(2,1)S(1)}, u32[]{:S(2)}, u32[]{:S(2)}) collective-permute-start(bf16[64,1024]{1,0:T(8,128)(2,1)S(1)} %get-tuple-element.35), channel_id=1, source_target_pairs={{0,48},{16,0},{32,16},{48,32},{1,49},{17,1},{33,17},{49,33},{2,50}... | collective-permute-start | bytes 393224 | tf_op jit(solution)/shard_map/ppermute | solution.py:246
  80.0 0.7 collective-permute-done.16
  80.8 1.7 %collective-permute-done.17 = bf16[64,1024]{1,0:T(8,128)(2,1)S(1)} collective-permute-done((bf16[64,1024]{1,0:T(8,128)(2,1)S(1)}, bf16[64,1024]{1,0:T(8,128)(2,1)S(1)}, u32[]{:S(2)}, u32[]{:S(2)}) %collective-permute-start.17) | collective-permute-done | bytes 131104 | tf_op jit(solution)/shard_map/ppermute | solution.py:246
  82.5 4.7 %collective-permute-done.18 = bf16[64,1024]{1,0:T(8,128)(2,1)S(1)} collective-permute-done((bf16[64,1024]{1,0:T(8,128)(2,1)S(1)}, bf16[64,1024]{1,0:T(8,128)(2,1)S(1)}, u32[]{:S(2)}, u32[]{:S(2)}) %collective-permute-start.18) | collective-permute-done | bytes 131104 | tf_op jit(solution)/shard_map/ppermute | solution.py:246
  87.1 0.8 fusion.2
  (26 shorter events, 0.7 us)
Async XLA Ops:
  0.6 51.0 %copy-start.1 = (s32[3,384]{1,0:T(4,128)S(1)}, s32[3,384]{1,0:T(4,128)}, u32[]{:S(2)}) copy-start(s32[3,384]{1,0:T(4,128)} %mask_ref.1) | copy-start | bytes 13828
  0.6 17.6 %collective-permute-start.4 = (bf16[2048,1024]{1,0:T(8,128)(2,1)}, bf16[2048,1024]{1,0:T(8,128)(2,1)}, u32[]{:S(2)}, u32[]{:S(2)}) collective-permute-start(bf16[2048,1024]{1,0:T(8,128)(2,1)} %param.9), channel_id=1, source_target_pairs={{0,8},{8,0},{1,9},{9,1},{2,10},{10,2},{3,11},{11,3},{4,12},{12,4},... | collective-permute-start | bytes 12582920 | tf_op jit(solution)/shard_map/ppermute | solution.py:246
  4.0 14.3 %collective-permute-start.3 = (bf16[384,1024]{1,0:T(8,128)(2,1)}, bf16[384,1024]{1,0:T(8,128)(2,1)S(1)}, u32[]{:S(2)}, u32[]{:S(2)}) collective-permute-start(bf16[384,1024]{1,0:T(8,128)(2,1)} %own_ref.1), channel_id=1, source_target_pairs={{0,8},{8,0},{1,9},{9,1},{2,10},{10,2},{3,11},{11,3},{4,12},{12,4},... | collective-permute-start | bytes 2359304 | tf_op jit(solution)/shard_map/ppermute | solution.py:246
  4.1 14.2 %collective-permute-start = (s32[384]{0:T(512)}, s32[384]{0:T(512)S(1)}, u32[]{:S(2)}, u32[]{:S(2)}) collective-permute-start(s32[384]{0:T(512)} %param.11), channel_id=1, source_target_pairs={{0,1},{1,2},{2,3},{3,0},{4,5},{5,6},{6,7},{7,4},{8,9},{9,10},{10,1... | collective-permute-start | bytes 4616 | tf_op jit(solution)/shard_map/ppermute | solution.py:246
  4.1 14.2 %collective-permute-start.1 = (s32[384]{0:T(512)}, s32[384]{0:T(512)S(1)}, u32[]{:S(2)}, u32[]{:S(2)}) collective-permute-start(s32[384]{0:T(512)} %param.11), channel_id=1, source_target_pairs={{0,8},{8,0},{1,9},{9,1},{2,10},{10,2},{3,11},{11,3},{4,12},{12,4},... | collective-permute-start | bytes 4616 | tf_op jit(solution)/shard_map/ppermute | solution.py:246
  4.5 13.8 %collective-permute-start.2 = (f32[3,1024]{1,0:T(4,128)}, f32[3,1024]{1,0:T(4,128)S(1)}, u32[]{:S(2)}, u32[]{:S(2)}) collective-permute-start(f32[3,1024]{1,0:T(4,128)} %param.8), channel_id=1, source_target_pairs={{0,8},{8,0},{1,9},{9,1},{2,10},{10,2},{3,11},{11,3},{4,12},{12,4},... | collective-permute-start | bytes 36872 | tf_op jit(solution)/shard_map/ppermute | solution.py:246
  18.3 1.1 %copy-start = (bf16[384,1024]{1,0:T(8,128)(2,1)S(1)}, bf16[384,1024]{1,0:T(8,128)(2,1)}, u32[]{:S(2)}) copy-start(bf16[384,1024]{1,0:T(8,128)(2,1)} %own_ref.1) | copy-start | bytes 2359300
  37.9 4.3 %collective-permute-start.5 = (f32[3,1536]{1,0:T(4,128)S(1)}, f32[3,1536]{1,0:T(4,128)S(1)}, u32[]{:S(2)}, u32[]{:S(2)}) collective-permute-start(f32[3,1536]{1,0:T(4,128)S(1)} %get-tuple-element.18.refs_0_), channel_id=1, source_target_pairs={{0,2},{1,3},{2,0},{3,1},{4,6},{5,7},{6,4},{7,5},{8,10},{9,11},{10,... | collective-permute-start | bytes 55304 | tf_op jit(solution)/shard_map/ppermute | solution.py:261
  40.6 3.1 %collective-permute-start.6 = (f32[3,1536]{1,0:T(4,128)S(1)}, f32[3,1536]{1,0:T(4,128)S(1)}, u32[]{:S(2)}, u32[]{:S(2)}) collective-permute-start(f32[3,1536]{1,0:T(4,128)S(1)} %get-tuple-element.18.refs_0_), channel_id=1, source_target_pairs={{0,1},{1,0},{2,3},{3,2},{4,5},{5,4},{6,7},{7,6},{8,9},{9,8},{10,11... | collective-permute-start | bytes 55304 | tf_op jit(solution)/shard_map/ppermute | solution.py:261
  40.6 4.3 %collective-permute-start.7 = (f32[3,1536]{1,0:T(4,128)S(1)}, f32[3,1536]{1,0:T(4,128)S(1)}, u32[]{:S(2)}, u32[]{:S(2)}) collective-permute-start(f32[3,1536]{1,0:T(4,128)S(1)} %get-tuple-element.18.refs_0_), channel_id=1, source_target_pairs={{0,3},{1,2},{2,1},{3,0},{4,7},{5,6},{6,5},{7,4},{8,11},{9,10},{10,... | collective-permute-start | bytes 55304 | tf_op jit(solution)/shard_map/ppermute | solution.py:261
  45.0 6.7 %collective-permute-start.8 = (f32[3,1536]{1,0:T(4,128)S(1)}, f32[3,1536]{1,0:T(4,128)S(1)}, u32[]{:S(2)}, u32[]{:S(2)}) collective-permute-start(f32[3,1536]{1,0:T(4,128)S(1)} %shard_map.87.msg_ref), channel_id=1, source_target_pairs={{0,4},{4,0},{1,5},{5,1},{2,6},{6,2},{3,7},{7,3},{8,12},{12,8},{9,1... | collective-permute-start | bytes 55304 | tf_op jit(solution)/shard_map/ppermute | solution.py:246
  51.7 2.7 %collective-permute-start.9 = (f32[3,1920]{1,0:T(4,128)S(1)}, f32[3,1920]{1,0:T(4,128)S(1)}, u32[]{:S(2)}, u32[]{:S(2)}) collective-permute-start(f32[3,1920]{1,0:T(4,128)S(1)} %shard_map.88.part_ref), channel_id=1, source_target_pairs={{0,8},{8,0},{1,9},{9,1},{2,10},{10,2},{3,11},{11,3},{4,12},{12,4},... | collective-permute-start | bytes 69128 | tf_op jit(solution)/shard_map/ppermute | solution.py:246
  56.3 8.8 %collective-permute-start.12 = (bf16[128,1024]{1,0:T(8,128)(2,1)S(1)}, bf16[128,1024]{1,0:T(8,128)(2,1)S(1)}, u32[]{:S(2)}, u32[]{:S(2)}) collective-permute-start(bf16[128,1024]{1,0:T(8,128)(2,1)S(1)} %get-tuple-element.28), channel_id=1, source_target_pairs={{0,64},{64,128},{128,192},{192,0},{1,65},{65,129},{129,193},{193,1... | collective-permute-start | bytes 786440 | tf_op jit(solution)/shard_map/ppermute | solution.py:246
  56.3 8.8 %collective-permute-start.13 = (bf16[128,1024]{1,0:T(8,128)(2,1)S(1)}, bf16[128,1024]{1,0:T(8,128)(2,1)S(1)}, u32[]{:S(2)}, u32[]{:S(2)}) collective-permute-start(bf16[128,1024]{1,0:T(8,128)(2,1)S(1)} %get-tuple-element.29), channel_id=1, source_target_pairs={{0,192},{64,0},{128,64},{192,128},{1,193},{65,1},{129,65},{193,129... | collective-permute-start | bytes 786440 | tf_op jit(solution)/shard_map/ppermute | solution.py:246
  61.6 8.0 %collective-permute-start.10 = (bf16[128,1024]{1,0:T(8,128)(2,1)S(1)}, bf16[128,1024]{1,0:T(8,128)(2,1)S(1)}, u32[]{:S(2)}, u32[]{:S(2)}) collective-permute-start(bf16[128,1024]{1,0:T(8,128)(2,1)S(1)} %get-tuple-element.24), channel_id=1, source_target_pairs={{0,192},{64,0},{128,64},{192,128},{1,193},{65,1},{129,65},{193,129... | collective-permute-start | bytes 786440 | tf_op jit(solution)/shard_map/ppermute | solution.py:246
  61.7 8.5 %collective-permute-start.11 = (bf16[128,1024]{1,0:T(8,128)(2,1)S(1)}, bf16[128,1024]{1,0:T(8,128)(2,1)S(1)}, u32[]{:S(2)}, u32[]{:S(2)}) collective-permute-start(bf16[128,1024]{1,0:T(8,128)(2,1)S(1)} %get-tuple-element.25), channel_id=1, source_target_pairs={{0,64},{64,128},{128,192},{192,0},{1,65},{65,129},{129,193},{193,1... | collective-permute-start | bytes 786440 | tf_op jit(solution)/shard_map/ppermute | solution.py:246
  65.1 10.7 %collective-permute-start.15 = (bf16[128,1024]{1,0:T(8,128)(2,1)S(1)}, bf16[128,1024]{1,0:T(8,128)(2,1)S(1)}, u32[]{:S(2)}, u32[]{:S(2)}) collective-permute-start(bf16[128,1024]{1,0:T(8,128)(2,1)S(1)} %add_convert_fusion.1), channel_id=1, source_target_pairs={{0,64},{64,128},{128,192},{192,0},{1,65},{65,129},{129,193},{193,1... | collective-permute-start | bytes 786440 | tf_op jit(solution)/shard_map/ppermute | solution.py:246
  65.3 14.6 %collective-permute-start.14 = (bf16[128,1024]{1,0:T(8,128)(2,1)S(1)}, bf16[128,1024]{1,0:T(8,128)(2,1)S(1)}, u32[]{:S(2)}, u32[]{:S(2)}) collective-permute-start(bf16[128,1024]{1,0:T(8,128)(2,1)S(1)} %add_convert_fusion.2), channel_id=1, source_target_pairs={{0,192},{64,0},{128,64},{192,128},{1,193},{65,1},{129,65},{193,129... | collective-permute-start | bytes 786440 | tf_op jit(solution)/shard_map/ppermute | solution.py:246
  75.9 4.9 %collective-permute-start.16 = (bf16[64,1024]{1,0:T(8,128)(2,1)S(1)}, bf16[64,1024]{1,0:T(8,128)(2,1)S(1)}, u32[]{:S(2)}, u32[]{:S(2)}) collective-permute-start(bf16[64,1024]{1,0:T(8,128)(2,1)S(1)} %get-tuple-element.34), channel_id=1, source_target_pairs={{0,32},{16,48},{32,0},{48,16},{1,33},{17,49},{33,1},{49,17},{2,34}... | collective-permute-start | bytes 393224 | tf_op jit(solution)/shard_map/ppermute | solution.py:246
  76.6 5.8 %collective-permute-start.17 = (bf16[64,1024]{1,0:T(8,128)(2,1)S(1)}, bf16[64,1024]{1,0:T(8,128)(2,1)S(1)}, u32[]{:S(2)}, u32[]{:S(2)}) collective-permute-start(bf16[64,1024]{1,0:T(8,128)(2,1)S(1)} %get-tuple-element.35), channel_id=1, source_target_pairs={{0,48},{16,0},{32,16},{48,32},{1,49},{17,1},{33,17},{49,33},{2,50}... | collective-permute-start | bytes 393224 | tf_op jit(solution)/shard_map/ppermute | solution.py:246
  79.9 7.2 %collective-permute-start.18 = (bf16[64,1024]{1,0:T(8,128)(2,1)S(1)}, bf16[64,1024]{1,0:T(8,128)(2,1)S(1)}, u32[]{:S(2)}, u32[]{:S(2)}) collective-permute-start(bf16[64,1024]{1,0:T(8,128)(2,1)S(1)} %slice.31), channel_id=1, source_target_pairs={{0,16},{16,32},{32,48},{48,0},{1,17},{17,33},{33,49},{49,1},{2,18}... | collective-permute-start | bytes 393224 | tf_op jit(solution)/shard_map/ppermute | solution.py:246

commit v6 on v5

--- a/solution.py
+++ b/solution.py
@@ -270,7 +270,6 @@
         (c,), e, q, 2 * quarter, 1, [(half, F32), (half, BF16), (half, BF16), (half, F32)]
     )
     up_b, down_a = shifted(up_b, "x", nx, 1), shifted(down_a, "x", nx, -1)
-    far_a, far_b = lax.optimization_barrier((far_a, far_b))
     up_a = shifted((up_a + far_a.astype(F32)).astype(BF16), "x", nx, 1)
     down_b = shifted((down_b + far_b.astype(F32)).astype(BF16), "x", nx, -1)
     own_a, own_b = grad((c, down_a, up_b), e, q, quarter, 1, [(half, F32)] * 2)

time: 89.3 us -> 89.3 us (level)
  no operation moved by 1% of the time
where the time goes in v6:
time: 89.3 us; the launch traced here: 87.9 us
  starting transfers between devices  25.9 us (29%)
  Pallas kernels  24.4 us (27%)
  waiting for transfers between devices  20.3 us (23%)
  blocking collectives  12.9 us (14%)
  other arithmetic  1.75 us (2%)
  between operations  1.44 us (2%)
  local copies, waits for them, and re-layouts  1.17 us (1%)
    ppermute x16, starting transfers between devices, shifted(): lax.ppermute(value, axis, [(i, (i + by) % size) for i in range(size)])  22.1 us
    pallas_call x1, Pallas kernels, scores(): pl.pallas_call(functools.partial(score_kernel, inv, nx, nz), grid=(1,), i...  18.4 us
    ppermute x16, waiting for transfers between devices, shifted(): lax.ppermute(value, axis, [(i, (i + by) % size) for i in range(size)])  17 us
    psum x1, blocking collectives, shards(): lax.psum(jnp.where(slot == x * nz + z, neg_ids[None], 0), ('x', 'z'))  12.9 us
    pallas_call x3, Pallas kernels, grad(): pl.pallas_call(body, grid=(1,), in_specs=[full(*s.shape) for s in small]...  5.96 us
    ppermute x3, starting transfers between devices, shards(): lax.ppermute(msg, 'y', [(i, i ^ k) for i in range(4)])  3.78 us
    ppermute x3, waiting for transfers between devices, shards(): lax.ppermute(msg, 'y', [(i, i ^ k) for i in range(4)])  3.27 us
  transfers between devices with their start and end apart: 19, of which 12 were waited for; matrix products, arithmetic and copies ran while one was open for 1% of the time, Pallas kernels for 5%

profile of v6, /device:TPU:1, one launch (start us, length us, event | category | flops | bytes accessed | tf_op | source)
XLA Modules:
  0.0 87.9 jit_solution(5594900599028077339)
XLA Ops:
  0.6 3.3 %collective-permute-start.4 = (bf16[2048,1024]{1,0:T(8,128)(2,1)}, bf16[2048,1024]{1,0:T(8,128)(2,1)}, u32[]{:S(2)}, u32[]{:S(2)}) collective-permute-start(bf16[2048,1024]{1,0:T(8,128)(2,1)} %param.9), channel_id=1, source_target_pairs={{0,8},{8,0},{1,9},{9,1},{2,10},{10,2},{3,11},{11,3},{4,12},{12,4},... | collective-permute-start | bytes 12582920 | tf_op jit(solution)/shard_map/ppermute | solution.py:246
  4.0 0.1 collective-permute-start.3
  4.1 0.4 collective-permute-start.1
  4.6 0.7 broadcast_select_fusion
  5.3 12.9 %psum.7.ids_ref = s32[16,64]{1,0:T(8,128)S(1)} all-reduce(s32[16,64]{1,0:T(8,128)S(1)} %broadcast_select_fusion), channel_id=1, replica_groups=mesh['x'=4,'z'=4,'core'=2,'zh'=2,'y'=4] {'x','z'}, use_global_device_ids=true, to_apply=%region_0.1 | all-reduce | flops 1024 | bytes 8192 | tf_op jit(solution)/shard_map/psum | solution.py:255
  18.3 1.1 %copy-done = bf16[384,1024]{1,0:T(8,128)(2,1)S(1)} copy-done((bf16[384,1024]{1,0:T(8,128)(2,1)S(1)}, bf16[384,1024]{1,0:T(8,128)(2,1)}, u32[]{:S(2)}) %copy-start) | copy-done | bytes 786456
  19.4 18.4 %shard_map.86 = (f32[1024,2304]{1,0:T(8,128)S(1)}, bf16[3,768,1024]{2,1,0:T(8,128)(2,1)S(1)}, f32[3,768]{1,0:T(4,128)S(1)}, f32[3,1536]{1,0:T(4,128)S(1)}) custom-call(s32[1]{0:T(128)} %bitcast.x_ref, s32[1]{0:T(128)} %bitcast.1.z_ref, s32[1]{0:T(128)} %bitcast.2.core_ref, s32[1]{0:T(128)} %bitcast.3.off_ref, s32[16,64]{1,0:T(8,128)S(1)} %psum.7.ids_ref, ...), custom_call_target="tpu_custom_call" | custom-call | tf_op jit(solution)/shard_map/pallas_call | solution.py:101
  37.9 2.7 %collective-permute-start.5 = (f32[3,1536]{1,0:T(4,128)S(1)}, f32[3,1536]{1,0:T(4,128)S(1)}, u32[]{:S(2)}, u32[]{:S(2)}) collective-permute-start(f32[3,1536]{1,0:T(4,128)S(1)} %get-tuple-element.16.refs_0_), channel_id=1, source_target_pairs={{0,2},{1,3},{2,0},{3,1},{4,6},{5,7},{6,4},{7,5},{8,10},{9,11},{10,... | collective-permute-start | bytes 55304 | tf_op jit(solution)/shard_map/ppermute | solution.py:261
  40.6 1.1 %collective-permute-start.7 = (f32[3,1536]{1,0:T(4,128)S(1)}, f32[3,1536]{1,0:T(4,128)S(1)}, u32[]{:S(2)}, u32[]{:S(2)}) collective-permute-start(f32[3,1536]{1,0:T(4,128)S(1)} %get-tuple-element.16.refs_0_), channel_id=1, source_target_pairs={{0,3},{1,2},{2,1},{3,0},{4,7},{5,6},{6,5},{7,4},{8,11},{9,10},{10,... | collective-permute-start | bytes 55304 | tf_op jit(solution)/shard_map/ppermute | solution.py:261
  41.7 0.5 collective-permute-done.5.refs_1_
  42.1 1.6 %collective-permute-done.6.refs_2_ = f32[3,1536]{1,0:T(4,128)S(1)} collective-permute-done((f32[3,1536]{1,0:T(4,128)S(1)}, f32[3,1536]{1,0:T(4,128)S(1)}, u32[]{:S(2)}, u32[]{:S(2)}) %collective-permute-start.6) | collective-permute-done | bytes 18464 | tf_op jit(solution)/shard_map/ppermute | solution.py:261
  43.7 1.2 %collective-permute-done.7.refs_3_ = f32[3,1536]{1,0:T(4,128)S(1)} collective-permute-done((f32[3,1536]{1,0:T(4,128)S(1)}, f32[3,1536]{1,0:T(4,128)S(1)}, u32[]{:S(2)}, u32[]{:S(2)}) %collective-permute-start.7) | collective-permute-done | bytes 18464 | tf_op jit(solution)/shard_map/ppermute | solution.py:261
  45.0 5.2 %collective-permute-start.8 = (f32[3,1536]{1,0:T(4,128)S(1)}, f32[3,1536]{1,0:T(4,128)S(1)}, u32[]{:S(2)}, u32[]{:S(2)}) collective-permute-start(f32[3,1536]{1,0:T(4,128)S(1)} %shard_map.87.msg_ref), channel_id=1, source_target_pairs={{0,4},{4,0},{1,5},{5,1},{2,6},{6,2},{3,7},{7,3},{8,12},{12,8},{9,1... | collective-permute-start | bytes 55304 | tf_op jit(solution)/shard_map/ppermute | solution.py:246
  50.8 0.8 collective-permute-done.8.near_ref
  51.7 1.9 %collective-permute-start.9 = (f32[3,1920]{1,0:T(4,128)S(1)}, f32[3,1920]{1,0:T(4,128)S(1)}, u32[]{:S(2)}, u32[]{:S(2)}) collective-permute-start(f32[3,1920]{1,0:T(4,128)S(1)} %shard_map.88.part_ref), channel_id=1, source_target_pairs={{0,8},{8,0},{1,9},{9,1},{2,10},{10,2},{3,11},{11,3},{4,12},{12,4},... | collective-permute-start | bytes 69128 | tf_op jit(solution)/shard_map/ppermute | solution.py:246
  53.5 0.9 collective-permute-done.9.cross_ref
  54.4 1.9 %shard_map.89 = (f32[3,768]{1,0:T(4,128)S(1)}, f32[3,384]{1,0:T(4,128)}, bf16[128,1024]{1,0:T(8,128)(2,1)S(1)}, bf16[128,1024]{1,0:T(8,128)(2,1)S(1)}) custom-call(f32[3,1920]{1,0:T(4,128)S(1)} %shard_map.88.part_ref, f32[3,1920]{1,0:T(4,128)S(1)} %collective-permute-done.9.cross_ref, f32[3,768]{1,0:T(4,128)S(1)} %get-tuple-element.17.m_ref, ...), custom_call_target="tpu_custom_call" | custom-call | flops 1207959552 | bytes 7077888 | tf_op jit(solution)/shard_map/pallas_call | solution.py:218
  56.3 2.7 %collective-permute-start.12 = (bf16[128,1024]{1,0:T(8,128)(2,1)S(1)}, bf16[128,1024]{1,0:T(8,128)(2,1)S(1)}, u32[]{:S(2)}, u32[]{:S(2)}) collective-permute-start(bf16[128,1024]{1,0:T(8,128)(2,1)S(1)} %get-tuple-element.26), channel_id=1, source_target_pairs={{0,192},{64,0},{128,64},{192,128},{1,193},{65,1},{129,65},{193,129... | collective-permute-start | bytes 786440 | tf_op jit(solution)/shard_map/ppermute | solution.py:246
  59.0 2.6 %shard_map.90 = (f32[128,1024]{1,0:T(8,128)S(1)}, bf16[128,1024]{1,0:T(8,128)(2,1)S(1)}, bf16[128,1024]{1,0:T(8,128)(2,1)S(1)}, f32[128,1024]{1,0:T(8,128)S(1)}) custom-call(f32[3,768]{1,0:T(4,128)S(1)} %get-tuple-element.21.c_ref, f32[1024,2304]{1,0:T(8,128)S(1)} %get-tuple-element.18.e_ref, bf16[3,768,1024]{2,1,0:T(8,128)(2,1)S(1)} %get-tuple-element.19.q_ref), custom_call_target="tpu_custom_call" | custom-call | flops 2415919104 | bytes 9437184 | tf_op jit(solution)/shard_map/pallas_call | solution.py:218
  61.7 1.5 %collective-permute-start.11 = (bf16[128,1024]{1,0:T(8,128)(2,1)S(1)}, bf16[128,1024]{1,0:T(8,128)(2,1)S(1)}, u32[]{:S(2)}, u32[]{:S(2)}) collective-permute-start(bf16[128,1024]{1,0:T(8,128)(2,1)S(1)} %get-tuple-element.23), channel_id=1, source_target_pairs={{0,64},{64,128},{128,192},{192,0},{1,65},{65,129},{129,193},{193,1... | collective-permute-start | bytes 786440 | tf_op jit(solution)/shard_map/ppermute | solution.py:246
  63.1 1.9 %collective-permute-done.14 = bf16[128,1024]{1,0:T(8,128)(2,1)S(1)} collective-permute-done((bf16[128,1024]{1,0:T(8,128)(2,1)S(1)}, bf16[128,1024]{1,0:T(8,128)(2,1)S(1)}, u32[]{:S(2)}, u32[]{:S(2)}) %collective-permute-start.14) | collective-permute-done | bytes 262176 | tf_op jit(solution)/shard_map/ppermute | solution.py:246
  65.3 2.7 %collective-permute-start.13 = (bf16[128,1024]{1,0:T(8,128)(2,1)S(1)}, bf16[128,1024]{1,0:T(8,128)(2,1)S(1)}, u32[]{:S(2)}, u32[]{:S(2)}) collective-permute-start(bf16[128,1024]{1,0:T(8,128)(2,1)S(1)} %add_convert_fusion.2), channel_id=1, source_target_pairs={{0,192},{64,0},{128,64},{192,128},{1,193},{65,1},{129,65},{193,129... | collective-permute-start | bytes 786440 | tf_op jit(solution)/shard_map/ppermute | solution.py:246
  68.0 1.6 %collective-permute-done.10.in_a_ref = bf16[128,1024]{1,0:T(8,128)(2,1)S(1)} collective-permute-done((bf16[128,1024]{1,0:T(8,128)(2,1)S(1)}, bf16[128,1024]{1,0:T(8,128)(2,1)S(1)}, u32[]{:S(2)}, u32[]{:S(2)}) %collective-permute-start.10) | collective-permute-done | bytes 262176 | tf_op jit(solution)/shard_map/ppermute | solution.py:246
  69.6 0.6 collective-permute-done.11.in_b_ref
  70.1 1.4 %shard_map.91 = (f32[128,1024]{1,0:T(8,128)S(1)}, f32[128,1024]{1,0:T(8,128)S(1)}) custom-call(f32[3,768]{1,0:T(4,128)S(1)} %get-tuple-element.21.c_ref, bf16[128,1024]{1,0:T(8,128)(2,1)S(1)} %collective-permute-done.10.in_a_ref, bf16[128,1024]{1,0:T(8,128)(2,1)S(1)} %collective-permute-done.11.in_b_ref, f32[1024,2304]{1,0:T(8,128)S(1)} %get-tuple-element.18.e_ref, ...), custom_call_target="tpu_custom_call" | custom-call | flops 1207959552 | bytes 7077888 | tf_op jit(solution)/shard_map/pallas_call | solution.py:218
  71.6 4.2 %collective-permute-done.15 = bf16[128,1024]{1,0:T(8,128)(2,1)S(1)} collective-permute-done((bf16[128,1024]{1,0:T(8,128)(2,1)S(1)}, bf16[128,1024]{1,0:T(8,128)(2,1)S(1)}, u32[]{:S(2)}, u32[]{:S(2)}) %collective-permute-start.15) | collective-permute-done | bytes 262176 | tf_op jit(solution)/shard_map/ppermute | solution.py:246
  75.9 0.8 collective-permute-start.16
  76.6 3.2 %collective-permute-start.17 = (bf16[64,1024]{1,0:T(8,128)(2,1)S(1)}, bf16[64,1024]{1,0:T(8,128)(2,1)S(1)}, u32[]{:S(2)}, u32[]{:S(2)}) collective-permute-start(bf16[64,1024]{1,0:T(8,128)(2,1)S(1)} %get-tuple-element.31), channel_id=1, source_target_pairs={{0,48},{16,0},{32,16},{48,32},{1,49},{17,1},{33,17},{49,33},{2,50}... | collective-permute-start | bytes 393224 | tf_op jit(solution)/shard_map/ppermute | solution.py:246
  80.0 0.7 collective-permute-done.16
  80.8 1.7 %collective-permute-done.17 = bf16[64,1024]{1,0:T(8,128)(2,1)S(1)} collective-permute-done((bf16[64,1024]{1,0:T(8,128)(2,1)S(1)}, bf16[64,1024]{1,0:T(8,128)(2,1)S(1)}, u32[]{:S(2)}, u32[]{:S(2)}) %collective-permute-start.17) | collective-permute-done | bytes 131104 | tf_op jit(solution)/shard_map/ppermute | solution.py:246
  82.5 4.7 %collective-permute-done.18 = bf16[64,1024]{1,0:T(8,128)(2,1)S(1)} collective-permute-done((bf16[64,1024]{1,0:T(8,128)(2,1)S(1)}, bf16[64,1024]{1,0:T(8,128)(2,1)S(1)}, u32[]{:S(2)}, u32[]{:S(2)}) %collective-permute-start.18) | collective-permute-done | bytes 131104 | tf_op jit(solution)/shard_map/ppermute | solution.py:246
  87.1 0.8 fusion.2
  (26 shorter events, 0.7 us)
Async XLA Ops:
  0.6 51.0 %copy-start.1 = (s32[3,384]{1,0:T(4,128)S(1)}, s32[3,384]{1,0:T(4,128)}, u32[]{:S(2)}) copy-start(s32[3,384]{1,0:T(4,128)} %mask_ref.1) | copy-start | bytes 13828
  0.6 17.6 %collective-permute-start.4 = (bf16[2048,1024]{1,0:T(8,128)(2,1)}, bf16[2048,1024]{1,0:T(8,128)(2,1)}, u32[]{:S(2)}, u32[]{:S(2)}) collective-permute-start(bf16[2048,1024]{1,0:T(8,128)(2,1)} %param.9), channel_id=1, source_target_pairs={{0,8},{8,0},{1,9},{9,1},{2,10},{10,2},{3,11},{11,3},{4,12},{12,4},... | collective-permute-start | bytes 12582920 | tf_op jit(solution)/shard_map/ppermute | solution.py:246
  4.0 14.3 %collective-permute-start.3 = (bf16[384,1024]{1,0:T(8,128)(2,1)}, bf16[384,1024]{1,0:T(8,128)(2,1)S(1)}, u32[]{:S(2)}, u32[]{:S(2)}) collective-permute-start(bf16[384,1024]{1,0:T(8,128)(2,1)} %own_ref.1), channel_id=1, source_target_pairs={{0,8},{8,0},{1,9},{9,1},{2,10},{10,2},{3,11},{11,3},{4,12},{12,4},... | collective-permute-start | bytes 2359304 | tf_op jit(solution)/shard_map/ppermute | solution.py:246
  4.1 14.2 %collective-permute-start = (s32[384]{0:T(512)}, s32[384]{0:T(512)S(1)}, u32[]{:S(2)}, u32[]{:S(2)}) collective-permute-start(s32[384]{0:T(512)} %param.11), channel_id=1, source_target_pairs={{0,1},{1,2},{2,3},{3,0},{4,5},{5,6},{6,7},{7,4},{8,9},{9,10},{10,1... | collective-permute-start | bytes 4616 | tf_op jit(solution)/shard_map/ppermute | solution.py:246
  4.1 14.2 %collective-permute-start.1 = (s32[384]{0:T(512)}, s32[384]{0:T(512)S(1)}, u32[]{:S(2)}, u32[]{:S(2)}) collective-permute-start(s32[384]{0:T(512)} %param.11), channel_id=1, source_target_pairs={{0,8},{8,0},{1,9},{9,1},{2,10},{10,2},{3,11},{11,3},{4,12},{12,4},... | collective-permute-start | bytes 4616 | tf_op jit(solution)/shard_map/ppermute | solution.py:246
  4.5 13.8 %collective-permute-start.2 = (f32[3,1024]{1,0:T(4,128)}, f32[3,1024]{1,0:T(4,128)S(1)}, u32[]{:S(2)}, u32[]{:S(2)}) collective-permute-start(f32[3,1024]{1,0:T(4,128)} %param.8), channel_id=1, source_target_pairs={{0,8},{8,0},{1,9},{9,1},{2,10},{10,2},{3,11},{11,3},{4,12},{12,4},... | collective-permute-start | bytes 36872 | tf_op jit(solution)/shard_map/ppermute | solution.py:246
  18.3 1.1 %copy-start = (bf16[384,1024]{1,0:T(8,128)(2,1)S(1)}, bf16[384,1024]{1,0:T(8,128)(2,1)}, u32[]{:S(2)}) copy-start(bf16[384,1024]{1,0:T(8,128)(2,1)} %own_ref.1) | copy-start | bytes 2359300
  37.9 4.3 %collective-permute-start.5 = (f32[3,1536]{1,0:T(4,128)S(1)}, f32[3,1536]{1,0:T(4,128)S(1)}, u32[]{:S(2)}, u32[]{:S(2)}) collective-permute-start(f32[3,1536]{1,0:T(4,128)S(1)} %get-tuple-element.16.refs_0_), channel_id=1, source_target_pairs={{0,2},{1,3},{2,0},{3,1},{4,6},{5,7},{6,4},{7,5},{8,10},{9,11},{10,... | collective-permute-start | bytes 55304 | tf_op jit(solution)/shard_map/ppermute | solution.py:261
  40.6 3.1 %collective-permute-start.6 = (f32[3,1536]{1,0:T(4,128)S(1)}, f32[3,1536]{1,0:T(4,128)S(1)}, u32[]{:S(2)}, u32[]{:S(2)}) collective-permute-start(f32[3,1536]{1,0:T(4,128)S(1)} %get-tuple-element.16.refs_0_), channel_id=1, source_target_pairs={{0,1},{1,0},{2,3},{3,2},{4,5},{5,4},{6,7},{7,6},{8,9},{9,8},{10,11... | collective-permute-start | bytes 55304 | tf_op jit(solution)/shard_map/ppermute | solution.py:261
  40.6 4.3 %collective-permute-start.7 = (f32[3,1536]{1,0:T(4,128)S(1)}, f32[3,1536]{1,0:T(4,128)S(1)}, u32[]{:S(2)}, u32[]{:S(2)}) collective-permute-start(f32[3,1536]{1,0:T(4,128)S(1)} %get-tuple-element.16.refs_0_), channel_id=1, source_target_pairs={{0,3},{1,2},{2,1},{3,0},{4,7},{5,6},{6,5},{7,4},{8,11},{9,10},{10,... | collective-permute-start | bytes 55304 | tf_op jit(solution)/shard_map/ppermute | solution.py:261
  45.0 6.7 %collective-permute-start.8 = (f32[3,1536]{1,0:T(4,128)S(1)}, f32[3,1536]{1,0:T(4,128)S(1)}, u32[]{:S(2)}, u32[]{:S(2)}) collective-permute-start(f32[3,1536]{1,0:T(4,128)S(1)} %shard_map.87.msg_ref), channel_id=1, source_target_pairs={{0,4},{4,0},{1,5},{5,1},{2,6},{6,2},{3,7},{7,3},{8,12},{12,8},{9,1... | collective-permute-start | bytes 55304 | tf_op jit(solution)/shard_map/ppermute | solution.py:246
  51.7 2.7 %collective-permute-start.9 = (f32[3,1920]{1,0:T(4,128)S(1)}, f32[3,1920]{1,0:T(4,128)S(1)}, u32[]{:S(2)}, u32[]{:S(2)}) collective-permute-start(f32[3,1920]{1,0:T(4,128)S(1)} %shard_map.88.part_ref), channel_id=1, source_target_pairs={{0,8},{8,0},{1,9},{9,1},{2,10},{10,2},{3,11},{11,3},{4,12},{12,4},... | collective-permute-start | bytes 69128 | tf_op jit(solution)/shard_map/ppermute | solution.py:246
  56.3 8.8 %collective-permute-start.14 = (bf16[128,1024]{1,0:T(8,128)(2,1)S(1)}, bf16[128,1024]{1,0:T(8,128)(2,1)S(1)}, u32[]{:S(2)}, u32[]{:S(2)}) collective-permute-start(bf16[128,1024]{1,0:T(8,128)(2,1)S(1)} %get-tuple-element.29), channel_id=1, source_target_pairs={{0,64},{64,128},{128,192},{192,0},{1,65},{65,129},{129,193},{193,1... | collective-permute-start | bytes 786440 | tf_op jit(solution)/shard_map/ppermute | solution.py:246
  56.3 8.9 %collective-permute-start.12 = (bf16[128,1024]{1,0:T(8,128)(2,1)S(1)}, bf16[128,1024]{1,0:T(8,128)(2,1)S(1)}, u32[]{:S(2)}, u32[]{:S(2)}) collective-permute-start(bf16[128,1024]{1,0:T(8,128)(2,1)S(1)} %get-tuple-element.26), channel_id=1, source_target_pairs={{0,192},{64,0},{128,64},{192,128},{1,193},{65,1},{129,65},{193,129... | collective-permute-start | bytes 786440 | tf_op jit(solution)/shard_map/ppermute | solution.py:246
  61.6 8.0 %collective-permute-start.10 = (bf16[128,1024]{1,0:T(8,128)(2,1)S(1)}, bf16[128,1024]{1,0:T(8,128)(2,1)S(1)}, u32[]{:S(2)}, u32[]{:S(2)}) collective-permute-start(bf16[128,1024]{1,0:T(8,128)(2,1)S(1)} %get-tuple-element.22), channel_id=1, source_target_pairs={{0,192},{64,0},{128,64},{192,128},{1,193},{65,1},{129,65},{193,129... | collective-permute-start | bytes 786440 | tf_op jit(solution)/shard_map/ppermute | solution.py:246
  61.7 8.5 %collective-permute-start.11 = (bf16[128,1024]{1,0:T(8,128)(2,1)S(1)}, bf16[128,1024]{1,0:T(8,128)(2,1)S(1)}, u32[]{:S(2)}, u32[]{:S(2)}) collective-permute-start(bf16[128,1024]{1,0:T(8,128)(2,1)S(1)} %get-tuple-element.23), channel_id=1, source_target_pairs={{0,64},{64,128},{128,192},{192,0},{1,65},{65,129},{129,193},{193,1... | collective-permute-start | bytes 786440 | tf_op jit(solution)/shard_map/ppermute | solution.py:246
  65.1 10.7 %collective-permute-start.15 = (bf16[128,1024]{1,0:T(8,128)(2,1)S(1)}, bf16[128,1024]{1,0:T(8,128)(2,1)S(1)}, u32[]{:S(2)}, u32[]{:S(2)}) collective-permute-start(bf16[128,1024]{1,0:T(8,128)(2,1)S(1)} %add_convert_fusion.1), channel_id=1, source_target_pairs={{0,64},{64,128},{128,192},{192,0},{1,65},{65,129},{129,193},{193,1... | collective-permute-start | bytes 786440 | tf_op jit(solution)/shard_map/ppermute | solution.py:246
  65.3 14.6 %collective-permute-start.13 = (bf16[128,1024]{1,0:T(8,128)(2,1)S(1)}, bf16[128,1024]{1,0:T(8,128)(2,1)S(1)}, u32[]{:S(2)}, u32[]{:S(2)}) collective-permute-start(bf16[128,1024]{1,0:T(8,128)(2,1)S(1)} %add_convert_fusion.2), channel_id=1, source_target_pairs={{0,192},{64,0},{128,64},{192,128},{1,193},{65,1},{129,65},{193,129... | collective-permute-start | bytes 786440 | tf_op jit(solution)/shard_map/ppermute | solution.py:246
  75.9 4.9 %collective-permute-start.16 = (bf16[64,1024]{1,0:T(8,128)(2,1)S(1)}, bf16[64,1024]{1,0:T(8,128)(2,1)S(1)}, u32[]{:S(2)}, u32[]{:S(2)}) collective-permute-start(bf16[64,1024]{1,0:T(8,128)(2,1)S(1)} %get-tuple-element.30), channel_id=1, source_target_pairs={{0,32},{16,48},{32,0},{48,16},{1,33},{17,49},{33,1},{49,17},{2,34}... | collective-permute-start | bytes 393224 | tf_op jit(solution)/shard_map/ppermute | solution.py:246
  76.6 5.8 %collective-permute-start.17 = (bf16[64,1024]{1,0:T(8,128)(2,1)S(1)}, bf16[64,1024]{1,0:T(8,128)(2,1)S(1)}, u32[]{:S(2)}, u32[]{:S(2)}) collective-permute-start(bf16[64,1024]{1,0:T(8,128)(2,1)S(1)} %get-tuple-element.31), channel_id=1, source_target_pairs={{0,48},{16,0},{32,16},{48,32},{1,49},{17,1},{33,17},{49,33},{2,50}... | collective-permute-start | bytes 393224 | tf_op jit(solution)/shard_map/ppermute | solution.py:246
  79.9 7.2 %collective-permute-start.18 = (bf16[64,1024]{1,0:T(8,128)(2,1)S(1)}, bf16[64,1024]{1,0:T(8,128)(2,1)S(1)}, u32[]{:S(2)}, u32[]{:S(2)}) collective-permute-start(bf16[64,1024]{1,0:T(8,128)(2,1)S(1)} %slice.31), channel_id=1, source_target_pairs={{0,16},{16,32},{32,48},{48,0},{1,17},{17,33},{33,49},{49,1},{2,18}... | collective-permute-start | bytes 393224 | tf_op jit(solution)/shard_map/ppermute | solution.py:246
